TPU v7x, 128 devices: a whole 4x4x4 slice. The times are simulated.
128 devices in a mesh: ctx: 32 (over z, y, x_lo), tp: 4 (over x_hi, core).
Axes of the slice: x: 4 (x_hi: 2, x_lo: 2; x = x_hi * 2 + x_lo), y: 4, z: 4, core: 2. Of those that a mesh axis runs over, the one named last changes fastest.
Arguments:
- queries: bfloat16 [512, 2, 6144], P('ctx', None, 'tp'), may hold values from -6 to 6
- new_keys: bfloat16 [512, 2, 1024], P('ctx', None, 'tp'), may hold values from -6 to 6
- new_values: bfloat16 [512, 2, 1024], P('ctx', None, 'tp'), may hold values from -18 to 18
- cached_key_rows: bfloat16 [16384, 2, 1024], P('ctx', None, 'tp'), may hold values from -6 to 6
- cache_values: bfloat16 [16384, 2, 1024], P('ctx', None, 'tp'), may hold values from -18 to 18
- cache_lengths: int32 [2], replicated, may hold values from 1 to 16384, as said below
- norm_gain: bfloat16 [6144], P('tp'), may hold values from 0.25 to 1.75
- routes: int32 [512, 2, 2], P('ctx'), may hold values from 0 to 7, all different within a row; in each aligned block of 32 rows (0 to 31, 32 to 63, ..., all dimensions but the last counted through in order) at most 16 rows name the same one
- gates: float32 [512, 2, 2], P('ctx'), may hold values from 0.2 to 1
- gate_proj: bfloat16 [32, 6144, 2048], P('ctx', None, 'tp'), may hold values from -0.078125 to 0.078125
- up_proj: bfloat16 [32, 6144, 2048], P('ctx', None, 'tp'), may hold values from -0.078125 to 0.078125
- down_proj: bfloat16 [32, 2048, 6144], P('ctx', None, 'tp'), may hold values from -0.0625 to 0.0625
Outputs:
- normed: float32 [512, 2, 6144], P('ctx', None, 'tp')
- moe_out: float32 [512, 2, 6144], P('ctx', None, 'tp')
Inputs may be any that keep to these rules, and one draw needn't show every extreme that they name: `routes`: in the tokens of one index of ctx (aligned blocks of 32 tokens) no expert is named more than 16 times, a bound that some block reaches; the 2 experts of a token differ. `cache_lengths`: at least one sequence has all 16384 slots filled.
All inputs are finite; a program needn't handle non-finite values.
Results may differ from a plain program's by a relative error of at most 0.02.
Values may be sent and summed in bfloat16 or wider, within the bound.
No kernel may reach another device: no remote copies, remote signals or barrier semaphores. Data moves between devices by JAX's collectives and lax.ppermute only.
A program may use at most 128 MiB of HBM per device.

v0:
```python
import math

import jax
import jax.numpy as jnp
from jax import lax
from jax.sharding import PartitionSpec as P

HEAD_SIZE = 128
EXPERTS = 8
TOPK = 2
CAP = 16


FLOOR = -1e30
EPS = 1e-05


def grouped_scores(query_group, key_group, multiplier):
    return (
        jnp.einsum("pgrd,kgd->grpk", query_group, key_group, preferred_element_type=jnp.float32)
        * multiplier
    )


def partial_softmax(scores, alive, rowmax, value_group):
    masked = jnp.where(alive[None, None], scores, FLOOR)
    expo = jnp.where(alive[None, None], jnp.exp(masked - rowmax[..., None]), 0.0)
    totals = jnp.sum(expo, axis=-1)
    weighted = jnp.einsum(
        "grpk,kgd->pgrd", expo.astype(jnp.bfloat16), value_group, preferred_element_type=jnp.float32
    )
    return (weighted, totals)


def head_major(values):
    return jnp.transpose(values, (2, 0, 1)).reshape(
        values.shape[2], values.shape[0] * values.shape[1]
    )


def by_owner(array, owners):
    return array.reshape((owners, array.shape[0] // owners) + array.shape[1:])


def on_device(
    queries,
    new_keys,
    new_values,
    cached_key_rows,
    cache_values,
    cache_lengths,
    norm_gain,
    routes,
    gates,
    gate_proj,
    up_proj,
    down_proj,
):
    new_dev, seq_count, q_width = queries.shape
    kv_heads = new_keys.shape[2] // HEAD_SIZE
    q_heads = q_width // HEAD_SIZE
    replicate = q_heads // kv_heads
    cache_dev = cached_key_rows.shape[0]
    ctx_size = lax.axis_size("ctx")
    ctx_index = lax.axis_index("ctx")
    multiplier = 1.0 / math.sqrt(HEAD_SIZE)
    everyone = lax.all_gather(queries, "ctx", axis=0, tiled=True)
    new_total = everyone.shape[0]
    position = jnp.arange(new_total)
    own_new = ctx_index * new_dev + jnp.arange(new_dev)
    own_slots = ctx_index * cache_dev + jnp.arange(cache_dev)
    pieces = []
    for sequence in range(seq_count):
        key_group = jnp.concatenate(
            [cached_key_rows[:, sequence], new_keys[:, sequence]], axis=0
        ).reshape(-1, kv_heads, HEAD_SIZE)
        value_group = jnp.concatenate(
            [cache_values[:, sequence], new_values[:, sequence]], axis=0
        ).reshape(-1, kv_heads, HEAD_SIZE)
        cache_alive = jnp.broadcast_to(
            (own_slots < cache_lengths[sequence])[None, :], (new_total, cache_dev)
        )
        new_alive = own_new[None, :] <= position[:, None]
        alive = jnp.concatenate([cache_alive, new_alive], axis=1)
        query_group = everyone[:, sequence].reshape(new_total, kv_heads, replicate, HEAD_SIZE)
        pieces.append((query_group, key_group, value_group, alive))
    outputs = []
    maxima = []
    totals = []
    for query_group, key_group, value_group, alive in pieces:
        scores = grouped_scores(query_group, key_group, multiplier)
        rowmax = jnp.max(jnp.where(alive[None, None], scores, FLOOR), axis=-1)
        weighted, total = partial_softmax(scores, alive, rowmax, value_group)
        outputs.append(weighted.reshape(new_total, q_width))
        maxima.append(head_major(rowmax))
        totals.append(head_major(total))
    sent_out = by_owner(jnp.stack(outputs, axis=1), ctx_size)
    sent_max = by_owner(jnp.stack(maxima, axis=1), ctx_size)
    sent_total = by_owner(jnp.stack(totals, axis=1), ctx_size)
    got_out, got_max, got_total = (
        lax.all_to_all(sent_out, "ctx", split_axis=0, concat_axis=0, tiled=True),
        lax.all_to_all(sent_max, "ctx", split_axis=0, concat_axis=0, tiled=True),
        lax.all_to_all(sent_total, "ctx", split_axis=0, concat_axis=0, tiled=True),
    )
    top = jnp.max(got_max, axis=0)
    scaling = jnp.exp(got_max - top[None])
    numerator = jnp.sum(
        scaling[..., None] * got_out.reshape(ctx_size, new_dev, seq_count, q_heads, HEAD_SIZE),
        axis=0,
    )
    denominator = jnp.sum(scaling * got_total, axis=0)
    merged = numerator / denominator[..., None]
    attended = merged.reshape(new_dev, seq_count, q_width)
    tp_index = lax.axis_index("tp")
    whole, whole_gain = (
        lax.all_gather(attended, "tp", axis=2, tiled=True),
        lax.all_gather(norm_gain.astype(jnp.float32), "tp", axis=0, tiled=True),
    )
    inverse = lax.rsqrt(jnp.mean(whole * whole, axis=-1) + EPS)
    whole_normed = whole * inverse[..., None] * whole_gain
    payload = whole_normed.astype(jnp.bfloat16)
    normed = lax.dynamic_slice_in_dim(whole_normed, tp_index * q_width, q_width, 2)
    rows_local = new_dev * seq_count
    width = payload.shape[-1]
    flat_routes = routes.reshape(rows_local * TOPK)
    onehot = (flat_routes[:, None] == jnp.arange(EXPERTS)[None, :]).astype(jnp.int32)
    earlier = jnp.cumsum(onehot, axis=0) - onehot
    slot = jnp.sum(earlier * onehot, axis=1)
    target = flat_routes * CAP + slot
    table = (
        (jnp.arange(EXPERTS * CAP)[:, None] == target[None, :])
        .astype(jnp.float32)
        .reshape(EXPERTS * CAP, rows_local, TOPK)
    )
    placing = jnp.sum(table, axis=-1)
    weighting = jnp.sum(table * gates.reshape(1, rows_local, TOPK), axis=-1)
    packed = jnp.dot(
        placing.astype(jnp.bfloat16),
        payload.reshape(rows_local, width),
        preferred_element_type=jnp.float32,
    ).astype(jnp.bfloat16)
    group = ctx_size // EXPERTS
    outgoing = jnp.broadcast_to(
        packed.reshape(EXPERTS, 1, CAP, width), (EXPERTS, group, CAP, width)
    ).reshape(ctx_size, CAP, width)
    w_gate = gate_proj[0]
    w_up = up_proj[0]
    w_down = down_proj[0]
    arrived = lax.all_to_all(outgoing, "ctx", split_axis=0, concat_axis=0, tiled=True)
    sources, count, arrived_width = arrived.shape
    token_rows = arrived.reshape(sources * count, arrived_width)
    gate_val = jnp.dot(token_rows, w_gate, preferred_element_type=jnp.float32)
    up_val = jnp.dot(token_rows, w_up, preferred_element_type=jnp.float32)
    hidden = (jax.nn.silu(gate_val) * up_val).astype(jnp.bfloat16)
    produced = jnp.dot(
        lax.all_gather(hidden, "tp", axis=1, tiled=True), w_down, preferred_element_type=jnp.float32
    )
    produced = produced.reshape(sources, count, w_down.shape[1])
    returned = lax.all_to_all(produced, "ctx", split_axis=0, concat_axis=0, tiled=True)
    summed_blocks = jnp.sum(returned.reshape(EXPERTS, group, CAP, q_width), axis=1).reshape(
        EXPERTS * CAP, q_width
    )
    mixed = jnp.dot(jnp.transpose(weighting), summed_blocks, precision=lax.Precision.HIGHEST)
    moe_out = mixed.reshape(new_dev, seq_count, q_width)
    return (normed, moe_out)


def solution(mesh):
    placed = (
        P("ctx", None, "tp"),
        P("ctx", None, "tp"),
        P("ctx", None, "tp"),
        P("ctx", None, "tp"),
        P("ctx", None, "tp"),
        P(),
        P("tp"),
        P("ctx", None, None),
        P("ctx", None, None),
        P("ctx", None, "tp"),
        P("ctx", None, "tp"),
        P("ctx", None, "tp"),
    )
    return jax.shard_map(
        on_device,
        mesh=mesh,
        in_specs=placed,
        out_specs=(P("ctx", None, "tp"), P("ctx", None, "tp")),
        check_vma=False,
    )
```

profile of v0, /device:TPU:0, one launch (start us, length us, event | category | flops | bytes accessed | tf_op | source)
XLA Modules:
  0.0 577.9 jit_solution(1808007736149893076)
XLA Ops:
  22.3 150.3 %all-gather.4.cloned.1.call-done = bf16[512,2,1536]{2,1,0:T(2,128)(2,1)} async-done(((bf16[16,2,1536]{2,1,0:T(2,128)(2,1)}), bf16[512,2,1536]{2,1,0:T(2,128)(2,1)}) %all-gather.4.cloned.1.call-update) | async-done | bytes 3145744 | tf_op jit(solution)/shard_map/all_gather | solution.py:67
  172.6 8.8 %fusion.57 = (bf16[512,1,1536]{2,1,0:T(2,128)(2,1)}, bf16[512,1,1536]{2,1,0:T(2,128)(2,1)S(1)}) fusion(bf16[512,2,1536]{2,1,0:T(2,128)(2,1)} %all-gather.4.cloned.1.call-done), kind=kLoop, calls=%fused_computation.86 | loop fusion | bytes 6291456 | tf_op jit(solution)/shard_map/slice | solution.py:85
  181.4 8.1 %copy.260 = bf16[512,1,1536]{0,2,1:T(8,128)(2,1)} copy(bf16[512,1,1536]{2,1,0:T(2,128)(2,1)} %get-tuple-element.28) | data formatting | bytes 3145728
  189.5 6.1 %copy.262 = bf16[512,1,1536]{0,2,1:T(8,128)(2,1)} copy(bf16[512,1,1536]{2,1,0:T(2,128)(2,1)S(1)} %get-tuple-element.29) | data formatting | bytes 3145728
  213.3 9.1 %all-to-all-start.2 = ((f32[32,1,384]{2,1,0:T(1,128)}), f32[32,1,384]{2,1,0:T(1,128)}, u32[]{:S(2)}, u32[]{:S(2)}) async-start(f32[32,1,384]{2,1,0:T(1,128)} %reshape.137), calls=%async_computation.2 | async-start | bytes 98304 | tf_op jit(solution)/shard_map/all_to_all | solution.py:103
  222.6 10.3 %fusion.21 = f32[512,2,6,128]{0,3,2,1:T(8,128)} fusion(f32[2,528,512,6]{2,1,3,0:T(8,128)} %copy-done, f32[2,6,512]{2,1,0:T(8,128)S(1)} %get-tuple-element.38, pred[512,528]{0,1:T(8,128)(4,1)S(1)} %copy-done.3, bf16[16,2,128]{2,0,1:T(8,128)(2,1)S(1)} %copy_bitcast_fusion, bf16[512,2,128]{2,0,1:T(8,128)(2,1)S(1)} %copy-done.6), kind=kOutput, calls=%fused_computation.25 | convolution fusion | flops 847233024 | bytes 16687104 | tf_op jit(solution)/shard_map/grpk,kgd->pgrd/dot_general | solution.py:29
  232.9 5.4 fusion.18
  238.3 5.1 copy.237
  249.8 5.1 copy.233
  254.9 4.9 stack.24
  259.8 8.4 %all-to-all-start = ((f32[32,1,384]{2,1,0:T(1,128)}), f32[32,1,384]{2,1,0:T(1,128)S(1)}, u32[]{:S(2)}, u32[]{:S(2)}) async-start(f32[32,1,384]{2,1,0:T(1,128)} %reshape.135), calls=%async_computation | async-start | bytes 98304 | tf_op jit(solution)/shard_map/all_to_all | solution.py:102
  268.2 5.2 pad_maximum_fusion
  273.4 10.7 %all-to-all-done = f32[32,1,384]{2,1,0:T(1,128)S(1)} async-done(((f32[32,1,384]{2,1,0:T(1,128)}), f32[32,1,384]{2,1,0:T(1,128)S(1)}, u32[]{:S(2)}, u32[]{:S(2)}) %all-to-all-start) | async-done | bytes 49184 | tf_op jit(solution)/shard_map/all_to_all | solution.py:102
  284.1 12.7 %all-to-all-start.1 = ((f32[32,16,2,1536]{3,1,2,0:T(8,128)}), f32[32,16,2,1536]{3,1,2,0:T(8,128)}, u32[]{:S(2)}, u32[]{:S(2)}) async-start(f32[32,16,2,1536]{3,1,2,0:T(8,128)} %pad_maximum_fusion), calls=%async_computation.1 | async-start | bytes 12582912 | tf_op jit(solution)/shard_map/all_to_all | solution.py:101
  298.1 52.0 %all-gather = f32[4,1,1536]{2,1,0:T(1,128)S(1)} all-gather(f32[1,1,1536]{2,1,0:T(1,128)S(1)} %reshape.121), channel_id=1, replica_groups=mesh['ctx'=32,'tp'=4] {'tp'}, dimensions={0}, use_global_device_ids=true | all-gather | bytes 30720 | tf_op jit(solution)/shard_map/all_gather | solution.py:117
  355.7 4.6 mul.93
  360.3 8.7 %mul.94 = f32[32,16,2,1536]{3,1,2,0:T(8,128)} reshape(f32[32,16,2,12,128]{4,3,1,2,0:T(8,128)} %mul.93) | data formatting | bytes 12582912 | tf_op jit(solution)/shard_map/mul | solution.py:108
  369.0 5.5 multiply_reduce_fusion
  374.6 10.2 %all_gather.13 = f32[16,2,6144]{2,0,1:T(8,128)S(1)} all-gather(f32[16,2,1536]{2,0,1:T(8,128)S(1)} %div.23), channel_id=1, replica_groups=mesh['ctx'=32,'tp'=4] {'tp'}, dimensions={2}, use_global_device_ids=true | all-gather | bytes 983040 | tf_op jit(solution)/shard_map/all_gather | solution.py:116
  388.0 91.8 %all_to_all.25 = bf16[32,16,6144]{2,1,0:T(8,128)(2,1)S(1)} all-to-all(bf16[32,16,6144]{2,1,0:T(8,128)(2,1)S(1)} %bitcast.150), channel_id=1, replica_groups=mesh['ctx'=32,'tp'=4] {'ctx'}, dimensions={0} | all-to-all | bytes 12582912 | tf_op jit(solution)/shard_map/all_to_all | solution.py:149
  487.5 22.3 %all-gather.6.cloned.1.call-done = bf16[512,2048]{1,0:T(8,128)(2,1)} async-done(((bf16[512,512]{1,0:T(8,128)(2,1)}), bf16[512,2048]{1,0:T(8,128)(2,1)}) %all-gather.6.cloned.1.call-update) | async-done | bytes 2097168 | tf_op jit(solution)/shard_map/all_gather | solution.py:156
  509.8 8.5 %fusion.12 = f32[32,16,1536]{2,1,0:T(8,128)} fusion(bf16[32,16,2048]{2,1,0:T(8,128)(2,1)} %bitcast.177, bf16[1,2048,1536]{2,1,0:T(8,128)(2,1)} %param.23), kind=kOutput, calls=%fused_computation.16 | convolution fusion | flops 3221225472 | bytes 11534336 | tf_op jit(solution)/shard_map/dot_general | solution.py:155
  518.3 7.3 %all-to-all-start.4 = ((f32[32,16,1536]{2,1,0:T(8,128)}), f32[32,16,1536]{2,1,0:T(8,128)S(1)}, u32[]{:S(2)}, u32[]{:S(2)}) async-start(f32[32,16,1536]{2,1,0:T(8,128)} %fusion.12), calls=%async_computation.4 | async-start | bytes 6291456 | tf_op jit(solution)/shard_map/all_to_all | solution.py:159
  527.4 41.9 %all-to-all-done.4 = f32[32,16,1536]{2,1,0:T(8,128)S(1)} async-done(((f32[32,16,1536]{2,1,0:T(8,128)}), f32[32,16,1536]{2,1,0:T(8,128)S(1)}, u32[]{:S(2)}, u32[]{:S(2)}) %all-to-all-start.4) | async-done | bytes 3145760 | tf_op jit(solution)/shard_map/all_to_all | solution.py:159
  (131 shorter events, 60.1 us)
Async XLA Ops:
  7.2 13.9 %copy-start.7 = (bf16[16,2,256]{2,1,0:T(2,128)(2,1)S(1)}, bf16[16,2,256]{2,1,0:T(2,128)(2,1)}, u32[]{:S(2)}) copy-start(bf16[16,2,256]{2,1,0:T(2,128)(2,1)} %param.13) | copy-start | bytes 49156
  7.2 14.0 %copy-start.8 = (bf16[16,2,256]{2,1,0:T(2,128)(2,1)S(1)}, bf16[16,2,256]{2,1,0:T(2,128)(2,1)}, u32[]{:S(2)}) copy-start(bf16[16,2,256]{2,1,0:T(2,128)(2,1)} %param.14) | copy-start | bytes 49156
  7.2 165.4 %all-gather.4.cloned.1.call-start = ((), (), s32[]{:S(2)}) async-start(), calls=%async_computation.5 | async-start | bytes 3244032 | tf_op jit(solution)/shard_map/all_gather | solution.py:67
  199.5 5.0 copy-start
  199.5 5.2 copy-start.2
  199.5 5.2 copy-start.4
  207.1 4.7 copy-start.1
  207.1 15.5 %copy-start.6 = (bf16[512,2,128]{2,0,1:T(8,128)(2,1)S(1)}, bf16[512,2,128]{2,0,1:T(8,128)(2,1)}, u32[]{:S(2)}) copy-start(bf16[512,2,128]{2,0,1:T(8,128)(2,1)} %copy.235) | copy-start | bytes 786436
  213.3 19.5 %slice-start = ((s8[12976128]{0:T(1024)(128)(4,1)}), s8[393216]{0:T(1024)(128)(4,1)S(1)}, s32[]{:S(2)}) async-start(s8[12976128]{0:T(1024)(128)(4,1)} %bitcast.148), calls=%async_computation.7 | async-start | bytes 786432
  213.3 46.4 %all-to-all-start.2 = ((f32[32,1,384]{2,1,0:T(1,128)}), f32[32,1,384]{2,1,0:T(1,128)}, u32[]{:S(2)}, u32[]{:S(2)}) async-start(f32[32,1,384]{2,1,0:T(1,128)} %reshape.137), calls=%async_computation.2 | async-start | bytes 98304 | tf_op jit(solution)/shard_map/all_to_all | solution.py:103
  222.5 10.3 %slice-start.1 = ((s8[12976128]{0:T(1024)(128)(4,1)}), s8[4194304]{0:T(1024)(128)(4,1)S(1)}, s32[]{:S(2)}) async-start(s8[12976128]{0:T(1024)(128)(4,1)} %bitcast.148), calls=%async_computation.8 | async-start | bytes 8388608
  222.5 10.3 %slice-start.2 = ((s8[12976128]{0:T(1024)(128)(4,1)}), s8[4194304]{0:T(1024)(128)(4,1)S(1)}, s32[]{:S(2)}) async-start(s8[12976128]{0:T(1024)(128)(4,1)} %bitcast.148), calls=%async_computation.9 | async-start | bytes 8388608
  222.6 10.3 %slice-start.3 = ((s8[12976128]{0:T(1024)(128)(4,1)}), s8[4194304]{0:T(1024)(128)(4,1)S(1)}, s32[]{:S(2)}) async-start(s8[12976128]{0:T(1024)(128)(4,1)} %bitcast.148), calls=%async_computation.10 | async-start | bytes 8388608
  222.6 10.3 %copy-start.5 = (bf16[512,2,128]{2,0,1:T(8,128)(2,1)S(1)}, bf16[512,2,128]{2,0,1:T(8,128)(2,1)}, u32[]{:S(2)}) copy-start(bf16[512,2,128]{2,0,1:T(8,128)(2,1)} %copy.231) | copy-start | bytes 786436
  259.8 24.3 %all-to-all-start = ((f32[32,1,384]{2,1,0:T(1,128)}), f32[32,1,384]{2,1,0:T(1,128)S(1)}, u32[]{:S(2)}, u32[]{:S(2)}) async-start(f32[32,1,384]{2,1,0:T(1,128)} %reshape.135), calls=%async_computation | async-start | bytes 98304 | tf_op jit(solution)/shard_map/all_to_all | solution.py:102
  273.4 23.5 %copy-start.10 = (bf16[1536]{0:T(1024)(128)(2,1)S(1)}, bf16[1536]{0:T(1024)(128)(2,1)}, u32[]{:S(2)}) copy-start(bf16[1536]{0:T(1024)(128)(2,1)} %param.18) | copy-start | bytes 9220
  273.4 23.5 %copy-start.9 = (s32[16,2,2]{0,2,1:T(2,128)S(1)}, s32[16,2,2]{0,2,1:T(2,128)}, u32[]{:S(2)}) copy-start(s32[16,2,2]{0,2,1:T(2,128)} %param.19) | copy-start | bytes 772
  273.4 23.8 %copy-start.11 = (f32[16,2,2]{0,2,1:T(2,128)S(1)}, f32[16,2,2]{0,2,1:T(2,128)}, u32[]{:S(2)}) copy-start(f32[16,2,2]{0,2,1:T(2,128)} %param.20) | copy-start | bytes 772
  284.1 84.8 %all-to-all-start.1 = ((f32[32,16,2,1536]{3,1,2,0:T(8,128)}), f32[32,16,2,1536]{3,1,2,0:T(8,128)}, u32[]{:S(2)}, u32[]{:S(2)}) async-start(f32[32,16,2,1536]{3,1,2,0:T(8,128)} %pad_maximum_fusion), calls=%async_computation.1 | async-start | bytes 12582912 | tf_op jit(solution)/shard_map/all_to_all | solution.py:101
  296.9 212.9 %all-gather.6.cloned.1.call-start = ((), (), s32[]{:S(2)}) async-start(), calls=%async_computation.6 | async-start | bytes 2621440 | tf_op jit(solution)/shard_map/all_gather | solution.py:156
  387.2 92.6 %slice-start.4 = ((s8[6291456]{0:T(1024)(128)(4,1)}), s8[2097152]{0:T(1024)(128)(4,1)S(1)}, s32[]{:S(2)}) async-start(s8[6291456]{0:T(1024)(128)(4,1)} %bitcast.173), calls=%async_computation.11 | async-start | bytes 4194304
  387.9 91.8 %slice-start.5 = ((s8[6291456]{0:T(1024)(128)(4,1)}), s8[4194304]{0:T(1024)(128)(4,1)S(1)}, s32[]{:S(2)}) async-start(s8[6291456]{0:T(1024)(128)(4,1)} %bitcast.173), calls=%async_computation.12 | async-start | bytes 8388608
  387.9 95.3 %slice-start.6 = ((s8[6291456]{0:T(1024)(128)(4,1)}), s8[4194304]{0:T(1024)(128)(4,1)S(1)}, s32[]{:S(2)}) async-start(s8[6291456]{0:T(1024)(128)(4,1)} %bitcast.175), calls=%async_computation.13 | async-start | bytes 8388608
  518.3 51.0 %all-to-all-start.4 = ((f32[32,16,1536]{2,1,0:T(8,128)}), f32[32,16,1536]{2,1,0:T(8,128)S(1)}, u32[]{:S(2)}, u32[]{:S(2)}) async-start(f32[32,16,1536]{2,1,0:T(8,128)} %fusion.12), calls=%async_computation.4 | async-start | bytes 6291456 | tf_op jit(solution)/shard_map/all_to_all | solution.py:159
  (2 other events, 7.3 us)
Sparse Core Ops, SparseCore 0:
  9.7 162.8 all-gather.3
  487.6 22.1 all-gather.5
where the time goes:
time: 588 us; the launch traced here: 578 us
  waiting for transfers between devices  226 us (38%)
  blocking collectives  154 us (26%)
  local copies, waits for them, and re-layouts  82.3 us (14%)
  matrix products  39.1 us (7%)
  starting transfers between devices  37.5 us (6%)
  other arithmetic  24.2 us (4%)
  between operations  14.9 us (3%)
    all_gather x1, waiting for transfers between devices, on_device(): everyone = lax.all_gather(queries, 'ctx', axis=0, tiled=True)  150 us
    all_to_all x1, blocking collectives, on_device(): lax.all_to_all(outgoing, 'ctx', split_axis=0, concat_axis=0, tiled=True)  91.8 us
    all_gather x1, blocking collectives, on_device(): lax.all_gather(norm_gain.astype(jnp.float32), 'tp', axis=0, tiled=True)  52 us
    all_to_all x1, waiting for transfers between devices, on_device(): lax.all_to_all(produced, 'ctx', split_axis=0, concat_axis=0, tiled=True)  41.9 us
    unnamed x55, local copies, waits for them, and re-layouts  26.5 us
    all_gather x1, waiting for transfers between devices, on_device(): lax.all_gather(hidden, 'tp', axis=1, tiled=True)  22.3 us
    dot_general x2, matrix products, partial_softmax(): jnp.einsum('grpk,kgd->pgrd', expo.astype(jnp.bfloat16), value_group, pref...  15.7 us
    mul x2, local copies, waits for them, and re-layouts, on_device(): scaling[..., None]  13.2 us
  transfers between devices with their start and end apart: 6, of which 4 were waited for; matrix products, arithmetic and copies ran while one was open for 14% of the time, Pallas kernels for 0%

commit v1 on v0

v1 whole, which is shorter than its diff:
```python
import math

import jax
import jax.numpy as jnp
from jax import lax
from jax.experimental import pallas as pl
from jax.experimental.pallas import tpu as pltpu
from jax.sharding import Mesh
from jax.sharding import PartitionSpec as P

HEAD_SIZE = 128
EXPERTS = 8
TOPK = 2
CAP = 16
EPS = 1e-05
DEAD = -1e30
LANES = 128
VMEM_LIMIT = 50 * 1024 * 1024

BF16 = jnp.bfloat16
F32 = jnp.float32


def attention_kernel(
    info_ref, q_ref, mine_ref, theirs_ref, out_ref, keys_ref, values_ref, causal_ref, lse_ref, *, chunks
):
    sequence = pl.program_id(0)
    head = pl.program_id(1)
    heads = pl.num_programs(1)
    sources, _, own_rows, _ = q_ref.shape
    rows = sources * own_rows
    count = mine_ref.shape[2]
    padded = keys_ref.shape[0]
    cache = count - own_rows
    length = info_ref[sequence]
    own = info_ref[2]
    other = info_ref[3]
    first = 2 * own_rows * info_ref[4]
    multiplier = 1.0 / math.sqrt(HEAD_SIZE)

    @pl.when(head == 0)
    def _():
        row = lax.broadcasted_iota(jnp.int32, (padded, LANES), 0)
        lane = lax.broadcasted_iota(jnp.int32, (padded, LANES), 1)
        second = row >= count
        index = jnp.where(second, row - count, row)
        index = jnp.where(row >= 2 * count, cache, index)
        owner = jnp.where(second, other, own)
        is_cache = index < cache
        cache_dead = is_cache & (owner * cache + index >= length)
        dead = (lane == 2 * own_rows) & (cache_dead | (row >= 2 * count))
        late = (
            (lane == owner * own_rows - first + index - cache)
            & jnp.logical_not(is_cache)
            & (row < 2 * count)
        )
        bias = jnp.where(dead | late, DEAD, 0.0).astype(BF16)
        keys_ref[:, LANES:] = bias
        values_ref[:, LANES:] = jnp.ones((padded, LANES), BF16)
        keys_ref[:count, :LANES] = mine_ref[0, 0]
        values_ref[:count, :LANES] = mine_ref[1, 0]
        keys_ref[count : 2 * count, :LANES] = theirs_ref[0, 0]
        values_ref[count : 2 * count, :LANES] = theirs_ref[1, 0]
        keys_ref[2 * count :, :LANES] = jnp.zeros((padded - 2 * count, LANES), BF16)
        values_ref[2 * count :, :LANES] = jnp.zeros((padded - 2 * count, LANES), BF16)
        position = lax.broadcasted_iota(jnp.int32, (rows, LANES), 0)
        token = lax.broadcasted_iota(jnp.int32, (rows, LANES), 1)
        blocked = ((token < 2 * own_rows) & (position < first + token)) | (token == 2 * own_rows)
        causal_ref[...] = jnp.where(blocked, 1.0, 0.0).astype(BF16)
        lse_ref[...] = jnp.zeros_like(lse_ref)

    size = rows // chunks
    group = sources // chunks
    for chunk in range(chunks):
        span = slice(chunk * size, (chunk + 1) * size)
        query = q_ref[chunk * group : (chunk + 1) * group, 0].reshape(size, HEAD_SIZE)
        wide = jnp.concatenate([query, causal_ref[span]], axis=1)
        scores = lax.dot_general(
            wide, keys_ref[...], (((1,), (1,)), ((), ())), preferred_element_type=F32
        )
        top = jnp.max(scores, axis=1, keepdims=True)
        expo = jnp.exp2((scores - top) * (multiplier * math.log2(math.e)))
        mixed = jnp.dot(expo.astype(BF16), values_ref[...], preferred_element_type=F32)
        total = mixed[:, LANES:]
        result = mixed[:, :LANES] / total
        lse = top * multiplier + jnp.log(total)
        pairs = group // 2
        out_ref[chunk * pairs : (chunk + 1) * pairs, 0, :, pl.ds(head * HEAD_SIZE, HEAD_SIZE)] = (
            result.astype(BF16).reshape(pairs, 2 * own_rows, HEAD_SIZE)
        )
        lane = lax.broadcasted_iota(jnp.int32, (size, LANES), 1)
        lse_ref[span] = jnp.where((lane % 8 == head) & (lane < 24), lse, lse_ref[span])

    @pl.when(head == heads - 1)
    def _():
        value = lse_ref[...]
        lane = lax.broadcasted_iota(jnp.int32, (rows, LANES), 1)
        high = value.astype(BF16).astype(F32)
        middle = (value - high).astype(BF16).astype(F32)
        low = value - high - middle
        packed = jnp.where(lane < 8, high, jnp.where(lane < 16, middle, low)).astype(BF16)
        out_ref[:, 0, :, pl.ds(heads * HEAD_SIZE, LANES)] = packed.reshape(
            sources // 2, 2 * own_rows, LANES
        )


def attend(info, queries, mine, theirs, chunks=2):
    sources, sequences, own_rows, width = queries.shape
    heads = width // HEAD_SIZE
    count = mine.shape[2]
    padded = -(-2 * count // LANES) * LANES
    rows = sources * own_rows
    return pl.pallas_call(
        lambda *refs: attention_kernel(*refs, chunks=chunks),
        grid_spec=pltpu.PrefetchScalarGridSpec(
            num_scalar_prefetch=1,
            grid=(sequences, heads),
            in_specs=[
                pl.BlockSpec((sources, 1, own_rows, HEAD_SIZE), lambda s, h, i: (0, s, 0, h)),
                pl.BlockSpec((2, 1, count, HEAD_SIZE), lambda s, h, i: (0, s, 0, 0)),
                pl.BlockSpec((2, 1, count, HEAD_SIZE), lambda s, h, i: (0, s, 0, 0)),
            ],
            out_specs=pl.BlockSpec(
                (sources // 2, 1, 2 * own_rows, width + LANES), lambda s, h, i: (0, s, 0, 0)
            ),
            scratch_shapes=[
                pltpu.VMEM((padded, 2 * LANES), BF16),
                pltpu.VMEM((padded, 2 * LANES), BF16),
                pltpu.VMEM((rows, LANES), BF16),
                pltpu.VMEM((rows, LANES), F32),
            ],
        ),
        out_shape=jax.ShapeDtypeStruct(
            (sources // 2, sequences, 2 * own_rows, width + LANES), BF16
        ),
        compiler_params=pltpu.CompilerParams(vmem_limit_bytes=VMEM_LIMIT),
        name="attend",
    )(info, queries, mine, theirs)


def merge_kernel(got_ref, out_ref, square_ref):
    sources, _, rows, wide = got_ref.shape
    width = wide - LANES
    parts = got_ref[:, 0, :, width:].astype(F32).reshape(sources * rows, LANES)
    lse = parts + pltpu.roll(parts, LANES - 8, 1) + pltpu.roll(parts, LANES - 16, 1)
    lse = lse.reshape(sources, rows, LANES)
    weight = jnp.exp(lse - jnp.max(lse, axis=0, keepdims=True))
    weight = weight / jnp.sum(weight, axis=0, keepdims=True)
    square = jnp.zeros((rows, 1), F32)
    for head in range(width // HEAD_SIZE):
        lanes = slice(head * HEAD_SIZE, (head + 1) * HEAD_SIZE)
        merged = jnp.zeros((rows, HEAD_SIZE), F32)
        for source in range(sources):
            merged = merged + weight[source, :, head : head + 1] * got_ref[
                source, 0, :, lanes
            ].astype(F32)
        out_ref[0, :, lanes] = merged
        square = square + jnp.sum(merged * merged, axis=1, keepdims=True)
    square_ref[0] = jnp.broadcast_to(square, (rows, LANES))


def merge(got):
    sources, sequences, rows, wide = got.shape
    width = wide - LANES
    return pl.pallas_call(
        merge_kernel,
        grid=(sequences,),
        in_specs=[pl.BlockSpec((sources, 1, rows, wide), lambda s: (0, s, 0, 0))],
        out_specs=[
            pl.BlockSpec((1, rows, width), lambda s: (s, 0, 0)),
            pl.BlockSpec((1, rows, LANES), lambda s: (s, 0, 0)),
        ],
        out_shape=[
            jax.ShapeDtypeStruct((sequences, rows, width), F32),
            jax.ShapeDtypeStruct((sequences, rows, LANES), F32),
        ],
        compiler_params=pltpu.CompilerParams(vmem_limit_bytes=VMEM_LIMIT),
        name="merge",
    )(got)


def hidden_kernel(info_ref, near_ref, far_ref, gate_ref, up_ref, out_ref, gate_sum, up_sum):
    step = pl.program_id(0)
    steps = pl.num_programs(0)

    @pl.when(step == 0)
    def _():
        gate_sum[...] = jnp.zeros_like(gate_sum)
        up_sum[...] = jnp.zeros_like(up_sum)

    def add(rows_ref):
        rows = rows_ref[:, 0].reshape(gate_sum.shape[0], rows_ref.shape[3])
        gate_sum[...] += jnp.dot(rows, gate_ref[0], preferred_element_type=F32)
        up_sum[...] += jnp.dot(rows, up_ref[0], preferred_element_type=F32)

    @pl.when(step < steps // 2)
    def _():
        add(near_ref)

    @pl.when(step >= steps // 2)
    def _():
        add(far_ref)

    @pl.when(step == steps - 1)
    def _():
        gate = gate_sum[...]
        out_ref[...] = (gate / (1.0 + jnp.exp(-gate)) * up_sum[...]).astype(BF16)


def hidden_units(info, near, far, gate_proj, up_proj):
    sources, quarters, rows, width = near.shape
    tokens = sources * rows
    units = gate_proj.shape[2]

    def weight_block(step, info):
        quarter = step % quarters
        core = jnp.where(step < quarters, info[0], 1 - info[0])
        return (0, ((quarter % 2) * 2 + core) * 2 + quarter // 2, 0)

    return pl.pallas_call(
        hidden_kernel,
        grid_spec=pltpu.PrefetchScalarGridSpec(
            num_scalar_prefetch=1,
            grid=(2 * quarters,),
            in_specs=[
                pl.BlockSpec(
                    (sources, 1, rows, width),
                    lambda k, i: (0, jnp.minimum(k, quarters - 1), 0, 0),
                ),
                pl.BlockSpec(
                    (sources, 1, rows, width),
                    lambda k, i: (0, jnp.maximum(k - quarters, 0), 0, 0),
                ),
                pl.BlockSpec((1, width, units), weight_block),
                pl.BlockSpec((1, width, units), weight_block),
            ],
            out_specs=pl.BlockSpec((tokens, units), lambda k, i: (0, 0)),
            scratch_shapes=[pltpu.VMEM((tokens, units), F32), pltpu.VMEM((tokens, units), F32)],
        ),
        out_shape=jax.ShapeDtypeStruct((tokens, units), BF16),
        compiler_params=pltpu.CompilerParams(vmem_limit_bytes=VMEM_LIMIT),
        name="hidden_units",
    )(info, near, far, gate_proj, up_proj)


def down_kernel(info_ref, a_ref, b_ref, c_ref, d_ref, down_ref, out_ref):
    mine = info_ref[1]
    units = a_ref.shape[1]
    total = None
    for index, rows_ref in enumerate((a_ref, b_ref, c_ref, d_ref)):
        start = pl.multiple_of((mine ^ index) * units, units)
        term = jnp.dot(
            rows_ref[...], down_ref[0, pl.ds(start, units), :], preferred_element_type=F32
        )
        total = term if total is None else total + term
    out_ref[...] = total.astype(BF16)


def block_outputs(info, hiddens, down_proj):
    tokens, units = hiddens[0].shape
    depth, columns = down_proj.shape[1:]
    tile = 512
    return pl.pallas_call(
        down_kernel,
        grid_spec=pltpu.PrefetchScalarGridSpec(
            num_scalar_prefetch=1,
            grid=(columns // tile,),
            in_specs=[pl.BlockSpec((tokens, units), lambda n, i: (0, 0)) for _ in hiddens]
            + [pl.BlockSpec((1, depth, tile), lambda n, i: (0, 0, n))],
            out_specs=pl.BlockSpec((tokens, tile), lambda n, i: (0, n)),
        ),
        out_shape=jax.ShapeDtypeStruct((tokens, columns), BF16),
        compiler_params=pltpu.CompilerParams(vmem_limit_bytes=VMEM_LIMIT),
        name="block_outputs",
    )(info, *hiddens, down_proj)


def swap(array, axis):
    return lax.ppermute(array, axis, [(0, 1), (1, 0)])


def on_device(
    queries,
    new_keys,
    new_values,
    cached_key_rows,
    cache_values,
    cache_lengths,
    norm_gain,
    routes,
    gates,
    gate_proj,
    up_proj,
    down_proj,
):
    new_dev, sequences, q_width = queries.shape
    half = q_width // 2
    half_heads = half // HEAD_SIZE
    z, y, x_lo, x_hi, core = (lax.axis_index(name) for name in ("z", "y", "xl", "xh", "c"))
    z_size, y_size = lax.axis_size("z"), lax.axis_size("y")
    column = z * y_size + y
    columns = z_size * y_size
    ctx_index = column * 2 + x_lo
    ctx_size = 2 * columns
    token_rows = new_dev * sequences

    packed = []
    for cached, new in ((cached_key_rows, new_keys), (cache_values, new_values)):
        packed.append(jnp.concatenate([cached, new], axis=0))
    both = jnp.stack(packed).reshape(2, -1, sequences, 2, HEAD_SIZE)
    low = jnp.transpose(both[:, :, :, 0], (0, 2, 1, 3))
    high = jnp.transpose(both[:, :, :, 1], (0, 2, 1, 3))
    mine = jnp.where(x_lo == 0, low, high)
    theirs = swap(jnp.where(x_lo == 0, high, low), "xl")
    partner_routes = swap(routes, "xl")

    halves = jnp.transpose(queries.reshape(new_dev, sequences, 2, half), (2, 1, 0, 3))
    sent = jnp.broadcast_to(halves[None], (columns, 2, sequences, new_dev, half)).reshape(
        ctx_size, sequences, new_dev, half
    )
    everyone = lax.all_to_all(sent, ("z", "y", "xl"), split_axis=0, concat_axis=0, tiled=True)

    info = jnp.stack(
        [cache_lengths[0], cache_lengths[1], ctx_index, ctx_index ^ 1, column]
    ).astype(jnp.int32)
    partial = attend(info, everyone, mine, theirs)
    got = lax.all_to_all(partial, ("z", "y"), split_axis=0, concat_axis=0, tiled=True)
    attended, square = merge(got)

    square = square[:, :, :1]
    others = [
        lax.ppermute(square, ("xl", "xh", "c"), [(i, i ^ k) for i in range(8)])
        for k in range(1, 8)
    ]
    summed = sum(others, square)
    inverse = lax.rsqrt(summed / (8 * half) + EPS)
    gain = norm_gain.astype(F32)
    own_gain = jnp.where(x_lo == 0, gain[:half], gain[half:])
    normed_half = attended * inverse * own_gain
    payload = normed_half.astype(BF16).reshape(sequences * 2 * new_dev, half)

    split = jnp.transpose(
        normed_half.reshape(sequences, 2, new_dev, half), (1, 2, 0, 3)
    )
    kept = jnp.where(x_lo == 0, split[0], split[1])
    came = swap(jnp.where(x_lo == 0, split[1], split[0]), "xl")
    normed = jnp.concatenate(
        [jnp.where(x_lo == 0, kept, came), jnp.where(x_lo == 0, came, kept)], axis=2
    )

    def slots_of(choice):
        flat = choice.reshape(token_rows * TOPK)
        count = flat.shape[0]
        earlier = jnp.arange(count)[None, :] < jnp.arange(count)[:, None]
        same = flat[:, None] == flat[None, :]
        return flat * CAP + jnp.sum((earlier & same).astype(jnp.int32), axis=1)

    own_target = slots_of(routes)
    partner_target = slots_of(partner_routes)
    targets = jnp.stack(
        [
            jnp.where(x_lo == 0, own_target, partner_target),
            jnp.where(x_lo == 0, partner_target, own_target),
        ]
    ).reshape(2, new_dev, sequences, TOPK)
    targets = jnp.transpose(targets, (2, 0, 1, 3))
    slot_ids = jnp.arange(EXPERTS * CAP).reshape(EXPERTS, 1, CAP, 1, 1, 1, 1)
    of_block = jnp.arange(2).reshape(1, 2, 1, 1, 1, 1, 1)
    block = jnp.arange(2).reshape(1, 1, 1, 1, 2, 1, 1)
    placing = jnp.any(
        (slot_ids == targets[None, None, None]) & (of_block == block), axis=-1
    ).reshape(EXPERTS * 2 * CAP, sequences * 2 * new_dev)
    placed = jnp.dot(placing.astype(BF16), payload, preferred_element_type=F32).astype(BF16)
    group = ctx_size // EXPERTS
    outgoing = jnp.broadcast_to(
        placed.reshape(EXPERTS, 1, 2 * CAP, half), (EXPERTS, 2 * group, 2 * CAP, half)
    ).reshape(2 * ctx_size, 2 * CAP, half)
    near = lax.all_to_all(
        outgoing, ("z", "y", "xl", "xh"), split_axis=0, concat_axis=0, tiled=True
    ).reshape(columns, 4, 2 * CAP, half)
    far = swap(near, "c")

    place = jnp.stack([core, x_hi * 2 + core]).astype(jnp.int32)
    hidden = hidden_units(place, near, far, gate_proj, up_proj)
    hidden_core = swap(hidden, "c")
    hidden_far = swap(hidden, "xh")
    hidden_both = swap(hidden_far, "c")
    produced = block_outputs(place, (hidden, hidden_core, hidden_far, hidden_both), down_proj)
    returned = lax.all_to_all(
        produced.reshape(ctx_size, CAP, q_width),
        ("z", "y", "xl"),
        split_axis=0,
        concat_axis=0,
        tiled=True,
    )

    slot_index = jnp.arange(EXPERTS * CAP).reshape(EXPERTS, 1, CAP, 1, 1)
    weighting = jnp.sum(
        jnp.where(
            slot_index == own_target.reshape(1, 1, 1, token_rows, TOPK),
            gates.reshape(1, 1, 1, token_rows, TOPK),
            0.0,
        ),
        axis=-1,
    )
    weighting = jnp.broadcast_to(weighting, (EXPERTS, group, CAP, token_rows)).reshape(
        ctx_size * CAP, token_rows
    )
    high_part = weighting.astype(BF16)
    rest = weighting - high_part.astype(F32)
    middle_part = rest.astype(BF16)
    low_part = (rest - middle_part.astype(F32)).astype(BF16)
    table = jnp.concatenate([high_part, middle_part, low_part], axis=1)
    mixed = lax.dot_general(
        table,
        returned.reshape(ctx_size * CAP, q_width),
        (((0,), (0,)), ((), ())),
        preferred_element_type=F32,
    ).reshape(3, token_rows, q_width)
    moe_out = (mixed[0] + mixed[1] + mixed[2]).reshape(new_dev, sequences, q_width)
    return (normed, moe_out)


def solution(mesh):
    fine = Mesh(mesh.devices.reshape(4, 4, 2, 2, 2), ("z", "y", "xl", "xh", "c"))
    ctx = ("z", "y", "xl")
    tp = ("xh", "c")
    split = P(ctx, None, tp)
    placed = (
        split,
        split,
        split,
        split,
        split,
        P(),
        P(tp),
        P(ctx, None, None),
        P(ctx, None, None),
        split,
        split,
        split,
    )
    return jax.shard_map(
        on_device,
        mesh=fine,
        in_specs=placed,
        out_specs=(split, split),
        check_vma=False,
    )
```

time: 588 us -> 231 us (0.39); the launches traced: 578 us -> 230 us
  waiting for transfers between devices: 226 us -> 95 us
  blocking collectives: 154 us -> 46.3 us
  local copies, waits for them, and re-layouts: 82.3 us -> 7.15 us
  Pallas kernels: 0 us -> 42 us
  matrix products: 39.1 us -> 0.68 us
  other arithmetic: 24.2 us -> 4.71 us
  between operations: 14.9 us -> 0.99 us
    all_gather x2 -> x0, waiting for transfers between devices: 173 us -> none  [the longest x1 150 us: on_device(): everyone = lax.all_gather(queries, 'ctx', axis=0, tiled=True)]
    ppermute x0 -> x14, waiting for transfers between devices: none -> 71.7 us  [the longest x7 69.1 us: swap(): return lax.ppermute(array, axis, [(0, 1), (1, 0)])]
    all_gather x2 -> x0, blocking collectives: 62.2 us -> none  [the longest x1 52 us: on_device(): lax.all_gather(norm_gain.astype(jnp.float32), 'tp', axis=0, tiled=True)]
    all_to_all x1, blocking collectives: 91.8 us -> 46.3 us  [on_device(): lax.all_to_all(outgoing, ('z', 'y', 'xl', 'xh'), split_axis=0, concat_axi...]
    pallas_call x0 -> x4, Pallas kernels: none -> 42 us  [the longest x1 19.5 us: attend(): pl.pallas_call(lambda *refs: attention_kernel(*refs, chunks=chunks), grid...]
    dot_general x9 -> x2, matrix products: 39.1 us -> 0.68 us  [the longest x1 0.39 us: on_device(): lax.dot_general(table, returned.reshape(ctx_size * CAP, q_width), (((0,),...]
    all_to_all x4 -> x3, waiting for transfers between devices: 52.6 us -> 23.3 us  [the longest x1 20.9 us: on_device(): lax.all_to_all(partial, ('z', 'y'), split_axis=0, concat_axis=0, tiled=True)]
    unnamed x55 -> x17, local copies, waits for them, and re-layouts: 26.5 us -> 0.29 us
  transfers between devices with their start and end apart: 6 -> 17, of which waited for: 4 -> 10; matrix products, arithmetic and copies ran while one was open for 14% -> 4% of each run, Pallas kernels for 0% -> 0%
where the time goes in v1:
time: 231 us; the launch traced here: 230 us
  waiting for transfers between devices  95 us (41%)
  blocking collectives  46.3 us (20%)
  Pallas kernels  42 us (18%)
  starting transfers between devices  33.7 us (15%)
  local copies, waits for them, and re-layouts  7.15 us (3%)
  other arithmetic  4.71 us (2%)
    ppermute x7, waiting for transfers between devices, swap(): return lax.ppermute(array, axis, [(0, 1), (1, 0)])  69.1 us
    all_to_all x1, blocking collectives, on_device(): lax.all_to_all(outgoing, ('z', 'y', 'xl', 'xh'), split_axis=0, concat_axi...  46.3 us
    all_to_all x1, waiting for transfers between devices, on_device(): lax.all_to_all(partial, ('z', 'y'), split_axis=0, concat_axis=0, tiled=True)  20.9 us
    pallas_call x1, Pallas kernels, attend(): pl.pallas_call(lambda *refs: attention_kernel(*refs, chunks=chunks), grid...  19.5 us
    pallas_call x1, Pallas kernels, hidden_units(): pl.pallas_call(hidden_kernel, grid_spec=pltpu.PrefetchScalarGridSpec(num_...  12.8 us
    all_to_all x1, starting transfers between devices, on_device(): lax.all_to_all(sent, ('z', 'y', 'xl'), split_axis=0, concat_axis=0, tiled...  9.47 us
    ppermute x7, starting transfers between devices, on_device(): lax.ppermute(square, ('xl', 'xh', 'c'), [(i, i ^ k) for i in range(8)])  8.17 us
    pallas_call x1, Pallas kernels, block_outputs(): pl.pallas_call(down_kernel, grid_spec=pltpu.PrefetchScalarGridSpec(num_sc...  7.29 us
  transfers between devices with their start and end apart: 17, of which 10 were waited for; matrix products, arithmetic and copies ran while one was open for 4% of the time, Pallas kernels for 0%

profile of v1, /device:TPU:0, one launch (start us, length us, event | category | flops | bytes accessed | tf_op | source)
XLA Modules:
  0.0 230.5 jit_solution(1328616435622674419)
XLA Ops:
  1.6 1.4 broadcast_in_dim.22
  3.0 9.5 %all-to-all-start = ((bf16[32,2,16,768]{3,2,1,0:T(8,128)(2,1)}), bf16[32,2,16,768]{3,2,1,0:T(8,128)(2,1)S(1)}, u32[]{:S(2)}, u32[]{:S(2)}) async-start(bf16[32,2,16,768]{3,2,1,0:T(8,128)(2,1)} %bitcast.4), calls=%async_computation | async-start | bytes 3145728 | tf_op jit(solution)/shard_map/all_to_all | solution.py:321
  13.6 1.7 pad_maximum_fusion.1
  16.0 1.9 collective-permute-start
  17.9 25.5 %collective-permute-done.refs_3_ = bf16[2,2,528,128]{3,2,1,0:T(8,128)(2,1)S(1)} collective-permute-done((bf16[2,2,528,128]{3,2,1,0:T(8,128)(2,1)S(1)}, bf16[2,2,528,128]{3,2,1,0:T(8,128)(2,1)S(1)}, u32[]{:S(2)}, u32[]{:S(2)}) %collective-permute-start) | collective-permute-done | bytes 540704 | tf_op jit(solution)/shard_map/ppermute | solution.py:279
  43.4 19.5 %attend.1 = bf16[16,2,32,896]{3,2,1,0:T(8,128)(2,1)} custom-call(s32[5]{0:T(128)S(1)} %pad_add_fusion.refs_0_, bf16[32,2,16,768]{3,2,1,0:T(8,128)(2,1)S(1)} %all-to-all-done.refs_1_, bf16[2,2,528,128]{3,2,1,0:T(8,128)(2,1)S(1)} %get-tuple-element.9.refs_2_, bf16[2,2,528,128]{3,2,1,0:T(8,128)(2,1)S(1)} %collective-permute-done.refs_3_), custom_call_target="tpu_custom_call" | custom-call | tf_op jit(solution)/shard_map/attend/pallas_call | solution.py:113
  62.8 6.6 %all-to-all-start.1 = ((bf16[16,2,32,896]{3,2,1,0:T(8,128)(2,1)}), bf16[16,2,32,896]{3,2,1,0:T(8,128)(2,1)S(1)}, u32[]{:S(2)}, u32[]{:S(2)}) async-start(bf16[16,2,32,896]{3,2,1,0:T(8,128)(2,1)} %attend.1), calls=%async_computation.1 | async-start | bytes 3670016 | tf_op jit(solution)/shard_map/all_to_all | solution.py:327
  70.5 2.8 %collective-permute-done.9 = s32[16,2,2]{2,1,0:T(2,128)S(1)} collective-permute-done((s32[16,2,2]{2,1,0:T(2,128)S(1)}, s32[16,2,2]{2,1,0:T(2,128)S(1)}, u32[]{:S(2)}, u32[]{:S(2)}) %collective-permute-start.9) | collective-permute-done | bytes 288 | tf_op jit(solution)/shard_map/ppermute | solution.py:279
  74.3 20.9 %all-to-all-done.1.got_ref = bf16[16,2,32,896]{3,2,1,0:T(8,128)(2,1)S(1)} async-done(((bf16[16,2,32,896]{3,2,1,0:T(8,128)(2,1)}), bf16[16,2,32,896]{3,2,1,0:T(8,128)(2,1)S(1)}, u32[]{:S(2)}, u32[]{:S(2)}) %all-to-all-start.1) | async-done | bytes 1835040 | tf_op jit(solution)/shard_map/all_to_all | solution.py:327
  95.3 2.4 %merge.1 = (f32[2,32,768]{2,1,0:T(8,128)S(1)}, f32[2,32,128]{2,1,0:T(8,128)S(1)}) custom-call(bf16[16,2,32,896]{3,2,1,0:T(8,128)(2,1)S(1)} %all-to-all-done.1.got_ref), custom_call_target="tpu_custom_call" | custom-call | tf_op jit(solution)/shard_map/merge/pallas_call | solution.py:165
  98.6 1.9 collective-permute-start.6
  101.2 2.2 collective-permute-start.4
  105.5 1.3 collective-permute-start.1
  108.2 1.6 collective-permute-done.2
  110.7 46.3 %all_to_all.20 = bf16[64,32,768]{2,1,0:T(8,128)(2,1)S(1)} all-to-all(bf16[64,32,768]{2,1,0:T(8,128)(2,1)S(1)} %bitcast.55), channel_id=1, replica_groups=mesh['z'=4,'y'=4,'xl'=2,'xh'=2,'c'=2] {'z','y','xl','xh'}, dimensions={0} | all-to-all | bytes 6291456 | tf_op jit(solution)/shard_map/all_to_all | solution.py:378
  157.1 5.7 %collective-permute-done.10.far_ref = bf16[16,4,32,768]{3,2,1,0:T(8,128)(2,1)} collective-permute-done((bf16[16,4,32,768]{3,2,1,0:T(8,128)(2,1)S(1)}, bf16[16,4,32,768]{3,2,1,0:T(8,128)(2,1)}, u32[]{:S(2)}, u32[]{:S(2)}) %collective-permute-start.10) | collective-permute-done | bytes 3145760 | tf_op jit(solution)/shard_map/ppermute | solution.py:279
  162.8 12.8 %hidden_units.1.a_ref = bf16[512,512]{1,0:T(8,128)(2,1)S(1)} custom-call(s32[2]{0:T(128)S(1)} %pad_add_fusion.1.info_ref, bf16[16,4,32,768]{3,2,1,0:T(8,128)(2,1)S(1)} %bitcast.47, bf16[16,4,32,768]{3,2,1,0:T(8,128)(2,1)} %collective-permute-done.10.far_ref, bf16[1,6144,512]{2,1,0:T(8,128)(2,1)} %gate_ref.1, bf16[1,6144,512]{2,1,0:T(8,128)(2,1)} %up_ref.1), custom_call_target="tpu_custom_call" | custom-call | tf_op jit(solution)/shard_map/hidden_units/pallas_call | solution.py:220
  176.7 14.4 %collective-permute-done.12.c_ref = bf16[512,512]{1,0:T(8,128)(2,1)S(1)} collective-permute-done((bf16[512,512]{1,0:T(8,128)(2,1)S(1)}, bf16[512,512]{1,0:T(8,128)(2,1)S(1)}, u32[]{:S(2)}, u32[]{:S(2)}) %collective-permute-start.12) | collective-permute-done | bytes 524320 | tf_op jit(solution)/shard_map/ppermute | solution.py:279
  191.1 1.9 collective-permute-done.13.d_ref
  193.0 7.3 %block_outputs.1 = bf16[512,1536]{1,0:T(8,128)(2,1)} custom-call(s32[2]{0:T(128)S(1)} %pad_add_fusion.1.info_ref, bf16[512,512]{1,0:T(8,128)(2,1)S(1)} %hidden_units.1.a_ref, bf16[512,512]{1,0:T(8,128)(2,1)S(1)} %collective-permute-done.11.b_ref, bf16[512,512]{1,0:T(8,128)(2,1)S(1)} %collective-permute-done.12.c_ref, ...), custom_call_target="tpu_custom_call" | custom-call | tf_op jit(solution)/shard_map/block_outputs/pallas_call | solution.py:263
  200.3 4.1 %all-to-all-start.3 = ((bf16[32,16,1536]{2,1,0:T(8,128)(2,1)}), bf16[32,16,1536]{2,1,0:T(8,128)(2,1)S(1)}, u32[]{:S(2)}, u32[]{:S(2)}) async-start(bf16[32,16,1536]{2,1,0:T(8,128)(2,1)} %bitcast.24), calls=%async_computation.3 | async-start | bytes 3145728 | tf_op jit(solution)/shard_map/all_to_all | solution.py:389
  205.4 1.8 collective-permute-start.8
  207.1 18.9 %collective-permute-done.8 = f32[16,2,768]{2,1,0:T(2,128)S(1)} collective-permute-done((f32[16,2,768]{2,1,0:T(2,128)S(1)}, f32[16,2,768]{2,1,0:T(2,128)S(1)}, u32[]{:S(2)}, u32[]{:S(2)}) %collective-permute-start.8) | collective-permute-done | bytes 98336 | tf_op jit(solution)/shard_map/ppermute | solution.py:279
  226.9 2.4 %all-to-all-done.3 = bf16[32,16,1536]{2,1,0:T(8,128)(2,1)S(1)} async-done(((bf16[32,16,1536]{2,1,0:T(8,128)(2,1)}), bf16[32,16,1536]{2,1,0:T(8,128)(2,1)S(1)}, u32[]{:S(2)}, u32[]{:S(2)}) %all-to-all-start.3) | async-done | bytes 1572896 | tf_op jit(solution)/shard_map/all_to_all | solution.py:389
  (80 shorter events, 15.0 us)
Async XLA Ops:
  3.0 9.5 %copy-start = (bf16[512,2,256]{2,1,0:T(2,128)(2,1)S(1)}, bf16[512,2,256]{2,1,0:T(2,128)(2,1)}, u32[]{:S(2)}) copy-start(bf16[512,2,256]{2,1,0:T(2,128)(2,1)} %param.15) | copy-start | bytes 1572868
  3.0 9.5 %copy-start.1 = (bf16[16,2,256]{2,1,0:T(2,128)(2,1)S(1)}, bf16[16,2,256]{2,1,0:T(2,128)(2,1)}, u32[]{:S(2)}) copy-start(bf16[16,2,256]{2,1,0:T(2,128)(2,1)} %param.13) | copy-start | bytes 49156
  3.0 40.4 %all-to-all-start = ((bf16[32,2,16,768]{3,2,1,0:T(8,128)(2,1)}), bf16[32,2,16,768]{3,2,1,0:T(8,128)(2,1)S(1)}, u32[]{:S(2)}, u32[]{:S(2)}) async-start(bf16[32,2,16,768]{3,2,1,0:T(8,128)(2,1)} %bitcast.4), calls=%async_computation | async-start | bytes 3145728 | tf_op jit(solution)/shard_map/all_to_all | solution.py:321
  12.5 1.1 copy-start.2
  15.7 2.1 copy-start.6
  16.0 27.4 %collective-permute-start = (bf16[2,2,528,128]{3,2,1,0:T(8,128)(2,1)S(1)}, bf16[2,2,528,128]{3,2,1,0:T(8,128)(2,1)S(1)}, u32[]{:S(2)}, u32[]{:S(2)}) collective-permute-start(bf16[2,2,528,128]{3,2,1,0:T(8,128)(2,1)S(1)} %get-tuple-element.8), channel_id=1, source_target_pairs={{0,4},{4,0},{1,5},{5,1},{2,6},{6,2},{3,7},{7,3},{8,12},{12,8},{9,1... | collective-permute-start | bytes 1622024 | tf_op jit(solution)/shard_map/ppermute | solution.py:279
  62.8 6.6 %copy-start.4 = (s32[16,2,2]{0,2,1:T(2,128)S(1)}, s32[16,2,2]{0,2,1:T(2,128)}, u32[]{:S(2)}) copy-start(s32[16,2,2]{0,2,1:T(2,128)} %param.19) | copy-start | bytes 772
  62.8 7.4 %copy-start.3 = (bf16[1536]{0:T(1024)(128)(2,1)S(1)}, bf16[1536]{0:T(1024)(128)(2,1)}, u32[]{:S(2)}) copy-start(bf16[1536]{0:T(1024)(128)(2,1)} %param.18) | copy-start | bytes 9220
  62.8 32.4 %all-to-all-start.1 = ((bf16[16,2,32,896]{3,2,1,0:T(8,128)(2,1)}), bf16[16,2,32,896]{3,2,1,0:T(8,128)(2,1)S(1)}, u32[]{:S(2)}, u32[]{:S(2)}) async-start(bf16[16,2,32,896]{3,2,1,0:T(8,128)(2,1)} %attend.1), calls=%async_computation.1 | async-start | bytes 3670016 | tf_op jit(solution)/shard_map/all_to_all | solution.py:327
  69.6 3.7 %collective-permute-start.9 = (s32[16,2,2]{2,1,0:T(2,128)S(1)}, s32[16,2,2]{2,1,0:T(2,128)S(1)}, u32[]{:S(2)}, u32[]{:S(2)}) collective-permute-start(s32[16,2,2]{2,1,0:T(2,128)S(1)} %copy.83), channel_id=1, source_target_pairs={{0,4},{4,0},{1,5},{5,1},{2,6},{6,2},{3,7},{7,3},{8,12},{12,8},{9,1... | collective-permute-start | bytes 776 | tf_op jit(solution)/shard_map/ppermute | solution.py:279
  97.7 6.7 %collective-permute-start.7 = (f32[2,32,1]{2,1,0:T(8,128)S(1)}, f32[2,32,1]{2,1,0:T(8,128)S(1)}, u32[]{:S(2)}, u32[]{:S(2)}) collective-permute-start(f32[2,32,1]{2,1,0:T(8,128)S(1)} %bitcast.48), channel_id=1, source_target_pairs={{0,7},{1,6},{2,5},{3,4},{4,3},{5,2},{6,1},{7,0},{8,15},{9,14},{10,... | collective-permute-start | bytes 776 | tf_op jit(solution)/shard_map/ppermute | solution.py:332
  98.6 6.9 %collective-permute-start.6 = (f32[2,32,1]{2,1,0:T(8,128)S(1)}, f32[2,32,1]{2,1,0:T(8,128)S(1)}, u32[]{:S(2)}, u32[]{:S(2)}) collective-permute-start(f32[2,32,1]{2,1,0:T(8,128)S(1)} %bitcast.49), channel_id=1, source_target_pairs={{0,6},{1,7},{2,4},{3,5},{4,2},{5,3},{6,0},{7,1},{8,14},{9,15},{10,... | collective-permute-start | bytes 776 | tf_op jit(solution)/shard_map/ppermute | solution.py:332
  100.5 6.7 %collective-permute-start.5 = (f32[2,32,1]{2,1,0:T(8,128)S(1)}, f32[2,32,1]{2,1,0:T(8,128)S(1)}, u32[]{:S(2)}, u32[]{:S(2)}) collective-permute-start(f32[2,32,1]{2,1,0:T(8,128)S(1)} %bitcast.50), channel_id=1, source_target_pairs={{0,5},{1,4},{2,7},{3,6},{4,1},{5,0},{6,3},{7,2},{8,13},{9,12},{10,... | collective-permute-start | bytes 776 | tf_op jit(solution)/shard_map/ppermute | solution.py:332
  101.2 6.0 %collective-permute-start.4 = (f32[2,32,1]{2,1,0:T(8,128)S(1)}, f32[2,32,1]{2,1,0:T(8,128)S(1)}, u32[]{:S(2)}, u32[]{:S(2)}) collective-permute-start(f32[2,32,1]{2,1,0:T(8,128)S(1)} %bitcast.51), channel_id=1, source_target_pairs={{0,4},{1,5},{2,6},{3,7},{4,0},{5,1},{6,2},{7,3},{8,12},{9,13},{10,... | collective-permute-start | bytes 776 | tf_op jit(solution)/shard_map/ppermute | solution.py:332
  103.4 4.8 %collective-permute-start.3 = (f32[2,32,1]{2,1,0:T(8,128)S(1)}, f32[2,32,1]{2,1,0:T(8,128)S(1)}, u32[]{:S(2)}, u32[]{:S(2)}) collective-permute-start(f32[2,32,1]{2,1,0:T(8,128)S(1)} %bitcast.52), channel_id=1, source_target_pairs={{0,3},{1,2},{2,1},{3,0},{4,7},{5,6},{6,5},{7,4},{8,11},{9,10},{10,... | collective-permute-start | bytes 776 | tf_op jit(solution)/shard_map/ppermute | solution.py:332
  104.4 5.5 %collective-permute-start.2 = (f32[2,32,1]{2,1,0:T(8,128)S(1)}, f32[2,32,1]{2,1,0:T(8,128)S(1)}, u32[]{:S(2)}, u32[]{:S(2)}) collective-permute-start(f32[2,32,1]{2,1,0:T(8,128)S(1)} %bitcast.53), channel_id=1, source_target_pairs={{0,2},{1,3},{2,0},{3,1},{4,6},{5,7},{6,4},{7,5},{8,10},{9,11},{10,... | collective-permute-start | bytes 776 | tf_op jit(solution)/shard_map/ppermute | solution.py:332
  105.5 4.4 %collective-permute-start.1 = (f32[2,32,1]{2,1,0:T(8,128)S(1)}, f32[2,32,1]{2,1,0:T(8,128)S(1)}, u32[]{:S(2)}, u32[]{:S(2)}) collective-permute-start(f32[2,32,1]{2,1,0:T(8,128)S(1)} %bitcast.54), channel_id=1, source_target_pairs={{0,1},{1,0},{2,3},{3,2},{4,5},{5,4},{6,7},{7,6},{8,9},{9,8},{10,11... | collective-permute-start | bytes 776 | tf_op jit(solution)/shard_map/ppermute | solution.py:332
  157.0 5.8 %collective-permute-start.10 = (bf16[16,4,32,768]{3,2,1,0:T(8,128)(2,1)S(1)}, bf16[16,4,32,768]{3,2,1,0:T(8,128)(2,1)}, u32[]{:S(2)}, u32[]{:S(2)}) collective-permute-start(bf16[16,4,32,768]{3,2,1,0:T(8,128)(2,1)S(1)} %bitcast.46), channel_id=1, source_target_pairs={{0,1},{1,0},{2,3},{3,2},{4,5},{5,4},{6,7},{7,6},{8,9},{9,8},{10,11... | collective-permute-start | bytes 9437192 | tf_op jit(solution)/shard_map/ppermute | solution.py:279
  175.6 15.6 %collective-permute-start.12 = (bf16[512,512]{1,0:T(8,128)(2,1)S(1)}, bf16[512,512]{1,0:T(8,128)(2,1)S(1)}, u32[]{:S(2)}, u32[]{:S(2)}) collective-permute-start(bf16[512,512]{1,0:T(8,128)(2,1)S(1)} %hidden_units.1.a_ref), channel_id=1, source_target_pairs={{0,2},{2,0},{1,3},{3,1},{4,6},{6,4},{5,7},{7,5},{8,10},{10,8},{9,1... | collective-permute-start | bytes 1572872 | tf_op jit(solution)/shard_map/ppermute | solution.py:279
  176.7 14.4 %collective-permute-start.11 = (bf16[512,512]{1,0:T(8,128)(2,1)S(1)}, bf16[512,512]{1,0:T(8,128)(2,1)S(1)}, u32[]{:S(2)}, u32[]{:S(2)}) collective-permute-start(bf16[512,512]{1,0:T(8,128)(2,1)S(1)} %hidden_units.1.a_ref), channel_id=1, source_target_pairs={{0,1},{1,0},{2,3},{3,2},{4,5},{5,4},{6,7},{7,6},{8,9},{9,8},{10,11... | collective-permute-start | bytes 1572872 | tf_op jit(solution)/shard_map/ppermute | solution.py:279
  191.1 1.9 collective-permute-start.13
  200.3 4.2 %copy-start.5 = (f32[16,2,2]{0,2,1:T(2,128)S(1)}, f32[16,2,2]{0,2,1:T(2,128)}, u32[]{:S(2)}) copy-start(f32[16,2,2]{0,2,1:T(2,128)} %param.20) | copy-start | bytes 772
  200.3 28.9 %all-to-all-start.3 = ((bf16[32,16,1536]{2,1,0:T(8,128)(2,1)}), bf16[32,16,1536]{2,1,0:T(8,128)(2,1)S(1)}, u32[]{:S(2)}, u32[]{:S(2)}) async-start(bf16[32,16,1536]{2,1,0:T(8,128)(2,1)} %bitcast.24), calls=%async_computation.3 | async-start | bytes 3145728 | tf_op jit(solution)/shard_map/all_to_all | solution.py:389
  205.4 20.6 %collective-permute-start.8 = (f32[16,2,768]{2,1,0:T(2,128)S(1)}, f32[16,2,768]{2,1,0:T(2,128)S(1)}, u32[]{:S(2)}, u32[]{:S(2)}) collective-permute-start(f32[16,2,768]{2,1,0:T(2,128)S(1)} %select_bitcast_fusion.2), channel_id=1, source_target_pairs={{0,4},{4,0},{1,5},{5,1},{2,6},{6,2},{3,7},{7,3},{8,12},{12,8},{9,1... | collective-permute-start | bytes 294920 | tf_op jit(solution)/shard_map/ppermute | solution.py:279

commit v2 on v0

v2 whole, which is shorter than its diff:
```python
import math

import jax
import jax.numpy as jnp
from jax import lax
from jax.experimental import pallas as pl
from jax.experimental.pallas import tpu as pltpu
from jax.sharding import Mesh
from jax.sharding import PartitionSpec as P

HEAD_SIZE = 128
EXPERTS = 8
TOPK = 2
CAP = 16
EPS = 1e-05
DEAD = -1e30
LANES = 128
VMEM_LIMIT = 40 * 1024 * 1024

BF16 = jnp.bfloat16
F32 = jnp.float32


def attention_kernel(info_ref, q_ref, *refs, parts, last):
    key_parts, value_parts = refs[:parts], refs[parts : 2 * parts]
    if last:
        before_ref, before_lse_ref, out_ref, keys_ref, values_ref, lse_ref = refs[2 * parts :]
    else:
        out_ref, out_lse_ref, keys_ref, values_ref = refs[2 * parts :]
    sequence = pl.program_id(0)
    group = pl.program_id(1)
    sources, _, own_rows, width = q_ref.shape
    heads = width // HEAD_SIZE
    tokens = sources * own_rows
    count = key_parts[0].shape[0]
    padded = keys_ref.shape[0]
    cache = count - own_rows
    length = info_ref[sequence]
    z_index = info_ref[2]
    lane_index = info_ref[3]
    planes = info_ref[4]
    multiplier = 1.0 / math.sqrt(HEAD_SIZE)
    flag = 4 * own_rows

    for part in range(parts):
        plane = info_ref[5 + part]
        span = slice(part * count, (part + 1) * count)
        keys_ref[span, :LANES] = key_parts[part][...]
        values_ref[span, :LANES] = value_parts[part][...]
        row = lax.broadcasted_iota(jnp.int32, (count, LANES), 0)
        lane = lax.broadcasted_iota(jnp.int32, (count, LANES), 1)
        first = (plane * sources + lane_index) * cache
        dead = (lane == flag) & (row < cache) & (first + row >= length)
        late = (lane - plane * own_rows == row - cache) & (row >= cache)
        keys_ref[span, LANES:] = jnp.where(dead | late, DEAD, 0.0).astype(BF16)
    rest = padded - parts * count
    if rest:
        lane = lax.broadcasted_iota(jnp.int32, (rest, LANES), 1)
        keys_ref[parts * count :, :LANES] = jnp.zeros((rest, LANES), BF16)
        values_ref[parts * count :, :LANES] = jnp.zeros((rest, LANES), BF16)
        keys_ref[parts * count :, LANES:] = jnp.where(lane == flag, DEAD, 0.0).astype(BF16)
    values_ref[:, LANES:] = jnp.ones((padded, LANES), BF16)

    row = lax.broadcasted_iota(jnp.int32, (tokens, LANES), 0)
    lane = lax.broadcasted_iota(jnp.int32, (tokens, LANES), 1)
    position = z_index * tokens + row
    key_position = ((lane // own_rows) * sources + lane_index) * own_rows + lane % own_rows
    blocked = ((lane < planes * own_rows) & (position < key_position)) | (lane == flag)
    causal = jnp.where(blocked, 1.0, 0.0).astype(BF16)

    together = 2
    packed = None
    for start in range(0, heads, together):
        members = range(start, start + together)
        query = jnp.concatenate(
            [
                q_ref[:, 0, :, h * HEAD_SIZE : (h + 1) * HEAD_SIZE].reshape(tokens, HEAD_SIZE)
                for h in members
            ],
            axis=0,
        )
        wide = jnp.concatenate([query, jnp.concatenate([causal] * together, axis=0)], axis=1)
        scores = lax.dot_general(
            wide, keys_ref[...], (((1,), (1,)), ((), ())), preferred_element_type=F32
        )
        top = jnp.max(scores, axis=1, keepdims=True)
        expo = jnp.exp2((scores - top) * (multiplier * math.log2(math.e)))
        mixed = jnp.dot(expo.astype(BF16), values_ref[...], preferred_element_type=F32)
        total = mixed[:, LANES:]
        result = mixed[:, :LANES] / total
        lse = top * multiplier + jnp.log(total)
        rows = slice(start * tokens, (start + together) * tokens)
        if not last:
            out_ref[0, 0, rows] = result
            out_lse_ref[0, 0, rows] = lse
            continue
        other = before_lse_ref[0, 0, rows]
        peak = jnp.maximum(lse, other)
        here, there = jnp.exp(lse - peak), jnp.exp(other - peak)
        both = here + there
        result = (here * result + there * before_ref[0, 0, rows]) / both
        lse = peak + jnp.log(both)
        for place, h in enumerate(members):
            chosen = slice(place * tokens, (place + 1) * tokens)
            out_ref[:, 0, :, pl.ds(group * width + h * HEAD_SIZE, HEAD_SIZE)] = (
                result[chosen].astype(BF16).reshape(sources, own_rows, HEAD_SIZE)
            )
            mark = (lane % 16 == group * heads + h) & (lane < 48)
            packed = jnp.where(mark, lse[chosen], jnp.zeros((tokens, LANES), F32) if packed is None else packed)

    if last:
        @pl.when(group == 0)
        def _():
            lse_ref[...] = packed

        @pl.when(group == pl.num_programs(1) - 1)
        def _():
            value = lse_ref[...] + packed
            high = value.astype(BF16).astype(F32)
            middle = (value - high).astype(BF16).astype(F32)
            low = value - high - middle
            terms = jnp.where(lane < 16, high, jnp.where(lane < 32, middle, low)).astype(BF16)
            edge = out_ref.shape[3] - LANES
            out_ref[:, 0, :, edge:] = terms.reshape(sources, own_rows, LANES)


def attend(info, queries, keys, values, before=None):
    sources, sequences, own_rows, q_width = queries.shape
    parts = len(keys)
    count = keys[0].shape[0]
    groups = keys[0].shape[1] // HEAD_SIZE // sequences
    width = q_width // groups
    padded = -(-parts * count // LANES) * LANES
    rows = sources * own_rows * width // HEAD_SIZE
    key_spec = pl.BlockSpec((count, HEAD_SIZE), lambda s, g, i: (0, s * groups + g))
    state_spec = pl.BlockSpec((1, 1, rows, HEAD_SIZE), lambda s, g, i: (s, g, 0, 0))
    in_specs = [
        pl.BlockSpec((sources, 1, own_rows, width), lambda s, g, i: (0, s, 0, g))
    ] + [key_spec] * (2 * parts)
    scratch = [pltpu.VMEM((padded, 2 * LANES), BF16), pltpu.VMEM((padded, 2 * LANES), BF16)]
    args = [queries, *keys, *values]
    if before is None:
        state = jax.ShapeDtypeStruct((sequences, groups, rows, HEAD_SIZE), F32)
        out_specs, out_shape = [state_spec] * 2, [state] * 2
    else:
        in_specs += [state_spec] * 2
        args += list(before)
        out_specs = pl.BlockSpec(
            (sources, 1, own_rows, q_width + LANES), lambda s, g, i: (0, s, 0, 0)
        )
        out_shape = jax.ShapeDtypeStruct((sources, sequences, own_rows, q_width + LANES), BF16)
        scratch.append(pltpu.VMEM((sources * own_rows, LANES), F32))
    return pl.pallas_call(
        lambda *refs: attention_kernel(*refs, parts=parts, last=before is not None),
        grid_spec=pltpu.PrefetchScalarGridSpec(
            num_scalar_prefetch=1,
            grid=(sequences, groups),
            in_specs=in_specs,
            out_specs=out_specs,
            scratch_shapes=scratch,
        ),
        out_shape=out_shape,
        compiler_params=pltpu.CompilerParams(vmem_limit_bytes=VMEM_LIMIT),
        name="attend",
    )(info, *args)


def merge_kernel(got_ref, placing_ref, gain_ref, out_ref, square_ref, sent_ref):
    sources, sequences, own_rows, wide = got_ref.shape
    rows = sequences * own_rows
    width = wide - LANES
    parts = got_ref[:, :, :, width:].astype(F32).reshape(sources * rows, LANES)
    lse = parts + pltpu.roll(parts, LANES - 16, 1) + pltpu.roll(parts, LANES - 32, 1)
    lse = lse.reshape(sources, rows, LANES)
    weight = jnp.exp(lse - jnp.max(lse, axis=0, keepdims=True))
    weight = weight / jnp.sum(weight, axis=0, keepdims=True)
    pieces = []
    square = jnp.zeros((rows, LANES), F32)
    for head in range(width // HEAD_SIZE):
        lanes = slice(head * HEAD_SIZE, (head + 1) * HEAD_SIZE)
        merged = jnp.zeros((rows, HEAD_SIZE), F32)
        for source in range(sources):
            part = got_ref[source, :, :, lanes].astype(F32).reshape(rows, HEAD_SIZE)
            merged = merged + weight[source, :, head : head + 1] * part
        out_ref[:, :, lanes] = merged.reshape(sequences, own_rows, HEAD_SIZE)
        square = square + merged * merged
        pieces.append((merged * gain_ref[:, lanes]).astype(BF16))
    square = jnp.sum(square, axis=1, keepdims=True)
    square_ref[...] = jnp.broadcast_to(square, (rows, LANES))
    payload = jnp.concatenate(pieces, axis=1)
    placed = jnp.dot(placing_ref[...], payload, preferred_element_type=F32).astype(BF16)
    placed = placed.reshape(EXPERTS, CAP, width)
    copies = sent_ref.shape[0] // EXPERTS
    for expert in range(EXPERTS):
        for copy in range(copies):
            sent_ref[expert * copies + copy] = placed[expert]


def merge(got, placing, gain, targets):
    sources, sequences, own_rows, wide = got.shape
    width = wide - LANES
    return pl.pallas_call(
        merge_kernel,
        out_shape=[
            jax.ShapeDtypeStruct((sequences, own_rows, width), F32),
            jax.ShapeDtypeStruct((sequences * own_rows, LANES), F32),
            jax.ShapeDtypeStruct((targets, CAP, width), BF16),
        ],
        compiler_params=pltpu.CompilerParams(vmem_limit_bytes=VMEM_LIMIT),
        name="merge",
    )(got, placing, gain)


def hidden_kernel(info_ref, *refs, parts):
    rows_refs = refs[: sum(parts)]
    gate_ref, up_ref, scale_ref, out_ref, square_ref = refs[sum(parts) :]
    tile = pl.program_id(0)
    pieces = []
    place = 0
    for index, count in enumerate(parts):
        members = [rows_refs[place + i][...] for i in range(count)]
        place += count
        pieces.append((info_ref[index], members))

    @pl.when(tile == 0)
    def _():
        total = None
        for block, members in pieces:
            rows = jnp.concatenate(members, axis=0) if len(members) > 1 else members[0]
            for start in range(0, rows.shape[1], LANES):
                part = rows[:, start : start + LANES].astype(F32)
                term = part * part * scale_ref[block, :, start : start + LANES]
                total = term if total is None else total + term
        mean = jnp.sum(total, axis=1, keepdims=True) / (len(parts) * rows_refs[0].shape[1])
        square_ref[...] = jnp.broadcast_to(lax.rsqrt(mean + EPS), square_ref.shape)

    gate = up = None
    for block, members in pieces:
        rows = jnp.concatenate(members, axis=0) if len(members) > 1 else members[0]
        gate_term = jnp.dot(rows, gate_ref[block], preferred_element_type=F32)
        up_term = jnp.dot(rows, up_ref[block], preferred_element_type=F32)
        gate = gate_term if gate is None else gate + gate_term
        up = up_term if up is None else up + up_term
    inverse = square_ref[:, :1]
    gate = gate * inverse
    out_ref[...] = (gate / (1.0 + jnp.exp(-gate)) * (up * inverse)).astype(BF16)


def hidden_units(info, pieces, gate_proj, up_proj, scale):
    parts = [len(piece) for piece in pieces]
    rows = [part for piece in pieces for part in piece]
    tokens = sum(part.shape[0] for part in pieces[0])
    width = rows[0].shape[1]
    blocks = len(parts)
    units = gate_proj.shape[2]
    tile = units // 2
    weight = pl.BlockSpec((blocks, width, tile), lambda n, i: (0, 0, n))
    return pl.pallas_call(
        lambda *refs: hidden_kernel(*refs, parts=parts),
        grid_spec=pltpu.PrefetchScalarGridSpec(
            num_scalar_prefetch=1,
            grid=(units // tile,),
            in_specs=[pl.BlockSpec(part.shape, lambda n, i: (0, 0)) for part in rows]
            + [weight, weight, pl.BlockSpec((blocks, 1, width), lambda n, i: (0, 0, 0))],
            out_specs=pl.BlockSpec((tokens, tile), lambda n, i: (0, n)),
            scratch_shapes=[pltpu.VMEM((tokens, LANES), F32)],
        ),
        out_shape=jax.ShapeDtypeStruct((tokens, units), BF16),
        compiler_params=pltpu.CompilerParams(vmem_limit_bytes=VMEM_LIMIT),
        name="hidden_units",
    )(
        info,
        *rows,
        gate_proj.reshape(blocks, width, units),
        up_proj.reshape(blocks, width, units),
        scale,
    )


def down_kernel(info_ref, a_ref, b_ref, c_ref, d_ref, down_ref, *refs):
    mine = info_ref[0]
    units = a_ref.shape[1]
    total = None
    for index, rows_ref in enumerate((a_ref, b_ref, c_ref, d_ref)):
        start = pl.multiple_of((mine ^ index) * units, units)
        term = jnp.dot(
            rows_ref[...], down_ref[0, pl.ds(start, units), :], preferred_element_type=F32
        )
        total = term if total is None else total + term
    if len(refs) > 1:
        total = total + refs[0][...].astype(F32)
    refs[-1][...] = total.astype(BF16)


def block_outputs(info, hiddens, down_proj, added=None):
    tokens, units = hiddens[0].shape
    depth, columns = down_proj.shape[1:]
    tile = 512
    out_spec = pl.BlockSpec((tokens, tile), lambda n, i: (0, n))
    extra = [] if added is None else [added]
    return pl.pallas_call(
        down_kernel,
        grid_spec=pltpu.PrefetchScalarGridSpec(
            num_scalar_prefetch=1,
            grid=(columns // tile,),
            in_specs=[pl.BlockSpec((tokens, units), lambda n, i: (0, 0)) for _ in hiddens]
            + [pl.BlockSpec((1, depth, tile), lambda n, i: (0, 0, n))]
            + [out_spec] * len(extra),
            out_specs=out_spec,
        ),
        out_shape=jax.ShapeDtypeStruct((tokens, columns), BF16),
        compiler_params=pltpu.CompilerParams(vmem_limit_bytes=VMEM_LIMIT),
        name="block_outputs",
    )(info, *hiddens, down_proj, *extra)


def swap(array, axis):
    return lax.ppermute(array, axis, [(0, 1), (1, 0)])


def shift(array, axis, size, by):
    return lax.ppermute(array, axis, [(i, (i + by) % size) for i in range(size)])


def shift_x(array, by):
    index = [(x % 2) * 2 + x // 2 for x in range(4)]
    return lax.ppermute(
        array, ("xl", "xh"), [(index[x], index[(x + by) % 4]) for x in range(4)]
    )


def exchange_hidden(hidden):
    far = swap(hidden, "xh")
    return (hidden, swap(hidden, "c"), far, swap(far, "c"))


def on_device(
    queries,
    new_keys,
    new_values,
    cached_key_rows,
    cache_values,
    cache_lengths,
    norm_gain,
    routes,
    gates,
    gate_proj,
    up_proj,
    down_proj,
):
    new_dev, sequences, q_width = queries.shape
    z, y, x_lo, x_hi, core = (lax.axis_index(name) for name in ("z", "y", "xl", "xh", "c"))
    z_size, y_size = lax.axis_size("z"), lax.axis_size("y")
    columns = z_size * y_size
    token_rows = new_dev * sequences
    group = columns // EXPERTS

    def rows_of(cached, new):
        return jnp.concatenate([cached, new], axis=0).reshape(cached.shape[0] + new_dev, -1)

    own_keys = rows_of(cached_key_rows, new_keys)
    own_values = rows_of(cache_values, new_values)
    keys_up, values_up = shift(own_keys, "z", 4, 1), shift(own_values, "z", 4, 1)
    keys_down, values_down = shift(own_keys, "z", 4, -1), shift(own_values, "z", 4, -1)
    keys_far = shift(keys_up, "z", 4, 1)
    values_far = shift(values_down, "z", 4, -1)

    sent = jnp.broadcast_to(
        jnp.transpose(queries, (1, 0, 2))[None], (2 * y_size, sequences, new_dev, q_width)
    )
    everyone = lax.all_to_all(sent, ("y", "xl"), split_axis=0, concat_axis=0, tiled=True)

    basis = [cache_lengths[0], cache_lengths[1], z, y * 2 + x_lo, jnp.int32(4)]
    near_info = jnp.stack(basis + [z, (z + 3) % 4, (z + 1) % 4]).astype(jnp.int32)
    far_info = jnp.stack(basis + [(z + 2) % 4]).astype(jnp.int32)
    state = attend(
        near_info,
        everyone,
        (own_keys, keys_up, keys_down),
        (own_values, values_up, values_down),
    )
    partial = attend(far_info, everyone, (keys_far,), (values_far,), state)
    got = lax.all_to_all(partial, ("y", "xl"), split_axis=0, concat_axis=0, tiled=True)

    gain = norm_gain.astype(F32)
    gain_core = swap(norm_gain, "c")
    gain_pair = jnp.stack([norm_gain, gain_core])
    gain_pair = jnp.where(core == 0, gain_pair, gain_pair[::-1])
    gain_far = swap(gain_pair, "xh")
    gain_all = jnp.stack([gain_pair, gain_far])
    gain_all = jnp.where(x_hi == 0, gain_all, gain_all[::-1]).astype(F32)
    scales = (1.0 / (gain_all * gain_all)).reshape(4, 1, q_width)

    flat_routes = routes.reshape(token_rows * TOPK)
    order = jnp.arange(token_rows * TOPK)
    earlier = (order[None, :] < order[:, None]) & (flat_routes[:, None] == flat_routes[None, :])
    target = flat_routes * CAP + jnp.sum(earlier.astype(jnp.int32), axis=1)
    by_row = target.reshape(new_dev, sequences, TOPK)
    slot_ids = jnp.arange(EXPERTS * CAP).reshape(EXPERTS * CAP, 1, 1, 1)
    hits = slot_ids == by_row[None]
    placing = jnp.transpose(jnp.any(hits, axis=-1), (0, 2, 1)).reshape(EXPERTS * CAP, token_rows)
    weighting = jnp.sum(jnp.where(hits, gates[None], 0.0), axis=-1).reshape(
        EXPERTS, 1, CAP, token_rows
    )

    attended, square, outgoing = merge(
        got, placing.astype(BF16), gain.reshape(1, q_width), columns
    )
    own_block = lax.all_to_all(
        outgoing, ("z", "y"), split_axis=0, concat_axis=0, tiled=True
    ).reshape(columns * CAP, q_width)

    middle = own_block.shape[0] // 2
    from_below = shift_x(own_block, 1)
    from_above = shift_x(own_block, -1)
    far_low = shift_x(from_below[:middle], 1)
    far_high = shift_x(from_above[middle:], -1)
    own_other = swap(own_block, "c")
    below_other = swap(from_below, "c")
    above_other = swap(from_above, "c")
    far_low_other = swap(far_low, "c")
    far_high_other = swap(far_high, "c")

    below = ((x_hi * 2 + x_lo + 3) % 4) // 2
    above = ((x_hi * 2 + x_lo + 1) % 4) // 2
    first_info = jnp.stack(
        [below * 2 + core, below * 2 + 1 - core, above * 2 + core, above * 2 + 1 - core]
    ).astype(jnp.int32)
    second_info = jnp.stack(
        [
            x_hi * 2 + core,
            x_hi * 2 + 1 - core,
            (1 - x_hi) * 2 + core,
            (1 - x_hi) * 2 + 1 - core,
        ]
    ).astype(jnp.int32)
    place = jnp.reshape(x_hi * 2 + core, (1,)).astype(jnp.int32)
    hidden_first = hidden_units(
        first_info,
        ((from_below,), (below_other,), (from_above,), (above_other,)),
        gate_proj,
        up_proj,
        scales,
    )
    produced_first = block_outputs(place, exchange_hidden(hidden_first), down_proj)
    returned_first = swap(produced_first, "xl")
    hidden_second = hidden_units(
        second_info,
        ((own_block,), (own_other,), (far_low, far_high), (far_low_other, far_high_other)),
        gate_proj,
        up_proj,
        scales,
    )
    produced = block_outputs(
        place, exchange_hidden(hidden_second), down_proj, returned_first
    )

    square = square + swap(square, "c")
    square = square + swap(square, "xh")
    inverse = lax.rsqrt(square[:, :1] / (4 * q_width) + EPS).reshape(sequences, new_dev, 1)
    normed = jnp.transpose(attended * inverse * gain, (1, 0, 2))

    returned = lax.all_to_all(
        produced.reshape(columns, CAP, q_width),
        ("z", "y"),
        split_axis=0,
        concat_axis=0,
        tiled=True,
    )
    weighting = jnp.broadcast_to(weighting, (EXPERTS, group, CAP, token_rows)).reshape(
        columns * CAP, token_rows
    )
    high_part = weighting.astype(BF16)
    rest = weighting - high_part.astype(F32)
    middle_part = rest.astype(BF16)
    low_part = (rest - middle_part.astype(F32)).astype(BF16)
    table = jnp.concatenate([high_part, middle_part, low_part], axis=1)
    mixed = lax.dot_general(
        table,
        returned.reshape(columns * CAP, q_width),
        (((0,), (0,)), ((), ())),
        preferred_element_type=F32,
    ).reshape(3, token_rows, q_width)
    moe_out = (mixed[0] + mixed[1] + mixed[2]).reshape(new_dev, sequences, q_width)
    return (normed, moe_out)


def solution(mesh):
    fine = Mesh(mesh.devices.reshape(4, 4, 2, 2, 2), ("z", "y", "xl", "xh", "c"))
    ctx = ("z", "y", "xl")
    tp = ("xh", "c")
    split = P(ctx, None, tp)
    placed = (
        split,
        split,
        split,
        split,
        split,
        P(),
        P(tp),
        P(ctx, None, None),
        P(ctx, None, None),
        split,
        split,
        split,
    )
    return jax.shard_map(
        on_device,
        mesh=fine,
        in_specs=placed,
        out_specs=(split, split),
        check_vma=False,
    )
```

time: 588 us -> 195 us (0.33); the launches traced: 578 us -> 194 us
  blocking collectives: 154 us -> 0 us
  waiting for transfers between devices: 226 us -> 83.6 us
  local copies, waits for them, and re-layouts: 82.3 us -> 17 us
  Pallas kernels: 0 us -> 42.9 us
  matrix products: 39.1 us -> 0.25 us
  other arithmetic: 24.2 us -> 4.4 us
  between operations: 14.9 us -> 1.08 us
  starting transfers between devices: 37.5 us -> 44.6 us
    all_gather x2 -> x0, waiting for transfers between devices: 173 us -> none  [the longest x1 150 us: on_device(): everyone = lax.all_gather(queries, 'ctx', axis=0, tiled=True)]
    all_to_all x1 -> x0, blocking collectives: 91.8 us -> none  [on_device(): lax.all_to_all(outgoing, 'ctx', split_axis=0, concat_axis=0, tiled=True)]
    all_gather x2 -> x0, blocking collectives: 62.2 us -> none  [the longest x1 52 us: on_device(): lax.all_gather(norm_gain.astype(jnp.float32), 'tp', axis=0, tiled=True)]
    ppermute x0 -> x26, waiting for transfers between devices: none -> 49.1 us  [the longest x16 23.3 us: swap(): return lax.ppermute(array, axis, [(0, 1), (1, 0)])]
    pallas_call x0 -> x7, Pallas kernels: none -> 42.9 us  [the longest x2 19 us: attend(): pl.pallas_call(lambda *refs: attention_kernel(*refs, parts=parts, last=be...]
    dot_general x9 -> x1, matrix products: 39.1 us -> 0.25 us  [on_device(): lax.dot_general(table, returned.reshape(columns * CAP, q_width), (((0,),...]
    ppermute x0 -> x26, starting transfers between devices: none -> 24.7 us  [the longest x6 9.7 us: shift(): lax.ppermute(array, axis, [(i, (i + by) % size) for i in range(size)])]
    all_to_all x4, waiting for transfers between devices: 52.6 us -> 34.4 us  [the longest x1 13.4 us: on_device(): lax.all_to_all(produced.reshape(columns, CAP, q_width), ('z', 'y'), split...]
  transfers between devices with their start and end apart: 6 -> 30, of which waited for: 4 -> 14; matrix products, arithmetic and copies ran while one was open for 14% -> 4% of each run, Pallas kernels for 0% -> 18%
where the time goes in v2:
time: 195 us; the launch traced here: 194 us
  waiting for transfers between devices  83.6 us (43%)
  starting transfers between devices  44.6 us (23%)
  Pallas kernels  42.9 us (22%)
  local copies, waits for them, and re-layouts  17 us (9%)
  other arithmetic  4.4 us (2%)
    ppermute x16, waiting for transfers between devices, swap(): return lax.ppermute(array, axis, [(0, 1), (1, 0)])  23.3 us
    pallas_call x2, Pallas kernels, attend(): pl.pallas_call(lambda *refs: attention_kernel(*refs, parts=parts, last=be...  19 us
    pallas_call x2, Pallas kernels, hidden_units(): pl.pallas_call(lambda *refs: hidden_kernel(*refs, parts=parts), grid_spec...  16.2 us
    all_to_all x1, waiting for transfers between devices, on_device(): lax.all_to_all(produced.reshape(columns, CAP, q_width), ('z', 'y'), split...  13.4 us
    ppermute x6, waiting for transfers between devices, shift(): lax.ppermute(array, axis, [(i, (i + by) % size) for i in range(size)])  13 us
    unnamed x24, local copies, waits for them, and re-layouts  12.9 us
    ppermute x4, waiting for transfers between devices, shift_x(): lax.ppermute(array, ('xl', 'xh'), [(index[x], index[(x + by) % 4]) for x...  12.8 us
    all_to_all x1, waiting for transfers between devices, on_device(): lax.all_to_all(outgoing, ('z', 'y'), split_axis=0, concat_axis=0, tiled=T...  11.4 us
  transfers between devices with their start and end apart: 30, of which 14 were waited for; matrix products, arithmetic and copies ran while one was open for 4% of the time, Pallas kernels for 18%

profile of v2, /device:TPU:0, one launch (start us, length us, event | category | flops | bytes accessed | tf_op | source)
XLA Modules:
  0.0 193.9 jit_solution(7357637930703422126)
XLA Ops:
  6.4 2.2 %collective-permute-start.2 = (bf16[528,512]{1,0:T(8,128)(2,1)S(1)}, bf16[528,512]{1,0:T(8,128)(2,1)}, u32[]{:S(2)}, u32[]{:S(2)}) collective-permute-start(bf16[528,512]{1,0:T(8,128)(2,1)S(1)} %bitcast.44), channel_id=1, source_target_pairs={{0,96},{32,0},{64,32},{96,64},{1,97},{33,1},{65,33},{97,65},{2,98}... | collective-permute-start | bytes 1622024 | tf_op jit(solution)/shard_map/ppermute | solution.py:322
  10.5 5.5 %all-to-all-start = ((bf16[8,2,16,1536]{3,2,1,0:T(8,128)(2,1)}), bf16[8,2,16,1536]{3,2,1,0:T(8,128)(2,1)S(1)}, u32[]{:S(2)}, u32[]{:S(2)}) async-start(bf16[8,2,16,1536]{3,2,1,0:T(8,128)(2,1)} %broadcast_in_dim.18), calls=%async_computation | async-start | bytes 1572864 | tf_op jit(solution)/shard_map/all_to_all | solution.py:371
  19.0 2.8 %collective-permute-done.2.refs_7_ = bf16[528,512]{1,0:T(8,128)(2,1)} collective-permute-done((bf16[528,512]{1,0:T(8,128)(2,1)S(1)}, bf16[528,512]{1,0:T(8,128)(2,1)}, u32[]{:S(2)}, u32[]{:S(2)}) %collective-permute-start.2) | collective-permute-done | bytes 540704 | tf_op jit(solution)/shard_map/ppermute | solution.py:322
  21.8 3.3 %collective-permute-start.3 = (bf16[528,512]{1,0:T(8,128)(2,1)}, bf16[528,512]{1,0:T(8,128)(2,1)S(1)}, u32[]{:S(2)}, u32[]{:S(2)}) collective-permute-start(bf16[528,512]{1,0:T(8,128)(2,1)} %collective-permute-done.2.refs_7_), channel_id=1, source_target_pairs={{0,96},{32,0},{64,32},{96,64},{1,97},{33,1},{65,33},{97,65},{2,98}... | collective-permute-start | bytes 1622024 | tf_op jit(solution)/shard_map/ppermute | solution.py:322
  25.3 8.1 %collective-permute-done.4.refs_4_ = bf16[528,512]{1,0:T(8,128)(2,1)} collective-permute-done((bf16[528,512]{1,0:T(8,128)(2,1)S(1)}, bf16[528,512]{1,0:T(8,128)(2,1)}, u32[]{:S(2)}, u32[]{:S(2)}) %collective-permute-start.4) | collective-permute-done | bytes 540704 | tf_op jit(solution)/shard_map/ppermute | solution.py:322
  34.7 11.9 %attend.2 = (f32[2,2,768,128]{3,2,1,0:T(8,128)S(1)}, f32[2,2,768,128]{3,2,1,0:T(8,128)S(1)}) custom-call(s32[8]{0:T(128)S(1)} %stack.76.refs_0_, bf16[8,2,16,1536]{3,2,1,0:T(8,128)(2,1)S(1)} %all-to-all-done.refs_1_, bf16[528,512]{1,0:T(8,128)(2,1)S(1)} %bitcast.43, bf16[528,512]{1,0:T(8,128)(2,1)S(1)} %collective-permute-done.refs_3_, ...), custom_call_target="tpu_custom_call" | custom-call | tf_op jit(solution)/shard_map/attend/pallas_call | solution.py:153
  46.6 7.1 %attend.3 = bf16[8,2,16,1664]{3,2,1,0:T(8,128)(2,1)} custom-call(s32[6]{0:T(128)S(1)} %stack.73.refs_0_, bf16[8,2,16,1536]{3,2,1,0:T(8,128)(2,1)S(1)} %all-to-all-done.refs_1_, bf16[528,512]{1,0:T(8,128)(2,1)S(1)} %collective-permute-done.1.refs_2_, bf16[528,512]{1,0:T(8,128)(2,1)S(1)} %collective-permute-done.3.refs_3_, ...), custom_call_target="tpu_custom_call" | custom-call | tf_op jit(solution)/shard_map/attend/pallas_call | solution.py:153
  53.7 5.6 %all-to-all-start.1 = ((bf16[8,2,16,1664]{3,2,1,0:T(8,128)(2,1)}), bf16[8,2,16,1664]{3,2,1,0:T(8,128)(2,1)S(1)}, u32[]{:S(2)}, u32[]{:S(2)}) async-start(bf16[8,2,16,1664]{3,2,1,0:T(8,128)(2,1)} %attend.3), calls=%async_computation.1 | async-start | bytes 1703936 | tf_op jit(solution)/shard_map/all_to_all | solution.py:383
  60.2 9.6 %all-to-all-done.1.got_ref = bf16[8,2,16,1664]{3,2,1,0:T(8,128)(2,1)S(1)} async-done(((bf16[8,2,16,1664]{3,2,1,0:T(8,128)(2,1)}), bf16[8,2,16,1664]{3,2,1,0:T(8,128)(2,1)S(1)}, u32[]{:S(2)}, u32[]{:S(2)}) %all-to-all-start.1) | async-done | bytes 852000 | tf_op jit(solution)/shard_map/all_to_all | solution.py:383
  72.2 4.9 %all-to-all-start.2 = ((bf16[16,16,1536]{2,1,0:T(8,128)(2,1)}), bf16[16,16,1536]{2,1,0:T(8,128)(2,1)S(1)}, u32[]{:S(2)}, u32[]{:S(2)}) async-start(bf16[16,16,1536]{2,1,0:T(8,128)(2,1)} %get-tuple-element.11), calls=%async_computation.2 | async-start | bytes 1572864 | tf_op jit(solution)/shard_map/all_to_all | solution.py:409
  77.3 11.4 %all-to-all-done.2 = bf16[16,16,1536]{2,1,0:T(8,128)(2,1)S(1)} async-done(((bf16[16,16,1536]{2,1,0:T(8,128)(2,1)}), bf16[16,16,1536]{2,1,0:T(8,128)(2,1)S(1)}, u32[]{:S(2)}, u32[]{:S(2)}) %all-to-all-start.2) | async-done | bytes 786464 | tf_op jit(solution)/shard_map/all_to_all | solution.py:409
  94.0 12.6 %collective-permute-done.9.refs_1_ = bf16[256,1536]{1,0:T(8,128)(2,1)S(1)} collective-permute-done((bf16[256,1536]{1,0:T(8,128)(2,1)S(1)}, bf16[256,1536]{1,0:T(8,128)(2,1)S(1)}, u32[]{:S(2)}, u32[]{:S(2)}) %collective-permute-start.9) | collective-permute-done | bytes 786464 | tf_op jit(solution)/shard_map/ppermute | solution.py:327
  111.7 2.8 %copy-done = bf16[1,6144,512]{2,1,0:T(8,128)(2,1)S(1)} copy-done((bf16[1,6144,512]{2,1,0:T(8,128)(2,1)S(1)}, bf16[1,6144,512]{2,1,0:T(8,128)(2,1)}, u32[]{:S(2)}) %copy-start) | copy-done | bytes 6291480
  114.5 8.1 %hidden_units.3.a_ref = bf16[256,512]{1,0:T(8,128)(2,1)S(1)} custom-call(s32[4]{0:T(128)S(1)} %pad_add_fusion.1.refs_0_, bf16[256,1536]{1,0:T(8,128)(2,1)S(1)} %collective-permute-done.9.refs_1_, bf16[256,1536]{1,0:T(8,128)(2,1)} %collective-permute-done.20.refs_2_, bf16[256,1536]{1,0:T(8,128)(2,1)S(1)} %collective-permute-done.11.refs_3_, ...), custom_call_target="tpu_custom_call" | custom-call | tf_op jit(solution)/shard_map/hidden_units/pallas_call | solution.py:258
  123.7 8.6 %collective-permute-done.23.c_ref = bf16[256,512]{1,0:T(8,128)(2,1)S(1)} collective-permute-done((bf16[256,512]{1,0:T(8,128)(2,1)S(1)}, bf16[256,512]{1,0:T(8,128)(2,1)S(1)}, u32[]{:S(2)}, u32[]{:S(2)}) %collective-permute-start.23) | collective-permute-done | bytes 262176 | tf_op jit(solution)/shard_map/ppermute | solution.py:318
  134.2 2.8 %copy-done.2 = bf16[1,2048,1536]{2,1,0:T(8,128)(2,1)S(1)} copy-done((bf16[1,2048,1536]{2,1,0:T(8,128)(2,1)S(1)}, bf16[1,2048,1536]{2,1,0:T(8,128)(2,1)}, u32[]{:S(2)}) %copy-start.2) | copy-done | bytes 6291480
  137.0 2.6 %block_outputs.2 = bf16[256,1536]{1,0:T(8,128)(2,1)S(1)} custom-call(s32[1]{0:T(128)} %bitcast.10.info_ref, bf16[256,512]{1,0:T(8,128)(2,1)S(1)} %hidden_units.3.a_ref, bf16[256,512]{1,0:T(8,128)(2,1)S(1)} %collective-permute-done.22.b_ref, bf16[256,512]{1,0:T(8,128)(2,1)S(1)} %collective-permute-done.23.c_ref, ...), custom_call_target="tpu_custom_call" | custom-call | tf_op jit(solution)/shard_map/block_outputs/pallas_call | solution.py:301
  139.8 2.8 %copy-done.1 = bf16[1,6144,512]{2,1,0:T(8,128)(2,1)S(1)} copy-done((bf16[1,6144,512]{2,1,0:T(8,128)(2,1)S(1)}, bf16[1,6144,512]{2,1,0:T(8,128)(2,1)}, u32[]{:S(2)}) %copy-start.1) | copy-done | bytes 6291480
  142.6 8.1 %hidden_units.2.a_ref = bf16[256,512]{1,0:T(8,128)(2,1)S(1)} custom-call(s32[4]{0:T(128)S(1)} %pad_add_fusion.refs_0_, bf16[256,1536]{1,0:T(8,128)(2,1)S(1)} %bitcast.40, bf16[256,1536]{1,0:T(8,128)(2,1)S(1)} %collective-permute-done.8.refs_2_, bf16[128,1536]{1,0:T(8,128)(2,1)} %collective-permute-done.10.refs_3_, ...), custom_call_target="tpu_custom_call" | custom-call | tf_op jit(solution)/shard_map/hidden_units/pallas_call | solution.py:258
  152.8 12.0 %collective-permute-done.18.c_ref = bf16[256,512]{1,0:T(8,128)(2,1)S(1)} collective-permute-done((bf16[256,512]{1,0:T(8,128)(2,1)S(1)}, bf16[256,512]{1,0:T(8,128)(2,1)S(1)}, u32[]{:S(2)}, u32[]{:S(2)}) %collective-permute-start.18) | collective-permute-done | bytes 262176 | tf_op jit(solution)/shard_map/ppermute | solution.py:318
  168.2 2.8 %copy-done.3 = bf16[1,2048,1536]{2,1,0:T(8,128)(2,1)S(1)} copy-done((bf16[1,2048,1536]{2,1,0:T(8,128)(2,1)S(1)}, bf16[1,2048,1536]{2,1,0:T(8,128)(2,1)}, u32[]{:S(2)}) %copy-start.3) | copy-done | bytes 6291480
  171.0 3.4 %block_outputs.3 = bf16[256,1536]{1,0:T(8,128)(2,1)} custom-call(s32[1]{0:T(128)} %bitcast.10.info_ref, bf16[256,512]{1,0:T(8,128)(2,1)S(1)} %hidden_units.2.a_ref, bf16[256,512]{1,0:T(8,128)(2,1)S(1)} %collective-permute-done.17.b_ref, bf16[256,512]{1,0:T(8,128)(2,1)S(1)} %collective-permute-done.18.c_ref, ...), custom_call_target="tpu_custom_call" | custom-call | tf_op jit(solution)/shard_map/block_outputs/pallas_call | solution.py:301
  174.4 3.8 %all-to-all-start.3 = ((bf16[16,16,1536]{2,1,0:T(8,128)(2,1)}), bf16[16,16,1536]{2,1,0:T(8,128)(2,1)S(1)}, u32[]{:S(2)}, u32[]{:S(2)}) async-start(bf16[16,16,1536]{2,1,0:T(8,128)(2,1)} %bitcast.23), calls=%async_computation.3 | async-start | bytes 1572864 | tf_op jit(solution)/shard_map/all_to_all | solution.py:463
  179.3 13.4 %all-to-all-done.3 = bf16[16,16,1536]{2,1,0:T(8,128)(2,1)S(1)} async-done(((bf16[16,16,1536]{2,1,0:T(8,128)(2,1)}), bf16[16,16,1536]{2,1,0:T(8,128)(2,1)S(1)}, u32[]{:S(2)}, u32[]{:S(2)}) %all-to-all-start.3) | async-done | bytes 786464 | tf_op jit(solution)/shard_map/all_to_all | solution.py:463
  (110 shorter events, 36.4 us)
Async XLA Ops:
  2.5 16.5 %collective-permute-start = (bf16[528,512]{1,0:T(8,128)(2,1)S(1)}, bf16[528,512]{1,0:T(8,128)(2,1)S(1)}, u32[]{:S(2)}, u32[]{:S(2)}) collective-permute-start(bf16[528,512]{1,0:T(8,128)(2,1)S(1)} %bitcast.41), channel_id=1, source_target_pairs={{0,32},{32,64},{64,96},{96,0},{1,33},{33,65},{65,97},{97,1},{2,34}... | collective-permute-start | bytes 1622024 | tf_op jit(solution)/shard_map/ppermute | solution.py:322
  6.4 15.4 %collective-permute-start.2 = (bf16[528,512]{1,0:T(8,128)(2,1)S(1)}, bf16[528,512]{1,0:T(8,128)(2,1)}, u32[]{:S(2)}, u32[]{:S(2)}) collective-permute-start(bf16[528,512]{1,0:T(8,128)(2,1)S(1)} %bitcast.44), channel_id=1, source_target_pairs={{0,96},{32,0},{64,32},{96,64},{1,97},{33,1},{65,33},{97,65},{2,98}... | collective-permute-start | bytes 1622024 | tf_op jit(solution)/shard_map/ppermute | solution.py:322
  10.5 24.1 %all-to-all-start = ((bf16[8,2,16,1536]{3,2,1,0:T(8,128)(2,1)}), bf16[8,2,16,1536]{3,2,1,0:T(8,128)(2,1)S(1)}, u32[]{:S(2)}, u32[]{:S(2)}) async-start(bf16[8,2,16,1536]{3,2,1,0:T(8,128)(2,1)} %broadcast_in_dim.18), calls=%async_computation | async-start | bytes 1572864 | tf_op jit(solution)/shard_map/all_to_all | solution.py:371
  16.1 17.3 %collective-permute-start.4 = (bf16[528,512]{1,0:T(8,128)(2,1)S(1)}, bf16[528,512]{1,0:T(8,128)(2,1)}, u32[]{:S(2)}, u32[]{:S(2)}) collective-permute-start(bf16[528,512]{1,0:T(8,128)(2,1)S(1)} %bitcast.42), channel_id=1, source_target_pairs={{0,96},{32,0},{64,32},{96,64},{1,97},{33,1},{65,33},{97,65},{2,98}... | collective-permute-start | bytes 1622024 | tf_op jit(solution)/shard_map/ppermute | solution.py:322
  18.1 16.5 %collective-permute-start.5 = (bf16[528,512]{1,0:T(8,128)(2,1)S(1)}, bf16[528,512]{1,0:T(8,128)(2,1)}, u32[]{:S(2)}, u32[]{:S(2)}) collective-permute-start(bf16[528,512]{1,0:T(8,128)(2,1)S(1)} %bitcast.45), channel_id=1, source_target_pairs={{0,32},{32,64},{64,96},{96,0},{1,33},{33,65},{65,97},{97,1},{2,34}... | collective-permute-start | bytes 1622024 | tf_op jit(solution)/shard_map/ppermute | solution.py:322
  19.0 27.6 %collective-permute-start.1 = (bf16[528,512]{1,0:T(8,128)(2,1)S(1)}, bf16[528,512]{1,0:T(8,128)(2,1)S(1)}, u32[]{:S(2)}, u32[]{:S(2)}) collective-permute-start(bf16[528,512]{1,0:T(8,128)(2,1)S(1)} %collective-permute-done.refs_3_), channel_id=1, source_target_pairs={{0,32},{32,64},{64,96},{96,0},{1,33},{33,65},{65,97},{97,1},{2,34}... | collective-permute-start | bytes 1622024 | tf_op jit(solution)/shard_map/ppermute | solution.py:322
  21.8 24.8 %collective-permute-start.3 = (bf16[528,512]{1,0:T(8,128)(2,1)}, bf16[528,512]{1,0:T(8,128)(2,1)S(1)}, u32[]{:S(2)}, u32[]{:S(2)}) collective-permute-start(bf16[528,512]{1,0:T(8,128)(2,1)} %collective-permute-done.2.refs_7_), channel_id=1, source_target_pairs={{0,96},{32,0},{64,32},{96,64},{1,97},{33,1},{65,33},{97,65},{2,98}... | collective-permute-start | bytes 1622024 | tf_op jit(solution)/shard_map/ppermute | solution.py:322
  53.7 16.1 %all-to-all-start.1 = ((bf16[8,2,16,1664]{3,2,1,0:T(8,128)(2,1)}), bf16[8,2,16,1664]{3,2,1,0:T(8,128)(2,1)S(1)}, u32[]{:S(2)}, u32[]{:S(2)}) async-start(bf16[8,2,16,1664]{3,2,1,0:T(8,128)(2,1)} %attend.3), calls=%async_computation.1 | async-start | bytes 1703936 | tf_op jit(solution)/shard_map/all_to_all | solution.py:383
  72.2 16.5 %all-to-all-start.2 = ((bf16[16,16,1536]{2,1,0:T(8,128)(2,1)}), bf16[16,16,1536]{2,1,0:T(8,128)(2,1)S(1)}, u32[]{:S(2)}, u32[]{:S(2)}) async-start(bf16[16,16,1536]{2,1,0:T(8,128)(2,1)} %get-tuple-element.11), calls=%async_computation.2 | async-start | bytes 1572864 | tf_op jit(solution)/shard_map/all_to_all | solution.py:409
  77.1 14.9 %collective-permute-start.15 = (bf16[1536]{0:T(1024)(128)(2,1)S(1)}, bf16[1536]{0:T(1024)(128)(2,1)S(1)}, u32[]{:S(2)}, u32[]{:S(2)}) collective-permute-start(bf16[1536]{0:T(1024)(128)(2,1)S(1)} %copy-done.6), channel_id=1, source_target_pairs={{0,1},{1,0},{2,3},{3,2},{4,5},{5,4},{6,7},{7,6},{8,9},{9,8},{10,11... | collective-permute-start | bytes 9224 | tf_op jit(solution)/shard_map/ppermute | solution.py:318
  88.7 18.0 %collective-permute-start.9 = (bf16[256,1536]{1,0:T(8,128)(2,1)S(1)}, bf16[256,1536]{1,0:T(8,128)(2,1)S(1)}, u32[]{:S(2)}, u32[]{:S(2)}) collective-permute-start(bf16[256,1536]{1,0:T(8,128)(2,1)S(1)} %bitcast.37), channel_id=1, source_target_pairs={{0,4},{4,2},{2,6},{6,0},{1,5},{5,3},{3,7},{7,1},{8,12},{12,10},{10... | collective-permute-start | bytes 2359304 | tf_op jit(solution)/shard_map/ppermute | solution.py:327
  90.7 16.2 %collective-permute-start.11 = (bf16[256,1536]{1,0:T(8,128)(2,1)S(1)}, bf16[256,1536]{1,0:T(8,128)(2,1)S(1)}, u32[]{:S(2)}, u32[]{:S(2)}) collective-permute-start(bf16[256,1536]{1,0:T(8,128)(2,1)S(1)} %bitcast.38), channel_id=1, source_target_pairs={{0,6},{4,0},{2,4},{6,2},{1,7},{5,1},{3,5},{7,3},{8,14},{12,8},{10,... | collective-permute-start | bytes 2359304 | tf_op jit(solution)/shard_map/ppermute | solution.py:327
  92.5 15.4 %collective-permute-start.16 = (bf16[2,1536]{1,0:T(2,128)(2,1)S(1)}, bf16[2,1536]{1,0:T(2,128)(2,1)S(1)}, u32[]{:S(2)}, u32[]{:S(2)}) collective-permute-start(bf16[2,1536]{1,0:T(2,128)(2,1)S(1)} %broadcast_select_fusion.1), channel_id=1, source_target_pairs={{0,2},{2,0},{1,3},{3,1},{4,6},{6,4},{5,7},{7,5},{8,10},{10,8},{9,1... | collective-permute-start | bytes 18440 | tf_op jit(solution)/shard_map/ppermute | solution.py:318
  108.0 31.8 %collective-permute-start.8 = (bf16[256,1536]{1,0:T(8,128)(2,1)S(1)}, bf16[256,1536]{1,0:T(8,128)(2,1)S(1)}, u32[]{:S(2)}, u32[]{:S(2)}) collective-permute-start(bf16[256,1536]{1,0:T(8,128)(2,1)S(1)} %bitcast.39), channel_id=1, source_target_pairs={{0,1},{1,0},{2,3},{3,2},{4,5},{5,4},{6,7},{7,6},{8,9},{9,8},{10,11... | collective-permute-start | bytes 2359304 | tf_op jit(solution)/shard_map/ppermute | solution.py:318
  108.3 24.0 %collective-permute-start.10 = (bf16[128,1536]{1,0:T(8,128)(2,1)S(1)}, bf16[128,1536]{1,0:T(8,128)(2,1)}, u32[]{:S(2)}, u32[]{:S(2)}) collective-permute-start(bf16[128,1536]{1,0:T(8,128)(2,1)S(1)} %slice.33), channel_id=1, source_target_pairs={{0,4},{4,2},{2,6},{6,0},{1,5},{5,3},{3,7},{7,1},{8,12},{12,10},{10... | collective-permute-start | bytes 1179656 | tf_op jit(solution)/shard_map/ppermute | solution.py:327
  109.6 23.3 %collective-permute-start.12 = (bf16[128,1536]{1,0:T(8,128)(2,1)S(1)}, bf16[128,1536]{1,0:T(8,128)(2,1)}, u32[]{:S(2)}, u32[]{:S(2)}) collective-permute-start(bf16[128,1536]{1,0:T(8,128)(2,1)S(1)} %slice.34), channel_id=1, source_target_pairs={{0,6},{4,0},{2,4},{6,2},{1,7},{5,1},{3,5},{7,3},{8,14},{12,8},{10,... | collective-permute-start | bytes 1179656 | tf_op jit(solution)/shard_map/ppermute | solution.py:327
  122.6 9.7 %collective-permute-start.23 = (bf16[256,512]{1,0:T(8,128)(2,1)S(1)}, bf16[256,512]{1,0:T(8,128)(2,1)S(1)}, u32[]{:S(2)}, u32[]{:S(2)}) collective-permute-start(bf16[256,512]{1,0:T(8,128)(2,1)S(1)} %hidden_units.3.a_ref), channel_id=1, source_target_pairs={{0,2},{2,0},{1,3},{3,1},{4,6},{6,4},{5,7},{7,5},{8,10},{10,8},{9,1... | collective-permute-start | bytes 786440 | tf_op jit(solution)/shard_map/ppermute | solution.py:318
  123.7 9.2 %collective-permute-start.22 = (bf16[256,512]{1,0:T(8,128)(2,1)S(1)}, bf16[256,512]{1,0:T(8,128)(2,1)S(1)}, u32[]{:S(2)}, u32[]{:S(2)}) collective-permute-start(bf16[256,512]{1,0:T(8,128)(2,1)S(1)} %hidden_units.3.a_ref), channel_id=1, source_target_pairs={{0,1},{1,0},{2,3},{3,2},{4,5},{5,4},{6,7},{7,6},{8,9},{9,8},{10,11... | collective-permute-start | bytes 786440 | tf_op jit(solution)/shard_map/ppermute | solution.py:318
  132.3 7.4 %collective-permute-start.13 = (bf16[128,1536]{1,0:T(8,128)(2,1)}, bf16[128,1536]{1,0:T(8,128)(2,1)}, u32[]{:S(2)}, u32[]{:S(2)}) collective-permute-start(bf16[128,1536]{1,0:T(8,128)(2,1)} %collective-permute-done.10.refs_3_), channel_id=1, source_target_pairs={{0,1},{1,0},{2,3},{3,2},{4,5},{5,4},{6,7},{7,6},{8,9},{9,8},{10,11... | collective-permute-start | bytes 1179656 | tf_op jit(solution)/shard_map/ppermute | solution.py:318
  139.6 28.6 %collective-permute-start.25 = (bf16[256,1536]{1,0:T(8,128)(2,1)S(1)}, bf16[256,1536]{1,0:T(8,128)(2,1)S(1)}, u32[]{:S(2)}, u32[]{:S(2)}) collective-permute-start(bf16[256,1536]{1,0:T(8,128)(2,1)S(1)} %block_outputs.2), channel_id=1, source_target_pairs={{0,4},{4,0},{1,5},{5,1},{2,6},{6,2},{3,7},{7,3},{8,12},{12,8},{9,1... | collective-permute-start | bytes 2359304 | tf_op jit(solution)/shard_map/ppermute | solution.py:318
  150.7 14.1 %collective-permute-start.18 = (bf16[256,512]{1,0:T(8,128)(2,1)S(1)}, bf16[256,512]{1,0:T(8,128)(2,1)S(1)}, u32[]{:S(2)}, u32[]{:S(2)}) collective-permute-start(bf16[256,512]{1,0:T(8,128)(2,1)S(1)} %hidden_units.2.a_ref), channel_id=1, source_target_pairs={{0,2},{2,0},{1,3},{3,1},{4,6},{6,4},{5,7},{7,5},{8,10},{10,8},{9,1... | collective-permute-start | bytes 786440 | tf_op jit(solution)/shard_map/ppermute | solution.py:318
  152.8 15.4 %collective-permute-start.17 = (bf16[256,512]{1,0:T(8,128)(2,1)S(1)}, bf16[256,512]{1,0:T(8,128)(2,1)S(1)}, u32[]{:S(2)}, u32[]{:S(2)}) collective-permute-start(bf16[256,512]{1,0:T(8,128)(2,1)S(1)} %hidden_units.2.a_ref), channel_id=1, source_target_pairs={{0,1},{1,0},{2,3},{3,2},{4,5},{5,4},{6,7},{7,6},{8,9},{9,8},{10,11... | collective-permute-start | bytes 786440 | tf_op jit(solution)/shard_map/ppermute | solution.py:318
  166.4 11.8 %collective-permute-start.7 = (f32[32,128]{1,0:T(8,128)S(1)}, f32[32,128]{1,0:T(8,128)S(1)}, u32[]{:S(2)}, u32[]{:S(2)}) collective-permute-start(f32[32,128]{1,0:T(8,128)S(1)} %add.102), channel_id=1, source_target_pairs={{0,2},{2,0},{1,3},{3,1},{4,6},{6,4},{5,7},{7,5},{8,10},{10,8},{9,1... | collective-permute-start | bytes 49160 | tf_op jit(solution)/shard_map/ppermute | solution.py:318
  174.4 18.4 %all-to-all-start.3 = ((bf16[16,16,1536]{2,1,0:T(8,128)(2,1)}), bf16[16,16,1536]{2,1,0:T(8,128)(2,1)S(1)}, u32[]{:S(2)}, u32[]{:S(2)}) async-start(bf16[16,16,1536]{2,1,0:T(8,128)(2,1)} %bitcast.23), calls=%async_computation.3 | async-start | bytes 1572864 | tf_op jit(solution)/shard_map/all_to_all | solution.py:463
  (16 other events, 206.2 us)

commit v3 on v2

--- a/solution.py
+++ b/solution.py
@@ -15,7 +15,8 @@
 EPS = 1e-05
 DEAD = -1e30
 LANES = 128
-VMEM_LIMIT = 40 * 1024 * 1024
+VMEM_LIMIT = 20 * 1024 * 1024
+SMALL_LIMIT = 10 * 1024 * 1024
 
 BF16 = jnp.bfloat16
 F32 = jnp.float32
@@ -161,6 +162,11 @@
         ),
         out_shape=out_shape,
         compiler_params=pltpu.CompilerParams(vmem_limit_bytes=VMEM_LIMIT),
+        cost_estimate=cost(
+            8 * sequences * groups * rows * padded * HEAD_SIZE,
+            args,
+            sequences * groups * rows * padded,
+        ),
         name="attend",
     )(info, *args)
 
@@ -207,111 +213,114 @@
             jax.ShapeDtypeStruct((targets, CAP, width), BF16),
         ],
         compiler_params=pltpu.CompilerParams(vmem_limit_bytes=VMEM_LIMIT),
+        cost_estimate=cost(8 * got.size, [got, got]),
         name="merge",
     )(got, placing, gain)
 
 
 def hidden_kernel(info_ref, *refs, parts):
     rows_refs = refs[: sum(parts)]
-    gate_ref, up_ref, scale_ref, out_ref, square_ref = refs[sum(parts) :]
-    tile = pl.program_id(0)
+    gate_ref, up_ref, scale_ref, out_ref = refs[sum(parts) :]
+    units = out_ref.shape[1]
+    width = rows_refs[0].shape[1]
     pieces = []
     place = 0
     for index, count in enumerate(parts):
         members = [rows_refs[place + i][...] for i in range(count)]
         place += count
-        pieces.append((info_ref[index], members))
-
-    @pl.when(tile == 0)
-    def _():
-        total = None
-        for block, members in pieces:
-            rows = jnp.concatenate(members, axis=0) if len(members) > 1 else members[0]
-            for start in range(0, rows.shape[1], LANES):
-                part = rows[:, start : start + LANES].astype(F32)
-                term = part * part * scale_ref[block, :, start : start + LANES]
-                total = term if total is None else total + term
-        mean = jnp.sum(total, axis=1, keepdims=True) / (len(parts) * rows_refs[0].shape[1])
-        square_ref[...] = jnp.broadcast_to(lax.rsqrt(mean + EPS), square_ref.shape)
-
-    gate = up = None
-    for block, members in pieces:
-        rows = jnp.concatenate(members, axis=0) if len(members) > 1 else members[0]
-        gate_term = jnp.dot(rows, gate_ref[block], preferred_element_type=F32)
-        up_term = jnp.dot(rows, up_ref[block], preferred_element_type=F32)
-        gate = gate_term if gate is None else gate + gate_term
-        up = up_term if up is None else up + up_term
-    inverse = square_ref[:, :1]
-    gate = gate * inverse
-    out_ref[...] = (gate / (1.0 + jnp.exp(-gate)) * (up * inverse)).astype(BF16)
-
-
-def hidden_units(info, pieces, gate_proj, up_proj, scale):
+        rows = jnp.concatenate(members, axis=0) if count > 1 else members[0]
+        pieces.append((info_ref[index], rows))
+    total = None
+    for block, rows in pieces:
+        for start in range(0, width, LANES):
+            part = rows[:, start : start + LANES].astype(F32)
+            term = part * part * scale_ref[block, :, start : start + LANES]
+            total = term if total is None else total + term
+    mean = jnp.sum(total, axis=1, keepdims=True) / (len(parts) * width)
+    inverse = lax.rsqrt(mean + EPS)
+    tile = units // 2
+    for lane in range(0, units, tile):
+        gate = up = None
+        for block, rows in pieces:
+            span = pl.ds(pl.multiple_of(block * width, LANES), width)
+            gate_term = jnp.dot(
+                rows, gate_ref[span, lane : lane + tile], preferred_element_type=F32
+            )
+            up_term = jnp.dot(rows, up_ref[span, lane : lane + tile], preferred_element_type=F32)
+            gate = gate_term if gate is None else gate + gate_term
+            up = up_term if up is None else up + up_term
+        gate = gate * inverse
+        out_ref[:, lane : lane + tile] = (
+            gate / (1.0 + jnp.exp(-gate)) * (up * inverse)
+        ).astype(BF16)
+
+
+def hidden_units(info, pieces, w_gate, w_up, scale):
     parts = [len(piece) for piece in pieces]
     rows = [part for piece in pieces for part in piece]
     tokens = sum(part.shape[0] for part in pieces[0])
-    width = rows[0].shape[1]
-    blocks = len(parts)
-    units = gate_proj.shape[2]
-    tile = units // 2
-    weight = pl.BlockSpec((blocks, width, tile), lambda n, i: (0, 0, n))
     return pl.pallas_call(
         lambda *refs: hidden_kernel(*refs, parts=parts),
-        grid_spec=pltpu.PrefetchScalarGridSpec(
-            num_scalar_prefetch=1,
-            grid=(units // tile,),
-            in_specs=[pl.BlockSpec(part.shape, lambda n, i: (0, 0)) for part in rows]
-            + [weight, weight, pl.BlockSpec((blocks, 1, width), lambda n, i: (0, 0, 0))],
-            out_specs=pl.BlockSpec((tokens, tile), lambda n, i: (0, n)),
-            scratch_shapes=[pltpu.VMEM((tokens, LANES), F32)],
-        ),
-        out_shape=jax.ShapeDtypeStruct((tokens, units), BF16),
-        compiler_params=pltpu.CompilerParams(vmem_limit_bytes=VMEM_LIMIT),
+        in_specs=[pl.BlockSpec(memory_space=pltpu.SMEM)]
+        + [pl.BlockSpec(memory_space=pltpu.VMEM)] * (len(rows) + 3),
+        out_shape=jax.ShapeDtypeStruct((tokens, w_gate.shape[1]), BF16),
+        compiler_params=pltpu.CompilerParams(vmem_limit_bytes=SMALL_LIMIT),
+        cost_estimate=cost(4 * tokens * w_gate.size, [*rows, w_gate, w_up]),
         name="hidden_units",
-    )(
-        info,
-        *rows,
-        gate_proj.reshape(blocks, width, units),
-        up_proj.reshape(blocks, width, units),
-        scale,
-    )
+    )(info, *rows, w_gate, w_up, scale)
 
 
 def down_kernel(info_ref, a_ref, b_ref, c_ref, d_ref, down_ref, *refs):
     mine = info_ref[0]
     units = a_ref.shape[1]
-    total = None
-    for index, rows_ref in enumerate((a_ref, b_ref, c_ref, d_ref)):
-        start = pl.multiple_of((mine ^ index) * units, units)
-        term = jnp.dot(
-            rows_ref[...], down_ref[0, pl.ds(start, units), :], preferred_element_type=F32
+    tile = 512
+    for lane in range(0, down_ref.shape[1], tile):
+        total = None
+        for index, rows_ref in enumerate((a_ref, b_ref, c_ref, d_ref)):
+            start = pl.multiple_of((mine ^ index) * units, units)
+            term = jnp.dot(
+                rows_ref[...],
+                down_ref[pl.ds(start, units), lane : lane + tile],
+                preferred_element_type=F32,
+            )
+            total = term if total is None else total + term
+        result = total.astype(BF16)
+        if len(refs) == 1:
+            refs[0][:, lane : lane + tile] = result
+            continue
+        before_ref, out_ref = refs
+        sources, _, count, _ = out_ref.shape
+        here, there = pl.ds(info_ref[1], 1), pl.ds(1 - info_ref[1], 1)
+        out_ref[:, here, :, lane : lane + tile] = result.reshape(sources, 1, count, tile)
+        out_ref[:, there, :, lane : lane + tile] = before_ref[:, lane : lane + tile].reshape(
+            sources, 1, count, tile
         )
-        total = term if total is None else total + term
-    if len(refs) > 1:
-        total = total + refs[0][...].astype(F32)
-    refs[-1][...] = total.astype(BF16)
-
-
-def block_outputs(info, hiddens, down_proj, added=None):
-    tokens, units = hiddens[0].shape
-    depth, columns = down_proj.shape[1:]
-    tile = 512
-    out_spec = pl.BlockSpec((tokens, tile), lambda n, i: (0, n))
-    extra = [] if added is None else [added]
+
+
+def block_outputs(info, hiddens, w_down, before=None):
+    tokens = hiddens[0].shape[0]
+    columns = w_down.shape[1]
+    args = [*hiddens, w_down]
+    out_shape = (tokens, columns)
+    if before is not None:
+        args.append(before)
+        out_shape = (tokens // CAP, 2, CAP, columns)
     return pl.pallas_call(
         down_kernel,
-        grid_spec=pltpu.PrefetchScalarGridSpec(
-            num_scalar_prefetch=1,
-            grid=(columns // tile,),
-            in_specs=[pl.BlockSpec((tokens, units), lambda n, i: (0, 0)) for _ in hiddens]
-            + [pl.BlockSpec((1, depth, tile), lambda n, i: (0, 0, n))]
-            + [out_spec] * len(extra),
-            out_specs=out_spec,
-        ),
-        out_shape=jax.ShapeDtypeStruct((tokens, columns), BF16),
-        compiler_params=pltpu.CompilerParams(vmem_limit_bytes=VMEM_LIMIT),
+        in_specs=[pl.BlockSpec(memory_space=pltpu.SMEM)]
+        + [pl.BlockSpec(memory_space=pltpu.VMEM)] * len(args),
+        out_shape=jax.ShapeDtypeStruct(out_shape, BF16),
+        compiler_params=pltpu.CompilerParams(vmem_limit_bytes=SMALL_LIMIT),
+        cost_estimate=cost(2 * tokens * w_down.size, [w_down, w_down]),
         name="block_outputs",
-    )(info, *hiddens, down_proj, *extra)
+    )(info, *args)
+
+
+def cost(flops, arrays, transcendentals=0):
+    size = sum(array.size * array.dtype.itemsize for array in arrays)
+    return pl.CostEstimate(
+        flops=flops, bytes_accessed=size, transcendentals=transcendentals
+    )
 
 
 def swap(array, axis):
@@ -327,11 +336,6 @@
     return lax.ppermute(
         array, ("xl", "xh"), [(index[x], index[(x + by) % 4]) for x in range(4)]
     )
-
-
-def exchange_hidden(hidden):
-    far = swap(hidden, "xh")
-    return (hidden, swap(hidden, "c"), far, swap(far, "c"))
 
 
 def on_device(
@@ -384,11 +388,13 @@
 
     gain = norm_gain.astype(F32)
     gain_core = swap(norm_gain, "c")
-    gain_pair = jnp.stack([norm_gain, gain_core])
-    gain_pair = jnp.where(core == 0, gain_pair, gain_pair[::-1])
+    gain_pair = jnp.where(
+        core == 0, jnp.stack([norm_gain, gain_core]), jnp.stack([gain_core, norm_gain])
+    )
     gain_far = swap(gain_pair, "xh")
-    gain_all = jnp.stack([gain_pair, gain_far])
-    gain_all = jnp.where(x_hi == 0, gain_all, gain_all[::-1]).astype(F32)
+    gain_all = jnp.where(
+        x_hi == 0, jnp.stack([gain_pair, gain_far]), jnp.stack([gain_far, gain_pair])
+    ).astype(F32)
     scales = (1.0 / (gain_all * gain_all)).reshape(4, 1, q_width)
 
     flat_routes = routes.reshape(token_rows * TOPK)
@@ -406,9 +412,11 @@
     attended, square, outgoing = merge(
         got, placing.astype(BF16), gain.reshape(1, q_width), columns
     )
+    outgoing, scales = lax.optimization_barrier((outgoing, scales))
     own_block = lax.all_to_all(
         outgoing, ("z", "y"), split_axis=0, concat_axis=0, tiled=True
     ).reshape(columns * CAP, q_width)
+    w_gate, w_up, w_down = gate_proj[0], up_proj[0], down_proj[0]
 
     middle = own_block.shape[0] // 2
     from_below = shift_x(own_block, 1)
@@ -418,8 +426,6 @@
     own_other = swap(own_block, "c")
     below_other = swap(from_below, "c")
     above_other = swap(from_above, "c")
-    far_low_other = swap(far_low, "c")
-    far_high_other = swap(far_high, "c")
 
     below = ((x_hi * 2 + x_lo + 3) % 4) // 2
     above = ((x_hi * 2 + x_lo + 1) % 4) // 2
@@ -434,25 +440,39 @@
             (1 - x_hi) * 2 + 1 - core,
         ]
     ).astype(jnp.int32)
-    place = jnp.reshape(x_hi * 2 + core, (1,)).astype(jnp.int32)
+    place = jnp.stack([x_hi * 2 + core, x_lo]).astype(jnp.int32)
     hidden_first = hidden_units(
         first_info,
         ((from_below,), (below_other,), (from_above,), (above_other,)),
-        gate_proj,
-        up_proj,
+        w_gate,
+        w_up,
         scales,
     )
-    produced_first = block_outputs(place, exchange_hidden(hidden_first), down_proj)
-    returned_first = swap(produced_first, "xl")
+    far_low, far_high, hidden_first = lax.optimization_barrier((far_low, far_high, hidden_first))
+    first_far, first_other = swap(hidden_first, "xh"), swap(hidden_first, "c")
     hidden_second = hidden_units(
         second_info,
-        ((own_block,), (own_other,), (far_low, far_high), (far_low_other, far_high_other)),
-        gate_proj,
-        up_proj,
+        (
+            (own_block,),
+            (own_other,),
+            (far_low, far_high),
+            (swap(far_low, "c"), swap(far_high, "c")),
+        ),
+        w_gate,
+        w_up,
         scales,
     )
+    first_far, hidden_second = lax.optimization_barrier((first_far, hidden_second))
+    second_far, second_other = swap(hidden_second, "xh"), swap(hidden_second, "c")
+    produced_first = block_outputs(
+        place, (hidden_first, first_other, first_far, swap(first_far, "c")), w_down
+    )
+    second_far, produced_first = lax.optimization_barrier((second_far, produced_first))
     produced = block_outputs(
-        place, exchange_hidden(hidden_second), down_proj, returned_first
+        place,
+        (hidden_second, second_other, second_far, swap(second_far, "c")),
+        w_down,
+        produced_first,
     )
 
     square = square + swap(square, "c")
@@ -460,15 +480,16 @@
     inverse = lax.rsqrt(square[:, :1] / (4 * q_width) + EPS).reshape(sequences, new_dev, 1)
     normed = jnp.transpose(attended * inverse * gain, (1, 0, 2))
 
+    rows_back = 2 * columns * CAP
     returned = lax.all_to_all(
-        produced.reshape(columns, CAP, q_width),
-        ("z", "y"),
+        produced.reshape(2 * columns, CAP, q_width),
+        ("z", "y", "xl"),
         split_axis=0,
         concat_axis=0,
         tiled=True,
     )
-    weighting = jnp.broadcast_to(weighting, (EXPERTS, group, CAP, token_rows)).reshape(
-        columns * CAP, token_rows
+    weighting = jnp.broadcast_to(weighting, (EXPERTS, 2 * group, CAP, token_rows)).reshape(
+        rows_back, token_rows
     )
     high_part = weighting.astype(BF16)
     rest = weighting - high_part.astype(F32)
@@ -477,7 +498,7 @@
     table = jnp.concatenate([high_part, middle_part, low_part], axis=1)
     mixed = lax.dot_general(
         table,
-        returned.reshape(columns * CAP, q_width),
+        returned.reshape(rows_back, q_width),
         (((0,), (0,)), ((), ())),
         preferred_element_type=F32,
     ).reshape(3, token_rows, q_width)

time: 195 us -> 180 us (0.923)
  waiting for transfers between devices: 83.6 us -> 57.4 us
  blocking collectives: 0 us -> 17.9 us
  Pallas kernels: 42.9 us -> 36 us
  local copies, waits for them, and re-layouts: 17 us -> 20.8 us
  starting transfers between devices: 44.6 us -> 42 us
    all_to_all x2 -> x1, waiting for transfers between devices: 24.8 us -> 2.2 us  [on_device(): lax.all_to_all(produced.reshape(2 * columns, CAP, q_width), ('z', 'y', 'x...]
    all_to_all x0 -> x1, blocking collectives: none -> 17.9 us  [on_device(): lax.all_to_all(outgoing, ('z', 'y'), split_axis=0, concat_axis=0, tiled=T...]
    all_to_all x1, waiting for transfers between devices: 9.61 us -> 0.97 us  [on_device(): lax.all_to_all(partial, ('y', 'xl'), split_axis=0, concat_axis=0, tiled=T...]
    pallas_call x4, Pallas kernels: 22.2 us -> 15.5 us  [the longest x2 9.61 us: hidden_units(): pl.pallas_call(lambda *refs: hidden_kernel(*refs, parts=parts), in_specs=...]
    ppermute x16 -> x15, waiting for transfers between devices: 23.3 us -> 29.5 us  [swap(): return lax.ppermute(array, axis, [(0, 1), (1, 0)])]
    unnamed x24 -> x34, local copies, waits for them, and re-layouts: 12.9 us -> 17.9 us
    all_to_all x2 -> x1, starting transfers between devices: 8.71 us -> 4.12 us  [on_device(): lax.all_to_all(produced.reshape(2 * columns, CAP, q_width), ('z', 'y', 'x...]
    ppermute x16 -> x15, starting transfers between devices: 8.35 us -> 10.4 us  [swap(): return lax.ppermute(array, axis, [(0, 1), (1, 0)])]
  transfers between devices with their start and end apart: 30 -> 28, of which waited for: 14 -> 13; matrix products, arithmetic and copies ran while one was open for 4% -> 3% of each run, Pallas kernels for 18% -> 18%
where the time goes in v3:
time: 180 us; the launch traced here: 179 us
  waiting for transfers between devices  57.4 us (32%)
  starting transfers between devices  42 us (23%)
  Pallas kernels  36 us (20%)
  local copies, waits for them, and re-layouts  20.8 us (12%)
  blocking collectives  17.9 us (10%)
  other arithmetic  3.44 us (2%)
    ppermute x15, waiting for transfers between devices, swap(): return lax.ppermute(array, axis, [(0, 1), (1, 0)])  29.5 us
    pallas_call x2, Pallas kernels, attend(): pl.pallas_call(lambda *refs: attention_kernel(*refs, parts=parts, last=be...  19.7 us
    all_to_all x1, blocking collectives, on_device(): lax.all_to_all(outgoing, ('z', 'y'), split_axis=0, concat_axis=0, tiled=T...  17.9 us
    unnamed x34, local copies, waits for them, and re-layouts  17.9 us
    ppermute x4, waiting for transfers between devices, shift_x(): lax.ppermute(array, ('xl', 'xh'), [(index[x], index[(x + by) % 4]) for x...  12.5 us
    ppermute x6, waiting for transfers between devices, shift(): lax.ppermute(array, axis, [(i, (i + by) % size) for i in range(size)])  12.2 us
    ppermute x15, starting transfers between devices, swap(): return lax.ppermute(array, axis, [(0, 1), (1, 0)])  10.4 us
    ppermute x6, starting transfers between devices, shift(): lax.ppermute(array, axis, [(i, (i + by) % size) for i in range(size)])  9.8 us
  transfers between devices with their start and end apart: 28, of which 13 were waited for; matrix products, arithmetic and copies ran while one was open for 3% of the time, Pallas kernels for 18%

profile of v3, /device:TPU:0, one launch (start us, length us, event | category | flops | bytes accessed | tf_op | source)
XLA Modules:
  0.0 179.0 jit_solution(16460048240092422351)
XLA Ops:
  8.7 5.4 %all-to-all-start = ((bf16[8,2,16,1536]{3,2,1,0:T(8,128)(2,1)}), bf16[8,2,16,1536]{3,2,1,0:T(8,128)(2,1)S(1)}, u32[]{:S(2)}, u32[]{:S(2)}) async-start(bf16[8,2,16,1536]{3,2,1,0:T(8,128)(2,1)} %broadcast_in_dim.18), calls=%async_computation | async-start | bytes 1572864 | tf_op jit(solution)/shard_map/all_to_all | solution.py:375
  16.7 2.7 %collective-permute-done.refs_3_ = bf16[528,512]{1,0:T(8,128)(2,1)S(1)} collective-permute-done((bf16[528,512]{1,0:T(8,128)(2,1)S(1)}, bf16[528,512]{1,0:T(8,128)(2,1)S(1)}, u32[]{:S(2)}, u32[]{:S(2)}) %collective-permute-start) | collective-permute-done | bytes 540704 | tf_op jit(solution)/shard_map/ppermute | solution.py:331
  20.7 3.3 %collective-permute-start.3 = (bf16[528,512]{1,0:T(8,128)(2,1)S(1)}, bf16[528,512]{1,0:T(8,128)(2,1)}, u32[]{:S(2)}, u32[]{:S(2)}) collective-permute-start(bf16[528,512]{1,0:T(8,128)(2,1)S(1)} %collective-permute-done.2.refs_7_), channel_id=1, source_target_pairs={{0,96},{32,0},{64,32},{96,64},{1,97},{33,1},{65,33},{97,65},{2,98}... | collective-permute-start | bytes 1622024 | tf_op jit(solution)/shard_map/ppermute | solution.py:331
  24.3 8.1 %collective-permute-done.4.refs_4_ = bf16[528,512]{1,0:T(8,128)(2,1)S(1)} collective-permute-done((bf16[528,512]{1,0:T(8,128)(2,1)S(1)}, bf16[528,512]{1,0:T(8,128)(2,1)S(1)}, u32[]{:S(2)}, u32[]{:S(2)}) %collective-permute-start.4) | collective-permute-done | bytes 540704 | tf_op jit(solution)/shard_map/ppermute | solution.py:331
  32.6 11.9 %attend.2 = (f32[2,2,768,128]{3,2,1,0:T(8,128)S(1)}, f32[2,2,768,128]{3,2,1,0:T(8,128)S(1)}) custom-call(s32[8]{0:T(128)S(1)} %stack.101.refs_0_, bf16[8,2,16,1536]{3,2,1,0:T(8,128)(2,1)S(1)} %all-to-all-done.refs_1_, bf16[528,512]{1,0:T(8,128)(2,1)S(1)} %bitcast.47, bf16[528,512]{1,0:T(8,128)(2,1)S(1)} %collective-permute-done.refs_3_, ...), custom_call_target="tpu_custom_call" | custom-call | flops 5234491392 | bytes 4030464 | tf_op jit(solution)/shard_map/attend/pallas_call | solution.py:154
  44.5 7.8 %attend.3 = bf16[8,2,16,1664]{3,2,1,0:T(8,128)(2,1)} custom-call(s32[6]{0:T(128)S(1)} %stack.98.refs_0_, bf16[8,2,16,1536]{3,2,1,0:T(8,128)(2,1)S(1)} %all-to-all-done.refs_1_, bf16[528,512]{1,0:T(8,128)(2,1)} %collective-permute-done.1.refs_2_, bf16[528,512]{1,0:T(8,128)(2,1)} %collective-permute-done.3.refs_3_, ...), custom_call_target="tpu_custom_call" | custom-call | flops 2013265920 | bytes 5013504 | tf_op jit(solution)/shard_map/attend/pallas_call | solution.py:154
  52.3 5.7 %all-to-all-start.1 = ((bf16[8,2,16,1664]{3,2,1,0:T(8,128)(2,1)}), bf16[8,2,16,1664]{3,2,1,0:T(8,128)(2,1)S(1)}, u32[]{:S(2)}, u32[]{:S(2)}) async-start(bf16[8,2,16,1664]{3,2,1,0:T(8,128)(2,1)} %attend.3), calls=%async_computation.1 | async-start | bytes 1703936 | tf_op jit(solution)/shard_map/all_to_all | solution.py:387
  58.4 2.8 %collective-permute-start.9 = (bf16[2,1536]{1,0:T(2,128)(2,1)S(1)}, bf16[2,1536]{1,0:T(2,128)(2,1)S(1)}, u32[]{:S(2)}, u32[]{:S(2)}) collective-permute-start(bf16[2,1536]{1,0:T(2,128)(2,1)S(1)} %broadcast_select_fusion.1), channel_id=1, source_target_pairs={{0,2},{2,0},{1,3},{3,1},{4,6},{6,4},{5,7},{7,5},{8,10},{10,8},{9,1... | collective-permute-start | bytes 18440 | tf_op jit(solution)/shard_map/ppermute | solution.py:327
  61.2 6.8 %collective-permute-done.9 = bf16[2,1536]{1,0:T(2,128)(2,1)S(1)} collective-permute-done((bf16[2,1536]{1,0:T(2,128)(2,1)S(1)}, bf16[2,1536]{1,0:T(2,128)(2,1)S(1)}, u32[]{:S(2)}, u32[]{:S(2)}) %collective-permute-start.9) | collective-permute-done | bytes 6176 | tf_op jit(solution)/shard_map/ppermute | solution.py:327
  69.9 17.9 %all_to_all.20 = bf16[16,16,1536]{2,1,0:T(8,128)(2,1)S(1)} all-to-all(bf16[16,16,1536]{2,1,0:T(8,128)(2,1)S(1)} %get-tuple-element.21), channel_id=1, replica_groups=mesh['z'=4,'y'=4,'xl'=2,'xh'=2,'c'=2] {'z','y'}, dimensions={0} | all-to-all | bytes 1572864 | tf_op jit(solution)/shard_map/all_to_all | solution.py:416
  91.0 12.5 %collective-permute-done.10.refs_1_ = bf16[256,1536]{1,0:T(8,128)(2,1)S(1)} collective-permute-done((bf16[256,1536]{1,0:T(8,128)(2,1)S(1)}, bf16[256,1536]{1,0:T(8,128)(2,1)S(1)}, u32[]{:S(2)}, u32[]{:S(2)}) %collective-permute-start.10) | collective-permute-done | bytes 786464 | tf_op jit(solution)/shard_map/ppermute | solution.py:336
  104.6 3.3 %collective-permute-start.13 = (bf16[128,1536]{1,0:T(8,128)(2,1)S(1)}, bf16[128,1536]{1,0:T(8,128)(2,1)}, u32[]{:S(2)}, u32[]{:S(2)}) collective-permute-start(bf16[128,1536]{1,0:T(8,128)(2,1)S(1)} %slice.34), channel_id=1, source_target_pairs={{0,6},{4,0},{2,4},{6,2},{1,7},{5,1},{3,5},{7,3},{8,14},{12,8},{10,... | collective-permute-start | bytes 1179656 | tf_op jit(solution)/shard_map/ppermute | solution.py:336
  107.9 2.8 %copy-done = bf16[1,6144,512]{2,1,0:T(8,128)(2,1)S(1)} copy-done((bf16[1,6144,512]{2,1,0:T(8,128)(2,1)S(1)}, bf16[1,6144,512]{2,1,0:T(8,128)(2,1)}, u32[]{:S(2)}) %copy-start) | copy-done | bytes 6291480
  110.7 2.8 %copy-done.2 = bf16[1,6144,512]{2,1,0:T(8,128)(2,1)S(1)} copy-done((bf16[1,6144,512]{2,1,0:T(8,128)(2,1)S(1)}, bf16[1,6144,512]{2,1,0:T(8,128)(2,1)}, u32[]{:S(2)}) %copy-start.2) | copy-done | bytes 6291480
  113.5 4.6 %hidden_units.2.a_ref = bf16[256,512]{1,0:T(8,128)(2,1)S(1)} custom-call(s32[4]{0:T(128)S(1)} %pad_add_fusion.1.refs_0_, bf16[256,1536]{1,0:T(8,128)(2,1)S(1)} %collective-permute-done.10.refs_1_, bf16[256,1536]{1,0:T(8,128)(2,1)S(1)} %collective-permute-done.14.refs_2_, bf16[256,1536]{1,0:T(8,128)(2,1)S(1)} %collective-permute-done.12.refs_3_, ...), custom_call_target="tpu_custom_call" | custom-call | flops 3221225472 | bytes 15728640 | tf_op jit(solution)/shard_map/hidden_units/pallas_call | solution.py:262
  120.7 2.8 %copy-done.1 = bf16[1,6144,512]{2,1,0:T(8,128)(2,1)S(1)} copy-done((bf16[1,6144,512]{2,1,0:T(8,128)(2,1)S(1)}, bf16[1,6144,512]{2,1,0:T(8,128)(2,1)}, u32[]{:S(2)}) %copy-start.1) | copy-done | bytes 6291480
  123.5 2.8 %copy-done.3 = bf16[1,6144,512]{2,1,0:T(8,128)(2,1)S(1)} copy-done((bf16[1,6144,512]{2,1,0:T(8,128)(2,1)S(1)}, bf16[1,6144,512]{2,1,0:T(8,128)(2,1)}, u32[]{:S(2)}) %copy-start.3) | copy-done | bytes 6291480
  126.3 5.0 %hidden_units.3.a_ref = bf16[256,512]{1,0:T(8,128)(2,1)S(1)} custom-call(s32[4]{0:T(128)S(1)} %pad_add_fusion.2.refs_0_, bf16[256,1536]{1,0:T(8,128)(2,1)S(1)} %bitcast.44, bf16[256,1536]{1,0:T(8,128)(2,1)} %collective-permute-done.17.refs_2_, bf16[128,1536]{1,0:T(8,128)(2,1)} %collective-permute-done.11.refs_3_, ...), custom_call_target="tpu_custom_call" | custom-call | flops 3221225472 | bytes 15728640 | tf_op jit(solution)/shard_map/hidden_units/pallas_call | solution.py:262
  133.6 2.8 %copy-done.4 = bf16[1,2048,1536]{2,1,0:T(8,128)(2,1)S(1)} copy-done((bf16[1,2048,1536]{2,1,0:T(8,128)(2,1)S(1)}, bf16[1,2048,1536]{2,1,0:T(8,128)(2,1)}, u32[]{:S(2)}) %copy-start.4) | copy-done | bytes 6291480
  138.8 2.8 %collective-permute-done.21.c_ref = bf16[256,512]{1,0:T(8,128)(2,1)S(1)} collective-permute-done((bf16[256,512]{1,0:T(8,128)(2,1)S(1)}, bf16[256,512]{1,0:T(8,128)(2,1)S(1)}, u32[]{:S(2)}, u32[]{:S(2)}) %collective-permute-start.21) | collective-permute-done | bytes 262176 | tf_op jit(solution)/shard_map/ppermute | solution.py:327
  143.1 2.8 %copy-done.5 = bf16[1,2048,1536]{2,1,0:T(8,128)(2,1)S(1)} copy-done((bf16[1,2048,1536]{2,1,0:T(8,128)(2,1)S(1)}, bf16[1,2048,1536]{2,1,0:T(8,128)(2,1)}, u32[]{:S(2)}) %copy-start.5) | copy-done | bytes 6291480
  145.9 3.5 %block_outputs.3 = bf16[16,2,16,1536]{3,2,1,0:T(8,128)(2,1)} custom-call(s32[2]{0:T(128)S(1)} %pad_add_fusion.info_ref, bf16[256,512]{1,0:T(8,128)(2,1)S(1)} %hidden_units.3.a_ref, bf16[256,512]{1,0:T(8,128)(2,1)S(1)} %collective-permute-done.20.b_ref, bf16[256,512]{1,0:T(8,128)(2,1)S(1)} %collective-permute-done.21.c_ref, ...), custom_call_target="tpu_custom_call" | custom-call | flops 1610612736 | bytes 12582912 | tf_op jit(solution)/shard_map/block_outputs/pallas_call | solution.py:308
  149.5 4.1 %all-to-all-start.3 = ((bf16[32,16,1536]{2,1,0:T(8,128)(2,1)}), bf16[32,16,1536]{2,1,0:T(8,128)(2,1)S(1)}, u32[]{:S(2)}, u32[]{:S(2)}) async-start(bf16[32,16,1536]{2,1,0:T(8,128)(2,1)} %bitcast.24), calls=%async_computation.3 | async-start | bytes 3145728 | tf_op jit(solution)/shard_map/all_to_all | solution.py:484
  157.3 17.2 %collective-permute-done.7 = f32[32,128]{1,0:T(8,128)S(1)} collective-permute-done((f32[32,128]{1,0:T(8,128)S(1)}, f32[32,128]{1,0:T(8,128)S(1)}, u32[]{:S(2)}, u32[]{:S(2)}) %collective-permute-start.7) | collective-permute-done | bytes 16416 | tf_op jit(solution)/shard_map/ppermute | solution.py:327
  (117 shorter events, 35.9 us)
Async XLA Ops:
  2.6 16.8 %collective-permute-start = (bf16[528,512]{1,0:T(8,128)(2,1)S(1)}, bf16[528,512]{1,0:T(8,128)(2,1)S(1)}, u32[]{:S(2)}, u32[]{:S(2)}) collective-permute-start(bf16[528,512]{1,0:T(8,128)(2,1)S(1)} %bitcast.45), channel_id=1, source_target_pairs={{0,32},{32,64},{64,96},{96,0},{1,33},{33,65},{65,97},{97,1},{2,34}... | collective-permute-start | bytes 1622024 | tf_op jit(solution)/shard_map/ppermute | solution.py:331
  5.5 15.2 %collective-permute-start.2 = (bf16[528,512]{1,0:T(8,128)(2,1)S(1)}, bf16[528,512]{1,0:T(8,128)(2,1)S(1)}, u32[]{:S(2)}, u32[]{:S(2)}) collective-permute-start(bf16[528,512]{1,0:T(8,128)(2,1)S(1)} %bitcast.48), channel_id=1, source_target_pairs={{0,96},{32,0},{64,32},{96,64},{1,97},{33,1},{65,33},{97,65},{2,98}... | collective-permute-start | bytes 1622024 | tf_op jit(solution)/shard_map/ppermute | solution.py:331
  8.7 23.9 %all-to-all-start = ((bf16[8,2,16,1536]{3,2,1,0:T(8,128)(2,1)}), bf16[8,2,16,1536]{3,2,1,0:T(8,128)(2,1)S(1)}, u32[]{:S(2)}, u32[]{:S(2)}) async-start(bf16[8,2,16,1536]{3,2,1,0:T(8,128)(2,1)} %broadcast_in_dim.18), calls=%async_computation | async-start | bytes 1572864 | tf_op jit(solution)/shard_map/all_to_all | solution.py:375
  14.1 18.2 %collective-permute-start.4 = (bf16[528,512]{1,0:T(8,128)(2,1)S(1)}, bf16[528,512]{1,0:T(8,128)(2,1)S(1)}, u32[]{:S(2)}, u32[]{:S(2)}) collective-permute-start(bf16[528,512]{1,0:T(8,128)(2,1)S(1)} %bitcast.46), channel_id=1, source_target_pairs={{0,96},{32,0},{64,32},{96,64},{1,97},{33,1},{65,33},{97,65},{2,98}... | collective-permute-start | bytes 1622024 | tf_op jit(solution)/shard_map/ppermute | solution.py:331
  16.1 16.5 %collective-permute-start.5 = (bf16[528,512]{1,0:T(8,128)(2,1)S(1)}, bf16[528,512]{1,0:T(8,128)(2,1)}, u32[]{:S(2)}, u32[]{:S(2)}) collective-permute-start(bf16[528,512]{1,0:T(8,128)(2,1)S(1)} %bitcast.49), channel_id=1, source_target_pairs={{0,32},{32,64},{64,96},{96,0},{1,33},{33,65},{65,97},{97,1},{2,34}... | collective-permute-start | bytes 1622024 | tf_op jit(solution)/shard_map/ppermute | solution.py:331
  16.1 42.2 %collective-permute-start.8 = (bf16[1536]{0:T(1024)(128)(2,1)S(1)}, bf16[1536]{0:T(1024)(128)(2,1)S(1)}, u32[]{:S(2)}, u32[]{:S(2)}) collective-permute-start(bf16[1536]{0:T(1024)(128)(2,1)S(1)} %copy-done.10), channel_id=1, source_target_pairs={{0,1},{1,0},{2,3},{3,2},{4,5},{5,4},{6,7},{7,6},{8,9},{9,8},{10,11... | collective-permute-start | bytes 9224 | tf_op jit(solution)/shard_map/ppermute | solution.py:327
  19.4 25.1 %collective-permute-start.1 = (bf16[528,512]{1,0:T(8,128)(2,1)S(1)}, bf16[528,512]{1,0:T(8,128)(2,1)}, u32[]{:S(2)}, u32[]{:S(2)}) collective-permute-start(bf16[528,512]{1,0:T(8,128)(2,1)S(1)} %collective-permute-done.refs_3_), channel_id=1, source_target_pairs={{0,32},{32,64},{64,96},{96,0},{1,33},{33,65},{65,97},{97,1},{2,34}... | collective-permute-start | bytes 1622024 | tf_op jit(solution)/shard_map/ppermute | solution.py:331
  20.7 23.8 %collective-permute-start.3 = (bf16[528,512]{1,0:T(8,128)(2,1)S(1)}, bf16[528,512]{1,0:T(8,128)(2,1)}, u32[]{:S(2)}, u32[]{:S(2)}) collective-permute-start(bf16[528,512]{1,0:T(8,128)(2,1)S(1)} %collective-permute-done.2.refs_7_), channel_id=1, source_target_pairs={{0,96},{32,0},{64,32},{96,64},{1,97},{33,1},{65,33},{97,65},{2,98}... | collective-permute-start | bytes 1622024 | tf_op jit(solution)/shard_map/ppermute | solution.py:331
  52.3 16.7 %all-to-all-start.1 = ((bf16[8,2,16,1664]{3,2,1,0:T(8,128)(2,1)}), bf16[8,2,16,1664]{3,2,1,0:T(8,128)(2,1)S(1)}, u32[]{:S(2)}, u32[]{:S(2)}) async-start(bf16[8,2,16,1664]{3,2,1,0:T(8,128)(2,1)} %attend.3), calls=%async_computation.1 | async-start | bytes 1703936 | tf_op jit(solution)/shard_map/all_to_all | solution.py:387
  58.4 9.6 %collective-permute-start.9 = (bf16[2,1536]{1,0:T(2,128)(2,1)S(1)}, bf16[2,1536]{1,0:T(2,128)(2,1)S(1)}, u32[]{:S(2)}, u32[]{:S(2)}) collective-permute-start(bf16[2,1536]{1,0:T(2,128)(2,1)S(1)} %broadcast_select_fusion.1), channel_id=1, source_target_pairs={{0,2},{2,0},{1,3},{3,1},{4,6},{6,4},{5,7},{7,5},{8,10},{10,8},{9,1... | collective-permute-start | bytes 18440 | tf_op jit(solution)/shard_map/ppermute | solution.py:327
  87.8 15.7 %collective-permute-start.10 = (bf16[256,1536]{1,0:T(8,128)(2,1)S(1)}, bf16[256,1536]{1,0:T(8,128)(2,1)S(1)}, u32[]{:S(2)}, u32[]{:S(2)}) collective-permute-start(bf16[256,1536]{1,0:T(8,128)(2,1)S(1)} %bitcast.41), channel_id=1, source_target_pairs={{0,4},{4,2},{2,6},{6,0},{1,5},{5,3},{3,7},{7,1},{8,12},{12,10},{10... | collective-permute-start | bytes 2359304 | tf_op jit(solution)/shard_map/ppermute | solution.py:336
  88.9 14.6 %collective-permute-start.12 = (bf16[256,1536]{1,0:T(8,128)(2,1)S(1)}, bf16[256,1536]{1,0:T(8,128)(2,1)S(1)}, u32[]{:S(2)}, u32[]{:S(2)}) collective-permute-start(bf16[256,1536]{1,0:T(8,128)(2,1)S(1)} %bitcast.42), channel_id=1, source_target_pairs={{0,6},{4,0},{2,4},{6,2},{1,7},{5,1},{3,5},{7,3},{8,14},{12,8},{10,... | collective-permute-start | bytes 2359304 | tf_op jit(solution)/shard_map/ppermute | solution.py:336
  103.5 4.4 %collective-permute-start.14 = (bf16[256,1536]{1,0:T(8,128)(2,1)S(1)}, bf16[256,1536]{1,0:T(8,128)(2,1)S(1)}, u32[]{:S(2)}, u32[]{:S(2)}) collective-permute-start(bf16[256,1536]{1,0:T(8,128)(2,1)S(1)} %collective-permute-done.10.refs_1_), channel_id=1, source_target_pairs={{0,1},{1,0},{2,3},{3,2},{4,5},{5,4},{6,7},{7,6},{8,9},{9,8},{10,11... | collective-permute-start | bytes 2359304 | tf_op jit(solution)/shard_map/ppermute | solution.py:327
  103.5 4.4 %collective-permute-start.15 = (bf16[256,1536]{1,0:T(8,128)(2,1)S(1)}, bf16[256,1536]{1,0:T(8,128)(2,1)}, u32[]{:S(2)}, u32[]{:S(2)}) collective-permute-start(bf16[256,1536]{1,0:T(8,128)(2,1)S(1)} %collective-permute-done.12.refs_3_), channel_id=1, source_target_pairs={{0,1},{1,0},{2,3},{3,2},{4,5},{5,4},{6,7},{7,6},{8,9},{9,8},{10,11... | collective-permute-start | bytes 2359304 | tf_op jit(solution)/shard_map/ppermute | solution.py:327
  104.0 16.1 %collective-permute-start.17 = (bf16[256,1536]{1,0:T(8,128)(2,1)S(1)}, bf16[256,1536]{1,0:T(8,128)(2,1)}, u32[]{:S(2)}, u32[]{:S(2)}) collective-permute-start(bf16[256,1536]{1,0:T(8,128)(2,1)S(1)} %bitcast.43), channel_id=1, source_target_pairs={{0,1},{1,0},{2,3},{3,2},{4,5},{5,4},{6,7},{7,6},{8,9},{9,8},{10,11... | collective-permute-start | bytes 2359304 | tf_op jit(solution)/shard_map/ppermute | solution.py:327
  104.4 13.7 %collective-permute-start.11 = (bf16[128,1536]{1,0:T(8,128)(2,1)S(1)}, bf16[128,1536]{1,0:T(8,128)(2,1)}, u32[]{:S(2)}, u32[]{:S(2)}) collective-permute-start(bf16[128,1536]{1,0:T(8,128)(2,1)S(1)} %slice.33), channel_id=1, source_target_pairs={{0,4},{4,2},{2,6},{6,0},{1,5},{5,3},{3,7},{7,1},{8,12},{12,10},{10... | collective-permute-start | bytes 1179656 | tf_op jit(solution)/shard_map/ppermute | solution.py:336
  104.6 13.6 %collective-permute-start.13 = (bf16[128,1536]{1,0:T(8,128)(2,1)S(1)}, bf16[128,1536]{1,0:T(8,128)(2,1)}, u32[]{:S(2)}, u32[]{:S(2)}) collective-permute-start(bf16[128,1536]{1,0:T(8,128)(2,1)S(1)} %slice.34), channel_id=1, source_target_pairs={{0,6},{4,0},{2,4},{6,2},{1,7},{5,1},{3,5},{7,3},{8,14},{12,8},{10,... | collective-permute-start | bytes 1179656 | tf_op jit(solution)/shard_map/ppermute | solution.py:336
  118.2 2.5 %collective-permute-start.19 = (bf16[128,1536]{1,0:T(8,128)(2,1)}, bf16[128,1536]{1,0:T(8,128)(2,1)S(1)}, u32[]{:S(2)}, u32[]{:S(2)}) collective-permute-start(bf16[128,1536]{1,0:T(8,128)(2,1)} %collective-permute-done.13.refs_4_), channel_id=1, source_target_pairs={{0,1},{1,0},{2,3},{3,2},{4,5},{5,4},{6,7},{7,6},{8,9},{9,8},{10,11... | collective-permute-start | bytes 1179656 | tf_op jit(solution)/shard_map/ppermute | solution.py:327
  118.8 12.5 %collective-permute-start.16 = (bf16[256,512]{1,0:T(8,128)(2,1)S(1)}, bf16[256,512]{1,0:T(8,128)(2,1)S(1)}, u32[]{:S(2)}, u32[]{:S(2)}) collective-permute-start(bf16[256,512]{1,0:T(8,128)(2,1)S(1)} %hidden_units.2.a_ref), channel_id=1, source_target_pairs={{0,2},{2,0},{1,3},{3,1},{4,6},{6,4},{5,7},{7,5},{8,10},{10,8},{9,1... | collective-permute-start | bytes 786440 | tf_op jit(solution)/shard_map/ppermute | solution.py:327
  120.1 13.5 %collective-permute-start.22 = (bf16[256,512]{1,0:T(8,128)(2,1)S(1)}, bf16[256,512]{1,0:T(8,128)(2,1)S(1)}, u32[]{:S(2)}, u32[]{:S(2)}) collective-permute-start(bf16[256,512]{1,0:T(8,128)(2,1)S(1)} %hidden_units.2.a_ref), channel_id=1, source_target_pairs={{0,1},{1,0},{2,3},{3,2},{4,5},{5,4},{6,7},{7,6},{8,9},{9,8},{10,11... | collective-permute-start | bytes 786440 | tf_op jit(solution)/shard_map/ppermute | solution.py:327
  131.5 10.1 %collective-permute-start.21 = (bf16[256,512]{1,0:T(8,128)(2,1)S(1)}, bf16[256,512]{1,0:T(8,128)(2,1)S(1)}, u32[]{:S(2)}, u32[]{:S(2)}) collective-permute-start(bf16[256,512]{1,0:T(8,128)(2,1)S(1)} %hidden_units.3.a_ref), channel_id=1, source_target_pairs={{0,2},{2,0},{1,3},{3,1},{4,6},{6,4},{5,7},{7,5},{8,10},{10,8},{9,1... | collective-permute-start | bytes 786440 | tf_op jit(solution)/shard_map/ppermute | solution.py:327
  133.6 8.0 %collective-permute-start.20 = (bf16[256,512]{1,0:T(8,128)(2,1)S(1)}, bf16[256,512]{1,0:T(8,128)(2,1)S(1)}, u32[]{:S(2)}, u32[]{:S(2)}) collective-permute-start(bf16[256,512]{1,0:T(8,128)(2,1)S(1)} %hidden_units.3.a_ref), channel_id=1, source_target_pairs={{0,1},{1,0},{2,3},{3,2},{4,5},{5,4},{6,7},{7,6},{8,9},{9,8},{10,11... | collective-permute-start | bytes 786440 | tf_op jit(solution)/shard_map/ppermute | solution.py:327
  149.5 28.3 %all-to-all-start.3 = ((bf16[32,16,1536]{2,1,0:T(8,128)(2,1)}), bf16[32,16,1536]{2,1,0:T(8,128)(2,1)S(1)}, u32[]{:S(2)}, u32[]{:S(2)}) async-start(bf16[32,16,1536]{2,1,0:T(8,128)(2,1)} %bitcast.24), calls=%async_computation.3 | async-start | bytes 3145728 | tf_op jit(solution)/shard_map/all_to_all | solution.py:484
  154.9 19.6 %collective-permute-start.7 = (f32[32,128]{1,0:T(8,128)S(1)}, f32[32,128]{1,0:T(8,128)S(1)}, u32[]{:S(2)}, u32[]{:S(2)}) collective-permute-start(f32[32,128]{1,0:T(8,128)S(1)} %add.102), channel_id=1, source_target_pairs={{0,2},{2,0},{1,3},{3,1},{4,6},{6,4},{5,7},{7,5},{8,10},{10,8},{9,1... | collective-permute-start | bytes 49160 | tf_op jit(solution)/shard_map/ppermute | solution.py:327
  (19 other events, 140.3 us)

commit v4 on v3

--- a/solution.py
+++ b/solution.py
@@ -218,6 +218,26 @@
     )(got, placing, gain)
 
 
+def halves_kernel(below_ref, above_ref, low_ref, high_ref):
+    middle = low_ref.shape[0]
+    low_ref[...] = below_ref[:middle]
+    high_ref[...] = above_ref[middle:]
+
+
+def halves(below, above):
+    rows, width = below.shape
+    half = jax.ShapeDtypeStruct((rows // 2, width), BF16)
+    return pl.pallas_call(
+        halves_kernel,
+        in_specs=[pl.BlockSpec(memory_space=pltpu.VMEM)] * 2,
+        out_specs=[pl.BlockSpec(memory_space=pltpu.VMEM)] * 2,
+        out_shape=[half, half],
+        compiler_params=pltpu.CompilerParams(vmem_limit_bytes=SMALL_LIMIT),
+        cost_estimate=cost(0, [below, above]),
+        name="halves",
+    )(below, above)
+
+
 def hidden_kernel(info_ref, *refs, parts):
     rows_refs = refs[: sum(parts)]
     gate_ref, up_ref, scale_ref, out_ref = refs[sum(parts) :]
@@ -412,21 +432,6 @@
     attended, square, outgoing = merge(
         got, placing.astype(BF16), gain.reshape(1, q_width), columns
     )
-    outgoing, scales = lax.optimization_barrier((outgoing, scales))
-    own_block = lax.all_to_all(
-        outgoing, ("z", "y"), split_axis=0, concat_axis=0, tiled=True
-    ).reshape(columns * CAP, q_width)
-    w_gate, w_up, w_down = gate_proj[0], up_proj[0], down_proj[0]
-
-    middle = own_block.shape[0] // 2
-    from_below = shift_x(own_block, 1)
-    from_above = shift_x(own_block, -1)
-    far_low = shift_x(from_below[:middle], 1)
-    far_high = shift_x(from_above[middle:], -1)
-    own_other = swap(own_block, "c")
-    below_other = swap(from_below, "c")
-    above_other = swap(from_above, "c")
-
     below = ((x_hi * 2 + x_lo + 3) % 4) // 2
     above = ((x_hi * 2 + x_lo + 1) % 4) // 2
     first_info = jnp.stack(
@@ -441,6 +446,31 @@
         ]
     ).astype(jnp.int32)
     place = jnp.stack([x_hi * 2 + core, x_lo]).astype(jnp.int32)
+    rows_back = 2 * columns * CAP
+    weighting = jnp.broadcast_to(weighting, (EXPERTS, 2 * group, CAP, token_rows)).reshape(
+        rows_back, token_rows
+    )
+    high_part = weighting.astype(BF16)
+    rest = weighting - high_part.astype(F32)
+    middle_part = rest.astype(BF16)
+    low_part = (rest - middle_part.astype(F32)).astype(BF16)
+    table = jnp.concatenate([high_part, middle_part, low_part], axis=1)
+    outgoing, scales, first_info, second_info, place, table = lax.optimization_barrier(
+        (outgoing, scales, first_info, second_info, place, table)
+    )
+    own_block = lax.all_to_all(
+        outgoing, ("z", "y"), split_axis=0, concat_axis=0, tiled=True
+    ).reshape(columns * CAP, q_width)
+    w_gate, w_up, w_down = gate_proj[0], up_proj[0], down_proj[0]
+
+    from_below = shift_x(own_block, 1)
+    from_above = shift_x(own_block, -1)
+    low_half, high_half = halves(from_below, from_above)
+    far_low, far_high = shift_x(low_half, 1), shift_x(high_half, -1)
+    own_other = swap(own_block, "c")
+    below_other = swap(from_below, "c")
+    above_other = swap(from_above, "c")
+
     hidden_first = hidden_units(
         first_info,
         ((from_below,), (below_other,), (from_above,), (above_other,)),
@@ -448,8 +478,8 @@
         w_up,
         scales,
     )
+    first_far, first_other = swap(hidden_first, "xh"), swap(hidden_first, "c")
     far_low, far_high, hidden_first = lax.optimization_barrier((far_low, far_high, hidden_first))
-    first_far, first_other = swap(hidden_first, "xh"), swap(hidden_first, "c")
     hidden_second = hidden_units(
         second_info,
         (
@@ -462,8 +492,8 @@
         w_up,
         scales,
     )
-    first_far, hidden_second = lax.optimization_barrier((first_far, hidden_second))
     second_far, second_other = swap(hidden_second, "xh"), swap(hidden_second, "c")
+    first_far, second_other = lax.optimization_barrier((first_far, second_other))
     produced_first = block_outputs(
         place, (hidden_first, first_other, first_far, swap(first_far, "c")), w_down
     )
@@ -475,12 +505,12 @@
         produced_first,
     )
 
+    square, produced = lax.optimization_barrier((square, produced))
     square = square + swap(square, "c")
     square = square + swap(square, "xh")
     inverse = lax.rsqrt(square[:, :1] / (4 * q_width) + EPS).reshape(sequences, new_dev, 1)
     normed = jnp.transpose(attended * inverse * gain, (1, 0, 2))
 
-    rows_back = 2 * columns * CAP
     returned = lax.all_to_all(
         produced.reshape(2 * columns, CAP, q_width),
         ("z", "y", "xl"),
@@ -488,14 +518,6 @@
         concat_axis=0,
         tiled=True,
     )
-    weighting = jnp.broadcast_to(weighting, (EXPERTS, 2 * group, CAP, token_rows)).reshape(
-        rows_back, token_rows
-    )
-    high_part = weighting.astype(BF16)
-    rest = weighting - high_part.astype(F32)
-    middle_part = rest.astype(BF16)
-    low_part = (rest - middle_part.astype(F32)).astype(BF16)
-    table = jnp.concatenate([high_part, middle_part, low_part], axis=1)
     mixed = lax.dot_general(
         table,
         returned.reshape(rows_back, q_width),

time: 180 us -> 174 us (0.967)
  local copies, waits for them, and re-layouts: 20.8 us -> 10.5 us
  waiting for transfers between devices: 57.4 us -> 65.9 us
  Pallas kernels: 36 us -> 33.8 us
    unnamed x34 -> x32, local copies, waits for them, and re-layouts: 17.9 us -> 7.63 us
    ppermute x15, waiting for transfers between devices: 29.5 us -> 37.6 us  [swap(): return lax.ppermute(array, axis, [(0, 1), (1, 0)])]
    all_to_all x1, blocking collectives: 17.9 us -> 16.1 us  [on_device(): lax.all_to_all(outgoing, ('z', 'y'), split_axis=0, concat_axis=0, tiled=T...]
  transfers between devices with their start and end apart: 28 -> 28, of which waited for: 13 -> 11; matrix products, arithmetic and copies ran while one was open for 3% -> 3% of each run, Pallas kernels for 18% -> 17%
where the time goes in v4:
time: 174 us
  waiting for transfers between devices  65.9 us (38%)
  starting transfers between devices  42.5 us (24%)
  Pallas kernels  33.8 us (19%)
  blocking collectives  16.1 us (9%)
  local copies, waits for them, and re-layouts  10.5 us (6%)
  other arithmetic  3.4 us (2%)
    ppermute x15, waiting for transfers between devices, swap(): return lax.ppermute(array, axis, [(0, 1), (1, 0)])  37.6 us
    pallas_call x2, Pallas kernels, attend(): pl.pallas_call(lambda *refs: attention_kernel(*refs, parts=parts, last=be...  18.9 us
    all_to_all x1, blocking collectives, on_device(): lax.all_to_all(outgoing, ('z', 'y'), split_axis=0, concat_axis=0, tiled=T...  16.1 us
    ppermute x4, waiting for transfers between devices, shift_x(): lax.ppermute(array, ('xl', 'xh'), [(index[x], index[(x + by) % 4]) for x...  12.6 us
    ppermute x6, waiting for transfers between devices, shift(): lax.ppermute(array, axis, [(i, (i + by) % size) for i in range(size)])  12.4 us
    ppermute x15, starting transfers between devices, swap(): return lax.ppermute(array, axis, [(0, 1), (1, 0)])  11 us
    ppermute x6, starting transfers between devices, shift(): lax.ppermute(array, axis, [(i, (i + by) % size) for i in range(size)])  9.89 us
    pallas_call x2, Pallas kernels, hidden_units(): pl.pallas_call(lambda *refs: hidden_kernel(*refs, parts=parts), in_specs=...  8.16 us
  transfers between devices with their start and end apart: 28, of which 11 were waited for; matrix products, arithmetic and copies ran while one was open for 3% of the time, Pallas kernels for 17%

profile of v4, /device:TPU:0, one launch (start us, length us, event | category | flops | bytes accessed | tf_op | source)
XLA Modules:
  0.0 173.7 jit_solution(12976946999795568359)
XLA Ops:
  10.8 5.5 %all-to-all-start = ((bf16[8,2,16,1536]{3,2,1,0:T(8,128)(2,1)}), bf16[8,2,16,1536]{3,2,1,0:T(8,128)(2,1)S(1)}, u32[]{:S(2)}, u32[]{:S(2)}) async-start(bf16[8,2,16,1536]{3,2,1,0:T(8,128)(2,1)} %broadcast_in_dim.18), calls=%async_computation | async-start | bytes 1572864 | tf_op jit(solution)/shard_map/all_to_all | solution.py:395
  19.9 10.3 %collective-permute-done.2.refs_7_ = bf16[528,512]{1,0:T(8,128)(2,1)S(1)} collective-permute-done((bf16[528,512]{1,0:T(8,128)(2,1)S(1)}, bf16[528,512]{1,0:T(8,128)(2,1)S(1)}, u32[]{:S(2)}, u32[]{:S(2)}) %collective-permute-start.2) | collective-permute-done | bytes 540704 | tf_op jit(solution)/shard_map/ppermute | solution.py:351
  30.1 3.5 %collective-permute-start.3 = (bf16[528,512]{1,0:T(8,128)(2,1)S(1)}, bf16[528,512]{1,0:T(8,128)(2,1)}, u32[]{:S(2)}, u32[]{:S(2)}) collective-permute-start(bf16[528,512]{1,0:T(8,128)(2,1)S(1)} %collective-permute-done.2.refs_7_), channel_id=1, source_target_pairs={{0,96},{32,0},{64,32},{96,64},{1,97},{33,1},{65,33},{97,65},{2,98}... | collective-permute-start | bytes 1622024 | tf_op jit(solution)/shard_map/ppermute | solution.py:351
  33.9 11.8 %attend.2 = (f32[2,2,768,128]{3,2,1,0:T(8,128)S(1)}, f32[2,2,768,128]{3,2,1,0:T(8,128)S(1)}) custom-call(s32[8]{0:T(128)S(1)} %stack.101.refs_0_, bf16[8,2,16,1536]{3,2,1,0:T(8,128)(2,1)S(1)} %all-to-all-done.refs_1_, bf16[528,512]{1,0:T(8,128)(2,1)S(1)} %bitcast.52, bf16[528,512]{1,0:T(8,128)(2,1)S(1)} %collective-permute-done.refs_3_, ...), custom_call_target="tpu_custom_call" | custom-call | flops 5234491392 | bytes 4030464 | tf_op jit(solution)/shard_map/attend/pallas_call | solution.py:154
  45.8 7.1 %attend.3 = bf16[8,2,16,1664]{3,2,1,0:T(8,128)(2,1)S(1)} custom-call(s32[6]{0:T(128)S(1)} %stack.98.refs_0_, bf16[8,2,16,1536]{3,2,1,0:T(8,128)(2,1)S(1)} %all-to-all-done.refs_1_, bf16[528,512]{1,0:T(8,128)(2,1)} %collective-permute-done.1.refs_2_, bf16[528,512]{1,0:T(8,128)(2,1)} %collective-permute-done.3.refs_3_, ...), custom_call_target="tpu_custom_call" | custom-call | flops 2013265920 | bytes 5013504 | tf_op jit(solution)/shard_map/attend/pallas_call | solution.py:154
  53.8 5.5 %all-to-all-start.1 = ((bf16[8,2,16,1664]{3,2,1,0:T(8,128)(2,1)}), bf16[8,2,16,1664]{3,2,1,0:T(8,128)(2,1)S(1)}, u32[]{:S(2)}, u32[]{:S(2)}) async-start(bf16[8,2,16,1664]{3,2,1,0:T(8,128)(2,1)} %copy-done.2), calls=%async_computation.1 | async-start | bytes 1703936 | tf_op jit(solution)/shard_map/all_to_all | solution.py:407
  59.6 2.8 %collective-permute-start.7 = (bf16[2,1536]{1,0:T(2,128)(2,1)S(1)}, bf16[2,1536]{1,0:T(2,128)(2,1)S(1)}, u32[]{:S(2)}, u32[]{:S(2)}) collective-permute-start(bf16[2,1536]{1,0:T(2,128)(2,1)S(1)} %broadcast_select_fusion.1), channel_id=1, source_target_pairs={{0,2},{2,0},{1,3},{3,1},{4,6},{6,4},{5,7},{7,5},{8,10},{10,8},{9,1... | collective-permute-start | bytes 18440 | tf_op jit(solution)/shard_map/ppermute | solution.py:347
  62.5 8.3 %collective-permute-done.7 = bf16[2,1536]{1,0:T(2,128)(2,1)S(1)} collective-permute-done((bf16[2,1536]{1,0:T(2,128)(2,1)S(1)}, bf16[2,1536]{1,0:T(2,128)(2,1)S(1)}, u32[]{:S(2)}, u32[]{:S(2)}) %collective-permute-start.7) | collective-permute-done | bytes 6176 | tf_op jit(solution)/shard_map/ppermute | solution.py:347
  72.8 16.1 %all_to_all.20 = bf16[16,16,1536]{2,1,0:T(8,128)(2,1)S(1)} all-to-all(bf16[16,16,1536]{2,1,0:T(8,128)(2,1)S(1)} %get-tuple-element.31), channel_id=1, replica_groups=mesh['z'=4,'y'=4,'xl'=2,'xh'=2,'c'=2] {'z','y'}, dimensions={0} | all-to-all | bytes 1572864 | tf_op jit(solution)/shard_map/all_to_all | solution.py:461
  89.9 2.2 %collective-permute-start.10 = (bf16[256,1536]{1,0:T(8,128)(2,1)S(1)}, bf16[256,1536]{1,0:T(8,128)(2,1)S(1)}, u32[]{:S(2)}, u32[]{:S(2)}) collective-permute-start(bf16[256,1536]{1,0:T(8,128)(2,1)S(1)} %bitcast.47), channel_id=1, source_target_pairs={{0,6},{4,0},{2,4},{6,2},{1,7},{5,1},{3,5},{7,3},{8,14},{12,8},{10,... | collective-permute-start | bytes 2359304 | tf_op jit(solution)/shard_map/ppermute | solution.py:356
  92.1 12.6 %collective-permute-done.9.below_ref.refs_1_ = bf16[256,1536]{1,0:T(8,128)(2,1)S(1)} collective-permute-done((bf16[256,1536]{1,0:T(8,128)(2,1)S(1)}, bf16[256,1536]{1,0:T(8,128)(2,1)S(1)}, u32[]{:S(2)}, u32[]{:S(2)}) %collective-permute-start.9) | collective-permute-done | bytes 786464 | tf_op jit(solution)/shard_map/ppermute | solution.py:356
  105.6 2.9 %collective-permute-start.12 = (bf16[128,1536]{1,0:T(8,128)(2,1)S(1)}, bf16[128,1536]{1,0:T(8,128)(2,1)S(1)}, u32[]{:S(2)}, u32[]{:S(2)}) collective-permute-start(bf16[128,1536]{1,0:T(8,128)(2,1)S(1)} %get-tuple-element.33), channel_id=1, source_target_pairs={{0,6},{4,0},{2,4},{6,2},{1,7},{5,1},{3,5},{7,3},{8,14},{12,8},{10,... | collective-permute-start | bytes 1179656 | tf_op jit(solution)/shard_map/ppermute | solution.py:356
  108.6 2.8 %copy-done = bf16[1,6144,512]{2,1,0:T(8,128)(2,1)S(1)} copy-done((bf16[1,6144,512]{2,1,0:T(8,128)(2,1)S(1)}, bf16[1,6144,512]{2,1,0:T(8,128)(2,1)}, u32[]{:S(2)}) %copy-start) | copy-done | bytes 6291480
  111.4 2.8 %copy-done.1 = bf16[1,6144,512]{2,1,0:T(8,128)(2,1)S(1)} copy-done((bf16[1,6144,512]{2,1,0:T(8,128)(2,1)S(1)}, bf16[1,6144,512]{2,1,0:T(8,128)(2,1)}, u32[]{:S(2)}) %copy-start.1) | copy-done | bytes 6291480
  114.2 4.0 %hidden_units.2.a_ref = bf16[256,512]{1,0:T(8,128)(2,1)S(1)} custom-call(s32[4]{0:T(128)S(1)} %get-tuple-element.34.refs_0_, bf16[256,1536]{1,0:T(8,128)(2,1)S(1)} %collective-permute-done.9.below_ref.refs_1_, bf16[256,1536]{1,0:T(8,128)(2,1)S(1)} %collective-permute-done.13.refs_2_, bf16[256,1536]{1,0:T(8,128)(2,1)S(1)} %collective-permute-done.10.above_ref.refs_3_, ...), custom_call_target="tpu_custom_call" | custom-call | flops 3221225472 | bytes 15728640 | tf_op jit(solution)/shard_map/hidden_units/pallas_call | solution.py:282
  121.0 4.2 %hidden_units.3.a_ref = bf16[256,512]{1,0:T(8,128)(2,1)S(1)} custom-call(s32[4]{0:T(128)S(1)} %get-tuple-element.30.refs_0_, bf16[256,1536]{1,0:T(8,128)(2,1)S(1)} %bitcast.49, bf16[256,1536]{1,0:T(8,128)(2,1)S(1)} %collective-permute-done.8.refs_2_, bf16[128,1536]{1,0:T(8,128)(2,1)S(1)} %collective-permute-done.11.refs_3_, ...), custom_call_target="tpu_custom_call" | custom-call | flops 3221225472 | bytes 15728640 | tf_op jit(solution)/shard_map/hidden_units/pallas_call | solution.py:282
  125.8 3.2 %collective-permute-done.17.c_ref = bf16[256,512]{1,0:T(8,128)(2,1)S(1)} collective-permute-done((bf16[256,512]{1,0:T(8,128)(2,1)S(1)}, bf16[256,512]{1,0:T(8,128)(2,1)S(1)}, u32[]{:S(2)}, u32[]{:S(2)}) %collective-permute-start.17) | collective-permute-done | bytes 262176 | tf_op jit(solution)/shard_map/ppermute | solution.py:347
  130.8 2.3 %block_outputs.2.refs_0_ = bf16[256,1536]{1,0:T(8,128)(2,1)S(1)} custom-call(s32[2]{0:T(128)S(1)} %pad_add_fusion.2.info_ref, bf16[256,512]{1,0:T(8,128)(2,1)S(1)} %hidden_units.2.a_ref, bf16[256,512]{1,0:T(8,128)(2,1)S(1)} %collective-permute-done.20.b_ref, bf16[256,512]{1,0:T(8,128)(2,1)S(1)} %collective-permute-done.17.c_ref, ...), custom_call_target="tpu_custom_call" | custom-call | flops 1610612736 | bytes 12582912 | tf_op jit(solution)/shard_map/block_outputs/pallas_call | solution.py:328
  133.1 6.2 %collective-permute-done.19.c_ref = bf16[256,512]{1,0:T(8,128)(2,1)S(1)} collective-permute-done((bf16[256,512]{1,0:T(8,128)(2,1)S(1)}, bf16[256,512]{1,0:T(8,128)(2,1)S(1)}, u32[]{:S(2)}, u32[]{:S(2)}) %collective-permute-start.19) | collective-permute-done | bytes 262176 | tf_op jit(solution)/shard_map/ppermute | solution.py:347
  140.8 3.5 %block_outputs.3 = bf16[16,2,16,1536]{3,2,1,0:T(8,128)(2,1)} custom-call(s32[2]{0:T(128)S(1)} %pad_add_fusion.2.info_ref, bf16[256,512]{1,0:T(8,128)(2,1)S(1)} %hidden_units.3.a_ref, bf16[256,512]{1,0:T(8,128)(2,1)S(1)} %collective-permute-done.18.b_ref, bf16[256,512]{1,0:T(8,128)(2,1)S(1)} %collective-permute-done.19.c_ref, ...), custom_call_target="tpu_custom_call" | custom-call | flops 1610612736 | bytes 12582912 | tf_op jit(solution)/shard_map/block_outputs/pallas_call | solution.py:328
  144.3 4.0 %all-to-all-start.3 = ((bf16[32,16,1536]{2,1,0:T(8,128)(2,1)}), bf16[32,16,1536]{2,1,0:T(8,128)(2,1)S(1)}, u32[]{:S(2)}, u32[]{:S(2)}) async-start(bf16[32,16,1536]{2,1,0:T(8,128)(2,1)} %bitcast.24), calls=%async_computation.3 | async-start | bytes 3145728 | tf_op jit(solution)/shard_map/all_to_all | solution.py:514
  149.6 2.3 %collective-permute-start.24 = (f32[32,128]{1,0:T(8,128)S(1)}, f32[32,128]{1,0:T(8,128)S(1)}, u32[]{:S(2)}, u32[]{:S(2)}) collective-permute-start(f32[32,128]{1,0:T(8,128)S(1)} %add.115), channel_id=1, source_target_pairs={{0,2},{2,0},{1,3},{3,1},{4,6},{6,4},{5,7},{7,5},{8,10},{10,8},{9,1... | collective-permute-start | bytes 49160 | tf_op jit(solution)/shard_map/ppermute | solution.py:347
  151.9 17.2 %collective-permute-done.24 = f32[32,128]{1,0:T(8,128)S(1)} collective-permute-done((f32[32,128]{1,0:T(8,128)S(1)}, f32[32,128]{1,0:T(8,128)S(1)}, u32[]{:S(2)}, u32[]{:S(2)}) %collective-permute-start.24) | collective-permute-done | bytes 16416 | tf_op jit(solution)/shard_map/ppermute | solution.py:347
  170.2 2.3 %all-to-all-done.3 = bf16[32,16,1536]{2,1,0:T(8,128)(2,1)S(1)} async-done(((bf16[32,16,1536]{2,1,0:T(8,128)(2,1)}), bf16[32,16,1536]{2,1,0:T(8,128)(2,1)S(1)}, u32[]{:S(2)}, u32[]{:S(2)}) %all-to-all-start.3) | async-done | bytes 1572896 | tf_op jit(solution)/shard_map/all_to_all | solution.py:514
  (116 shorter events, 29.1 us)
Async XLA Ops:
  2.6 17.3 %collective-permute-start = (bf16[528,512]{1,0:T(8,128)(2,1)S(1)}, bf16[528,512]{1,0:T(8,128)(2,1)S(1)}, u32[]{:S(2)}, u32[]{:S(2)}) collective-permute-start(bf16[528,512]{1,0:T(8,128)(2,1)S(1)} %bitcast.50), channel_id=1, source_target_pairs={{0,32},{32,64},{64,96},{96,0},{1,33},{33,65},{65,97},{97,1},{2,34}... | collective-permute-start | bytes 1622024 | tf_op jit(solution)/shard_map/ppermute | solution.py:351
  4.6 29.3 %collective-permute-start.4 = (bf16[528,512]{1,0:T(8,128)(2,1)S(1)}, bf16[528,512]{1,0:T(8,128)(2,1)}, u32[]{:S(2)}, u32[]{:S(2)}) collective-permute-start(bf16[528,512]{1,0:T(8,128)(2,1)S(1)} %bitcast.51), channel_id=1, source_target_pairs={{0,96},{32,0},{64,32},{96,64},{1,97},{33,1},{65,33},{97,65},{2,98}... | collective-permute-start | bytes 1622024 | tf_op jit(solution)/shard_map/ppermute | solution.py:351
  7.7 22.5 %collective-permute-start.2 = (bf16[528,512]{1,0:T(8,128)(2,1)S(1)}, bf16[528,512]{1,0:T(8,128)(2,1)S(1)}, u32[]{:S(2)}, u32[]{:S(2)}) collective-permute-start(bf16[528,512]{1,0:T(8,128)(2,1)S(1)} %bitcast.53), channel_id=1, source_target_pairs={{0,96},{32,0},{64,32},{96,64},{1,97},{33,1},{65,33},{97,65},{2,98}... | collective-permute-start | bytes 1622024 | tf_op jit(solution)/shard_map/ppermute | solution.py:351
  9.7 24.2 %collective-permute-start.5 = (bf16[528,512]{1,0:T(8,128)(2,1)S(1)}, bf16[528,512]{1,0:T(8,128)(2,1)}, u32[]{:S(2)}, u32[]{:S(2)}) collective-permute-start(bf16[528,512]{1,0:T(8,128)(2,1)S(1)} %bitcast.54), channel_id=1, source_target_pairs={{0,32},{32,64},{64,96},{96,0},{1,33},{33,65},{65,97},{97,1},{2,34}... | collective-permute-start | bytes 1622024 | tf_op jit(solution)/shard_map/ppermute | solution.py:351
  10.8 23.1 %all-to-all-start = ((bf16[8,2,16,1536]{3,2,1,0:T(8,128)(2,1)}), bf16[8,2,16,1536]{3,2,1,0:T(8,128)(2,1)S(1)}, u32[]{:S(2)}, u32[]{:S(2)}) async-start(bf16[8,2,16,1536]{3,2,1,0:T(8,128)(2,1)} %broadcast_in_dim.18), calls=%async_computation | async-start | bytes 1572864 | tf_op jit(solution)/shard_map/all_to_all | solution.py:395
  16.3 43.3 %collective-permute-start.6 = (bf16[1536]{0:T(1024)(128)(2,1)S(1)}, bf16[1536]{0:T(1024)(128)(2,1)S(1)}, u32[]{:S(2)}, u32[]{:S(2)}) collective-permute-start(bf16[1536]{0:T(1024)(128)(2,1)S(1)} %copy-done.5), channel_id=1, source_target_pairs={{0,1},{1,0},{2,3},{3,2},{4,5},{5,4},{6,7},{7,6},{8,9},{9,8},{10,11... | collective-permute-start | bytes 9224 | tf_op jit(solution)/shard_map/ppermute | solution.py:347
  19.9 25.9 %collective-permute-start.1 = (bf16[528,512]{1,0:T(8,128)(2,1)S(1)}, bf16[528,512]{1,0:T(8,128)(2,1)}, u32[]{:S(2)}, u32[]{:S(2)}) collective-permute-start(bf16[528,512]{1,0:T(8,128)(2,1)S(1)} %collective-permute-done.refs_3_), channel_id=1, source_target_pairs={{0,32},{32,64},{64,96},{96,0},{1,33},{33,65},{65,97},{97,1},{2,34}... | collective-permute-start | bytes 1622024 | tf_op jit(solution)/shard_map/ppermute | solution.py:351
  30.1 15.6 %collective-permute-start.3 = (bf16[528,512]{1,0:T(8,128)(2,1)S(1)}, bf16[528,512]{1,0:T(8,128)(2,1)}, u32[]{:S(2)}, u32[]{:S(2)}) collective-permute-start(bf16[528,512]{1,0:T(8,128)(2,1)S(1)} %collective-permute-done.2.refs_7_), channel_id=1, source_target_pairs={{0,96},{32,0},{64,32},{96,64},{1,97},{33,1},{65,33},{97,65},{2,98}... | collective-permute-start | bytes 1622024 | tf_op jit(solution)/shard_map/ppermute | solution.py:351
  53.8 18.1 %all-to-all-start.1 = ((bf16[8,2,16,1664]{3,2,1,0:T(8,128)(2,1)}), bf16[8,2,16,1664]{3,2,1,0:T(8,128)(2,1)S(1)}, u32[]{:S(2)}, u32[]{:S(2)}) async-start(bf16[8,2,16,1664]{3,2,1,0:T(8,128)(2,1)} %copy-done.2), calls=%async_computation.1 | async-start | bytes 1703936 | tf_op jit(solution)/shard_map/all_to_all | solution.py:407
  59.6 11.2 %collective-permute-start.7 = (bf16[2,1536]{1,0:T(2,128)(2,1)S(1)}, bf16[2,1536]{1,0:T(2,128)(2,1)S(1)}, u32[]{:S(2)}, u32[]{:S(2)}) collective-permute-start(bf16[2,1536]{1,0:T(2,128)(2,1)S(1)} %broadcast_select_fusion.1), channel_id=1, source_target_pairs={{0,2},{2,0},{1,3},{3,1},{4,6},{6,4},{5,7},{7,5},{8,10},{10,8},{9,1... | collective-permute-start | bytes 18440 | tf_op jit(solution)/shard_map/ppermute | solution.py:347
  88.9 15.8 %collective-permute-start.9 = (bf16[256,1536]{1,0:T(8,128)(2,1)S(1)}, bf16[256,1536]{1,0:T(8,128)(2,1)S(1)}, u32[]{:S(2)}, u32[]{:S(2)}) collective-permute-start(bf16[256,1536]{1,0:T(8,128)(2,1)S(1)} %bitcast.46), channel_id=1, source_target_pairs={{0,4},{4,2},{2,6},{6,0},{1,5},{5,3},{3,7},{7,1},{8,12},{12,10},{10... | collective-permute-start | bytes 2359304 | tf_op jit(solution)/shard_map/ppermute | solution.py:356
  89.9 14.8 %collective-permute-start.10 = (bf16[256,1536]{1,0:T(8,128)(2,1)S(1)}, bf16[256,1536]{1,0:T(8,128)(2,1)S(1)}, u32[]{:S(2)}, u32[]{:S(2)}) collective-permute-start(bf16[256,1536]{1,0:T(8,128)(2,1)S(1)} %bitcast.47), channel_id=1, source_target_pairs={{0,6},{4,0},{2,4},{6,2},{1,7},{5,1},{3,5},{7,3},{8,14},{12,8},{10,... | collective-permute-start | bytes 2359304 | tf_op jit(solution)/shard_map/ppermute | solution.py:356
  104.7 3.9 %collective-permute-start.13 = (bf16[256,1536]{1,0:T(8,128)(2,1)S(1)}, bf16[256,1536]{1,0:T(8,128)(2,1)S(1)}, u32[]{:S(2)}, u32[]{:S(2)}) collective-permute-start(bf16[256,1536]{1,0:T(8,128)(2,1)S(1)} %collective-permute-done.9.below_ref.refs_1_), channel_id=1, source_target_pairs={{0,1},{1,0},{2,3},{3,2},{4,5},{5,4},{6,7},{7,6},{8,9},{9,8},{10,11... | collective-permute-start | bytes 2359304 | tf_op jit(solution)/shard_map/ppermute | solution.py:347
  104.7 3.9 %collective-permute-start.14 = (bf16[256,1536]{1,0:T(8,128)(2,1)S(1)}, bf16[256,1536]{1,0:T(8,128)(2,1)S(1)}, u32[]{:S(2)}, u32[]{:S(2)}) collective-permute-start(bf16[256,1536]{1,0:T(8,128)(2,1)S(1)} %collective-permute-done.10.above_ref.refs_3_), channel_id=1, source_target_pairs={{0,1},{1,0},{2,3},{3,2},{4,5},{5,4},{6,7},{7,6},{8,9},{9,8},{10,11... | collective-permute-start | bytes 2359304 | tf_op jit(solution)/shard_map/ppermute | solution.py:347
  105.3 12.9 %collective-permute-start.11 = (bf16[128,1536]{1,0:T(8,128)(2,1)S(1)}, bf16[128,1536]{1,0:T(8,128)(2,1)S(1)}, u32[]{:S(2)}, u32[]{:S(2)}) collective-permute-start(bf16[128,1536]{1,0:T(8,128)(2,1)S(1)} %get-tuple-element.32), channel_id=1, source_target_pairs={{0,4},{4,2},{2,6},{6,0},{1,5},{5,3},{3,7},{7,1},{8,12},{12,10},{10... | collective-permute-start | bytes 1179656 | tf_op jit(solution)/shard_map/ppermute | solution.py:356
  105.6 12.6 %collective-permute-start.12 = (bf16[128,1536]{1,0:T(8,128)(2,1)S(1)}, bf16[128,1536]{1,0:T(8,128)(2,1)S(1)}, u32[]{:S(2)}, u32[]{:S(2)}) collective-permute-start(bf16[128,1536]{1,0:T(8,128)(2,1)S(1)} %get-tuple-element.33), channel_id=1, source_target_pairs={{0,6},{4,0},{2,4},{6,2},{1,7},{5,1},{3,5},{7,3},{8,14},{12,8},{10,... | collective-permute-start | bytes 1179656 | tf_op jit(solution)/shard_map/ppermute | solution.py:356
  108.6 12.4 %collective-permute-start.8 = (bf16[256,1536]{1,0:T(8,128)(2,1)S(1)}, bf16[256,1536]{1,0:T(8,128)(2,1)S(1)}, u32[]{:S(2)}, u32[]{:S(2)}) collective-permute-start(bf16[256,1536]{1,0:T(8,128)(2,1)S(1)} %bitcast.48), channel_id=1, source_target_pairs={{0,1},{1,0},{2,3},{3,2},{4,5},{5,4},{6,7},{7,6},{8,9},{9,8},{10,11... | collective-permute-start | bytes 2359304 | tf_op jit(solution)/shard_map/ppermute | solution.py:347
  118.2 2.8 %collective-permute-start.15 = (bf16[128,1536]{1,0:T(8,128)(2,1)S(1)}, bf16[128,1536]{1,0:T(8,128)(2,1)S(1)}, u32[]{:S(2)}, u32[]{:S(2)}) collective-permute-start(bf16[128,1536]{1,0:T(8,128)(2,1)S(1)} %collective-permute-done.11.refs_3_), channel_id=1, source_target_pairs={{0,1},{1,0},{2,3},{3,2},{4,5},{5,4},{6,7},{7,6},{8,9},{9,8},{10,11... | collective-permute-start | bytes 1179656 | tf_op jit(solution)/shard_map/ppermute | solution.py:347
  118.9 10.1 %collective-permute-start.17 = (bf16[256,512]{1,0:T(8,128)(2,1)S(1)}, bf16[256,512]{1,0:T(8,128)(2,1)S(1)}, u32[]{:S(2)}, u32[]{:S(2)}) collective-permute-start(bf16[256,512]{1,0:T(8,128)(2,1)S(1)} %hidden_units.2.a_ref), channel_id=1, source_target_pairs={{0,2},{2,0},{1,3},{3,1},{4,6},{6,4},{5,7},{7,5},{8,10},{10,8},{9,1... | collective-permute-start | bytes 786440 | tf_op jit(solution)/shard_map/ppermute | solution.py:347
  125.2 3.8 %collective-permute-start.18 = (bf16[256,512]{1,0:T(8,128)(2,1)S(1)}, bf16[256,512]{1,0:T(8,128)(2,1)S(1)}, u32[]{:S(2)}, u32[]{:S(2)}) collective-permute-start(bf16[256,512]{1,0:T(8,128)(2,1)S(1)} %hidden_units.3.a_ref), channel_id=1, source_target_pairs={{0,1},{1,0},{2,3},{3,2},{4,5},{5,4},{6,7},{7,6},{8,9},{9,8},{10,11... | collective-permute-start | bytes 786440 | tf_op jit(solution)/shard_map/ppermute | solution.py:347
  125.3 5.4 %collective-permute-start.20 = (bf16[256,512]{1,0:T(8,128)(2,1)S(1)}, bf16[256,512]{1,0:T(8,128)(2,1)S(1)}, u32[]{:S(2)}, u32[]{:S(2)}) collective-permute-start(bf16[256,512]{1,0:T(8,128)(2,1)S(1)} %hidden_units.2.a_ref), channel_id=1, source_target_pairs={{0,1},{1,0},{2,3},{3,2},{4,5},{5,4},{6,7},{7,6},{8,9},{9,8},{10,11... | collective-permute-start | bytes 786440 | tf_op jit(solution)/shard_map/ppermute | solution.py:347
  129.0 10.2 %collective-permute-start.19 = (bf16[256,512]{1,0:T(8,128)(2,1)S(1)}, bf16[256,512]{1,0:T(8,128)(2,1)S(1)}, u32[]{:S(2)}, u32[]{:S(2)}) collective-permute-start(bf16[256,512]{1,0:T(8,128)(2,1)S(1)} %hidden_units.3.a_ref), channel_id=1, source_target_pairs={{0,2},{2,0},{1,3},{3,1},{4,6},{6,4},{5,7},{7,5},{8,10},{10,8},{9,1... | collective-permute-start | bytes 786440 | tf_op jit(solution)/shard_map/ppermute | solution.py:347
  144.3 28.2 %all-to-all-start.3 = ((bf16[32,16,1536]{2,1,0:T(8,128)(2,1)}), bf16[32,16,1536]{2,1,0:T(8,128)(2,1)S(1)}, u32[]{:S(2)}, u32[]{:S(2)}) async-start(bf16[32,16,1536]{2,1,0:T(8,128)(2,1)} %bitcast.24), calls=%async_computation.3 | async-start | bytes 3145728 | tf_op jit(solution)/shard_map/all_to_all | solution.py:514
  149.6 19.5 %collective-permute-start.24 = (f32[32,128]{1,0:T(8,128)S(1)}, f32[32,128]{1,0:T(8,128)S(1)}, u32[]{:S(2)}, u32[]{:S(2)}) collective-permute-start(f32[32,128]{1,0:T(8,128)S(1)} %add.115), channel_id=1, source_target_pairs={{0,2},{2,0},{1,3},{3,1},{4,6},{6,4},{5,7},{7,5},{8,10},{10,8},{9,1... | collective-permute-start | bytes 49160 | tf_op jit(solution)/shard_map/ppermute | solution.py:347
  (18 other events, 186.1 us)

commit v5 on v4

--- a/solution.py
+++ b/solution.py
@@ -16,7 +16,7 @@
 DEAD = -1e30
 LANES = 128
 VMEM_LIMIT = 20 * 1024 * 1024
-SMALL_LIMIT = 10 * 1024 * 1024
+SMALL_LIMIT = 6 * 1024 * 1024
 
 BF16 = jnp.bfloat16
 F32 = jnp.float32
@@ -290,48 +290,43 @@
     )(info, *rows, w_gate, w_up, scale)
 
 
-def down_kernel(info_ref, a_ref, b_ref, c_ref, d_ref, down_ref, *refs):
-    mine = info_ref[0]
-    units = a_ref.shape[1]
+def down_kernel(info_ref, *refs):
+    first_refs, second_refs, down_ref, out_ref = refs[:4], refs[4:8], refs[8], refs[9]
+    units = first_refs[0].shape[1]
+    sources, _, count, columns = out_ref.shape
+    middle = sources * count
     tile = 512
-    for lane in range(0, down_ref.shape[1], tile):
+    pieces = []
+    for index, (first_ref, second_ref) in enumerate(zip(first_refs, second_refs)):
+        start = pl.multiple_of((info_ref[0] ^ index) * units, units)
+        pieces.append((start, jnp.concatenate([first_ref[...], second_ref[...]], axis=0)))
+    here, there = pl.ds(info_ref[1], 1), pl.ds(1 - info_ref[1], 1)
+    for lane in range(0, columns, tile):
         total = None
-        for index, rows_ref in enumerate((a_ref, b_ref, c_ref, d_ref)):
-            start = pl.multiple_of((mine ^ index) * units, units)
+        for start, rows in pieces:
             term = jnp.dot(
-                rows_ref[...],
+                rows,
                 down_ref[pl.ds(start, units), lane : lane + tile],
                 preferred_element_type=F32,
             )
             total = term if total is None else total + term
         result = total.astype(BF16)
-        if len(refs) == 1:
-            refs[0][:, lane : lane + tile] = result
-            continue
-        before_ref, out_ref = refs
-        sources, _, count, _ = out_ref.shape
-        here, there = pl.ds(info_ref[1], 1), pl.ds(1 - info_ref[1], 1)
-        out_ref[:, here, :, lane : lane + tile] = result.reshape(sources, 1, count, tile)
-        out_ref[:, there, :, lane : lane + tile] = before_ref[:, lane : lane + tile].reshape(
-            sources, 1, count, tile
-        )
-
-
-def block_outputs(info, hiddens, w_down, before=None):
-    tokens = hiddens[0].shape[0]
+        shape = (sources, 1, count, tile)
+        out_ref[:, there, :, lane : lane + tile] = result[:middle].reshape(shape)
+        out_ref[:, here, :, lane : lane + tile] = result[middle:].reshape(shape)
+
+
+def block_outputs(info, first, second, w_down):
+    tokens = first[0].shape[0]
     columns = w_down.shape[1]
-    args = [*hiddens, w_down]
-    out_shape = (tokens, columns)
-    if before is not None:
-        args.append(before)
-        out_shape = (tokens // CAP, 2, CAP, columns)
+    args = [*first, *second, w_down]
     return pl.pallas_call(
         down_kernel,
         in_specs=[pl.BlockSpec(memory_space=pltpu.SMEM)]
         + [pl.BlockSpec(memory_space=pltpu.VMEM)] * len(args),
-        out_shape=jax.ShapeDtypeStruct(out_shape, BF16),
+        out_shape=jax.ShapeDtypeStruct((tokens // CAP, 2, CAP, columns), BF16),
         compiler_params=pltpu.CompilerParams(vmem_limit_bytes=SMALL_LIMIT),
-        cost_estimate=cost(2 * tokens * w_down.size, [w_down, w_down]),
+        cost_estimate=cost(4 * tokens * w_down.size, [w_down, w_down]),
         name="block_outputs",
     )(info, *args)
 
@@ -493,16 +488,11 @@
         scales,
     )
     second_far, second_other = swap(hidden_second, "xh"), swap(hidden_second, "c")
-    first_far, second_other = lax.optimization_barrier((first_far, second_other))
-    produced_first = block_outputs(
-        place, (hidden_first, first_other, first_far, swap(first_far, "c")), w_down
-    )
-    second_far, produced_first = lax.optimization_barrier((second_far, produced_first))
     produced = block_outputs(
         place,
+        (hidden_first, first_other, first_far, swap(first_far, "c")),
         (hidden_second, second_other, second_far, swap(second_far, "c")),
         w_down,
-        produced_first,
     )
 
     square, produced = lax.optimization_barrier((square, produced))

time: 174 us -> 172 us (0.989)
  waiting for transfers between devices: 65.9 us -> 63.9 us
    ppermute x15, waiting for transfers between devices: 37.6 us -> 35.7 us  [swap(): return lax.ppermute(array, axis, [(0, 1), (1, 0)])]
    pallas_call x2 -> x1, Pallas kernels: 5.87 us -> 5.16 us  [block_outputs(): pl.pallas_call(down_kernel, in_specs=[pl.BlockSpec(memory_space=pltpu.SME...]
    unnamed x32 -> x36, local copies, waits for them, and re-layouts: 7.63 us -> 7.64 us
  transfers between devices with their start and end apart: 28 -> 28, of which waited for: 11 -> 11; matrix products, arithmetic and copies ran while one was open for 3% -> 3% of each run, Pallas kernels for 17% -> 16%
where the time goes in v5:
time: 172 us; the launch traced here: 171 us
  waiting for transfers between devices  63.9 us (37%)
  starting transfers between devices  42.6 us (25%)
  Pallas kernels  33.2 us (19%)
  blocking collectives  16.1 us (9%)
  local copies, waits for them, and re-layouts  10.5 us (6%)
  other arithmetic  3.4 us (2%)
    ppermute x15, waiting for transfers between devices, swap(): return lax.ppermute(array, axis, [(0, 1), (1, 0)])  35.7 us
    pallas_call x2, Pallas kernels, attend(): pl.pallas_call(lambda *refs: attention_kernel(*refs, parts=parts, last=be...  18.9 us
    all_to_all x1, blocking collectives, on_device(): lax.all_to_all(outgoing, ('z', 'y'), split_axis=0, concat_axis=0, tiled=T...  16.1 us
    ppermute x4, waiting for transfers between devices, shift_x(): lax.ppermute(array, ('xl', 'xh'), [(index[x], index[(x + by) % 4]) for x...  12.6 us
    ppermute x6, waiting for transfers between devices, shift(): lax.ppermute(array, axis, [(i, (i + by) % size) for i in range(size)])  12.4 us
    ppermute x15, starting transfers between devices, swap(): return lax.ppermute(array, axis, [(0, 1), (1, 0)])  11.1 us
    ppermute x6, starting transfers between devices, shift(): lax.ppermute(array, axis, [(i, (i + by) % size) for i in range(size)])  9.89 us
    pallas_call x2, Pallas kernels, hidden_units(): pl.pallas_call(lambda *refs: hidden_kernel(*refs, parts=parts), in_specs=...  8.26 us
  transfers between devices with their start and end apart: 28, of which 11 were waited for; matrix products, arithmetic and copies ran while one was open for 3% of the time, Pallas kernels for 16%

profile of v5, /device:TPU:0, one launch (start us, length us, event | category | flops | bytes accessed | tf_op | source)
XLA Modules:
  0.0 171.3 jit_solution(11901724989251577353)
XLA Ops:
  4.6 2.2 %collective-permute-start.4 = (bf16[528,512]{1,0:T(8,128)(2,1)S(1)}, bf16[528,512]{1,0:T(8,128)(2,1)}, u32[]{:S(2)}, u32[]{:S(2)}) collective-permute-start(bf16[528,512]{1,0:T(8,128)(2,1)S(1)} %bitcast.49), channel_id=1, source_target_pairs={{0,96},{32,0},{64,32},{96,64},{1,97},{33,1},{65,33},{97,65},{2,98}... | collective-permute-start | bytes 1622024 | tf_op jit(solution)/shard_map/ppermute | solution.py:346
  10.8 5.5 %all-to-all-start = ((bf16[8,2,16,1536]{3,2,1,0:T(8,128)(2,1)}), bf16[8,2,16,1536]{3,2,1,0:T(8,128)(2,1)S(1)}, u32[]{:S(2)}, u32[]{:S(2)}) async-start(bf16[8,2,16,1536]{3,2,1,0:T(8,128)(2,1)} %broadcast_in_dim.18), calls=%async_computation | async-start | bytes 1572864 | tf_op jit(solution)/shard_map/all_to_all | solution.py:390
  17.7 2.2 %collective-permute-done.refs_3_ = bf16[528,512]{1,0:T(8,128)(2,1)S(1)} collective-permute-done((bf16[528,512]{1,0:T(8,128)(2,1)S(1)}, bf16[528,512]{1,0:T(8,128)(2,1)S(1)}, u32[]{:S(2)}, u32[]{:S(2)}) %collective-permute-start) | collective-permute-done | bytes 540704 | tf_op jit(solution)/shard_map/ppermute | solution.py:346
  19.9 10.3 %collective-permute-done.2.refs_7_ = bf16[528,512]{1,0:T(8,128)(2,1)S(1)} collective-permute-done((bf16[528,512]{1,0:T(8,128)(2,1)S(1)}, bf16[528,512]{1,0:T(8,128)(2,1)S(1)}, u32[]{:S(2)}, u32[]{:S(2)}) %collective-permute-start.2) | collective-permute-done | bytes 540704 | tf_op jit(solution)/shard_map/ppermute | solution.py:346
  30.1 3.5 %collective-permute-start.3 = (bf16[528,512]{1,0:T(8,128)(2,1)S(1)}, bf16[528,512]{1,0:T(8,128)(2,1)}, u32[]{:S(2)}, u32[]{:S(2)}) collective-permute-start(bf16[528,512]{1,0:T(8,128)(2,1)S(1)} %collective-permute-done.2.refs_7_), channel_id=1, source_target_pairs={{0,96},{32,0},{64,32},{96,64},{1,97},{33,1},{65,33},{97,65},{2,98}... | collective-permute-start | bytes 1622024 | tf_op jit(solution)/shard_map/ppermute | solution.py:346
  33.9 11.8 %attend.2 = (f32[2,2,768,128]{3,2,1,0:T(8,128)S(1)}, f32[2,2,768,128]{3,2,1,0:T(8,128)S(1)}) custom-call(s32[8]{0:T(128)S(1)} %stack.101.refs_0_, bf16[8,2,16,1536]{3,2,1,0:T(8,128)(2,1)S(1)} %all-to-all-done.refs_1_, bf16[528,512]{1,0:T(8,128)(2,1)S(1)} %bitcast.50, bf16[528,512]{1,0:T(8,128)(2,1)S(1)} %collective-permute-done.refs_3_, ...), custom_call_target="tpu_custom_call" | custom-call | flops 5234491392 | bytes 4030464 | tf_op jit(solution)/shard_map/attend/pallas_call | solution.py:154
  45.8 7.1 %attend.3 = bf16[8,2,16,1664]{3,2,1,0:T(8,128)(2,1)S(1)} custom-call(s32[6]{0:T(128)S(1)} %stack.98.refs_0_, bf16[8,2,16,1536]{3,2,1,0:T(8,128)(2,1)S(1)} %all-to-all-done.refs_1_, bf16[528,512]{1,0:T(8,128)(2,1)} %collective-permute-done.1.refs_2_, bf16[528,512]{1,0:T(8,128)(2,1)} %collective-permute-done.3.refs_3_, ...), custom_call_target="tpu_custom_call" | custom-call | flops 2013265920 | bytes 5013504 | tf_op jit(solution)/shard_map/attend/pallas_call | solution.py:154
  53.8 5.5 %all-to-all-start.1 = ((bf16[8,2,16,1664]{3,2,1,0:T(8,128)(2,1)}), bf16[8,2,16,1664]{3,2,1,0:T(8,128)(2,1)S(1)}, u32[]{:S(2)}, u32[]{:S(2)}) async-start(bf16[8,2,16,1664]{3,2,1,0:T(8,128)(2,1)} %copy-done.2), calls=%async_computation.1 | async-start | bytes 1703936 | tf_op jit(solution)/shard_map/all_to_all | solution.py:402
  59.7 2.8 %collective-permute-start.7 = (bf16[2,1536]{1,0:T(2,128)(2,1)S(1)}, bf16[2,1536]{1,0:T(2,128)(2,1)S(1)}, u32[]{:S(2)}, u32[]{:S(2)}) collective-permute-start(bf16[2,1536]{1,0:T(2,128)(2,1)S(1)} %broadcast_select_fusion.1), channel_id=1, source_target_pairs={{0,2},{2,0},{1,3},{3,1},{4,6},{6,4},{5,7},{7,5},{8,10},{10,8},{9,1... | collective-permute-start | bytes 18440 | tf_op jit(solution)/shard_map/ppermute | solution.py:342
  62.5 8.3 %collective-permute-done.7 = bf16[2,1536]{1,0:T(2,128)(2,1)S(1)} collective-permute-done((bf16[2,1536]{1,0:T(2,128)(2,1)S(1)}, bf16[2,1536]{1,0:T(2,128)(2,1)S(1)}, u32[]{:S(2)}, u32[]{:S(2)}) %collective-permute-start.7) | collective-permute-done | bytes 6176 | tf_op jit(solution)/shard_map/ppermute | solution.py:342
  72.8 16.1 %all_to_all.20 = bf16[16,16,1536]{2,1,0:T(8,128)(2,1)S(1)} all-to-all(bf16[16,16,1536]{2,1,0:T(8,128)(2,1)S(1)} %get-tuple-element.26), channel_id=1, replica_groups=mesh['z'=4,'y'=4,'xl'=2,'xh'=2,'c'=2] {'z','y'}, dimensions={0} | all-to-all | bytes 1572864 | tf_op jit(solution)/shard_map/all_to_all | solution.py:456
  89.9 2.2 %collective-permute-start.9 = (bf16[256,1536]{1,0:T(8,128)(2,1)S(1)}, bf16[256,1536]{1,0:T(8,128)(2,1)S(1)}, u32[]{:S(2)}, u32[]{:S(2)}) collective-permute-start(bf16[256,1536]{1,0:T(8,128)(2,1)S(1)} %bitcast.45), channel_id=1, source_target_pairs={{0,6},{4,0},{2,4},{6,2},{1,7},{5,1},{3,5},{7,3},{8,14},{12,8},{10,... | collective-permute-start | bytes 2359304 | tf_op jit(solution)/shard_map/ppermute | solution.py:351
  92.1 12.6 %collective-permute-done.8.below_ref.refs_1_ = bf16[256,1536]{1,0:T(8,128)(2,1)S(1)} collective-permute-done((bf16[256,1536]{1,0:T(8,128)(2,1)S(1)}, bf16[256,1536]{1,0:T(8,128)(2,1)S(1)}, u32[]{:S(2)}, u32[]{:S(2)}) %collective-permute-start.8) | collective-permute-done | bytes 786464 | tf_op jit(solution)/shard_map/ppermute | solution.py:351
  105.6 3.0 %collective-permute-start.11 = (bf16[128,1536]{1,0:T(8,128)(2,1)S(1)}, bf16[128,1536]{1,0:T(8,128)(2,1)S(1)}, u32[]{:S(2)}, u32[]{:S(2)}) collective-permute-start(bf16[128,1536]{1,0:T(8,128)(2,1)S(1)} %get-tuple-element.28), channel_id=1, source_target_pairs={{0,6},{4,0},{2,4},{6,2},{1,7},{5,1},{3,5},{7,3},{8,14},{12,8},{10,... | collective-permute-start | bytes 1179656 | tf_op jit(solution)/shard_map/ppermute | solution.py:351
  108.6 2.8 %copy-done = bf16[1,6144,512]{2,1,0:T(8,128)(2,1)S(1)} copy-done((bf16[1,6144,512]{2,1,0:T(8,128)(2,1)S(1)}, bf16[1,6144,512]{2,1,0:T(8,128)(2,1)}, u32[]{:S(2)}) %copy-start) | copy-done | bytes 6291480
  111.4 2.8 %copy-done.1 = bf16[1,6144,512]{2,1,0:T(8,128)(2,1)S(1)} copy-done((bf16[1,6144,512]{2,1,0:T(8,128)(2,1)S(1)}, bf16[1,6144,512]{2,1,0:T(8,128)(2,1)}, u32[]{:S(2)}) %copy-start.1) | copy-done | bytes 6291480
  114.2 4.1 %hidden_units.2.refs_0_ = bf16[256,512]{1,0:T(8,128)(2,1)S(1)} custom-call(s32[4]{0:T(128)S(1)} %get-tuple-element.29.refs_0_, bf16[256,1536]{1,0:T(8,128)(2,1)S(1)} %collective-permute-done.8.below_ref.refs_1_, bf16[256,1536]{1,0:T(8,128)(2,1)S(1)} %collective-permute-done.12.refs_2_, bf16[256,1536]{1,0:T(8,128)(2,1)S(1)} %collective-permute-done.9.above_ref.refs_3_, ...), custom_call_target="tpu_custom_call" | custom-call | flops 3221225472 | bytes 15728640 | tf_op jit(solution)/shard_map/hidden_units/pallas_call | solution.py:282
  121.1 4.2 %hidden_units.3.refs_4_ = bf16[256,512]{1,0:T(8,128)(2,1)S(1)} custom-call(s32[4]{0:T(128)S(1)} %get-tuple-element.32.refs_0_, bf16[256,1536]{1,0:T(8,128)(2,1)S(1)} %bitcast.47, bf16[256,1536]{1,0:T(8,128)(2,1)S(1)} %collective-permute-done.17.refs_2_, bf16[128,1536]{1,0:T(8,128)(2,1)S(1)} %collective-permute-done.10.refs_3_, ...), custom_call_target="tpu_custom_call" | custom-call | flops 3221225472 | bytes 15728640 | tf_op jit(solution)/shard_map/hidden_units/pallas_call | solution.py:282
  129.6 5.6 %collective-permute-done.21.refs_6_ = bf16[256,512]{1,0:T(8,128)(2,1)S(1)} collective-permute-done((bf16[256,512]{1,0:T(8,128)(2,1)S(1)}, bf16[256,512]{1,0:T(8,128)(2,1)S(1)}, u32[]{:S(2)}, u32[]{:S(2)}) %collective-permute-start.21) | collective-permute-done | bytes 262176 | tf_op jit(solution)/shard_map/ppermute | solution.py:342
  136.7 5.2 %block_outputs.1 = bf16[16,2,16,1536]{3,2,1,0:T(8,128)(2,1)} custom-call(s32[2]{0:T(128)S(1)} %pad_add_fusion.2.info_ref, bf16[256,512]{1,0:T(8,128)(2,1)S(1)} %hidden_units.2.refs_0_, bf16[256,512]{1,0:T(8,128)(2,1)S(1)} %collective-permute-done.14.refs_1_, bf16[256,512]{1,0:T(8,128)(2,1)S(1)} %collective-permute-done.15.refs_2_, ...), custom_call_target="tpu_custom_call" | custom-call | flops 3221225472 | bytes 12582912 | tf_op jit(solution)/shard_map/block_outputs/pallas_call | solution.py:323
  141.9 4.0 %all-to-all-start.3 = ((bf16[32,16,1536]{2,1,0:T(8,128)(2,1)}), bf16[32,16,1536]{2,1,0:T(8,128)(2,1)S(1)}, u32[]{:S(2)}, u32[]{:S(2)}) async-start(bf16[32,16,1536]{2,1,0:T(8,128)(2,1)} %bitcast.24), calls=%async_computation.3 | async-start | bytes 3145728 | tf_op jit(solution)/shard_map/all_to_all | solution.py:504
  147.1 2.4 %collective-permute-start.24 = (f32[32,128]{1,0:T(8,128)S(1)}, f32[32,128]{1,0:T(8,128)S(1)}, u32[]{:S(2)}, u32[]{:S(2)}) collective-permute-start(f32[32,128]{1,0:T(8,128)S(1)} %add.115), channel_id=1, source_target_pairs={{0,2},{2,0},{1,3},{3,1},{4,6},{6,4},{5,7},{7,5},{8,10},{10,8},{9,1... | collective-permute-start | bytes 49160 | tf_op jit(solution)/shard_map/ppermute | solution.py:342
  149.5 17.2 %collective-permute-done.24 = f32[32,128]{1,0:T(8,128)S(1)} collective-permute-done((f32[32,128]{1,0:T(8,128)S(1)}, f32[32,128]{1,0:T(8,128)S(1)}, u32[]{:S(2)}, u32[]{:S(2)}) %collective-permute-start.24) | collective-permute-done | bytes 16416 | tf_op jit(solution)/shard_map/ppermute | solution.py:342
  167.9 2.2 %all-to-all-done.3 = bf16[32,16,1536]{2,1,0:T(8,128)(2,1)S(1)} async-done(((bf16[32,16,1536]{2,1,0:T(8,128)(2,1)}), bf16[32,16,1536]{2,1,0:T(8,128)(2,1)S(1)}, u32[]{:S(2)}, u32[]{:S(2)}) %all-to-all-start.3) | async-done | bytes 1572896 | tf_op jit(solution)/shard_map/all_to_all | solution.py:504
  (120 shorter events, 26.6 us)
Async XLA Ops:
  2.6 17.3 %collective-permute-start = (bf16[528,512]{1,0:T(8,128)(2,1)S(1)}, bf16[528,512]{1,0:T(8,128)(2,1)S(1)}, u32[]{:S(2)}, u32[]{:S(2)}) collective-permute-start(bf16[528,512]{1,0:T(8,128)(2,1)S(1)} %bitcast.48), channel_id=1, source_target_pairs={{0,32},{32,64},{64,96},{96,0},{1,33},{33,65},{65,97},{97,1},{2,34}... | collective-permute-start | bytes 1622024 | tf_op jit(solution)/shard_map/ppermute | solution.py:346
  4.6 29.3 %collective-permute-start.4 = (bf16[528,512]{1,0:T(8,128)(2,1)S(1)}, bf16[528,512]{1,0:T(8,128)(2,1)}, u32[]{:S(2)}, u32[]{:S(2)}) collective-permute-start(bf16[528,512]{1,0:T(8,128)(2,1)S(1)} %bitcast.49), channel_id=1, source_target_pairs={{0,96},{32,0},{64,32},{96,64},{1,97},{33,1},{65,33},{97,65},{2,98}... | collective-permute-start | bytes 1622024 | tf_op jit(solution)/shard_map/ppermute | solution.py:346
  7.7 22.5 %collective-permute-start.2 = (bf16[528,512]{1,0:T(8,128)(2,1)S(1)}, bf16[528,512]{1,0:T(8,128)(2,1)S(1)}, u32[]{:S(2)}, u32[]{:S(2)}) collective-permute-start(bf16[528,512]{1,0:T(8,128)(2,1)S(1)} %bitcast.51), channel_id=1, source_target_pairs={{0,96},{32,0},{64,32},{96,64},{1,97},{33,1},{65,33},{97,65},{2,98}... | collective-permute-start | bytes 1622024 | tf_op jit(solution)/shard_map/ppermute | solution.py:346
  9.7 24.2 %collective-permute-start.5 = (bf16[528,512]{1,0:T(8,128)(2,1)S(1)}, bf16[528,512]{1,0:T(8,128)(2,1)}, u32[]{:S(2)}, u32[]{:S(2)}) collective-permute-start(bf16[528,512]{1,0:T(8,128)(2,1)S(1)} %bitcast.52), channel_id=1, source_target_pairs={{0,32},{32,64},{64,96},{96,0},{1,33},{33,65},{65,97},{97,1},{2,34}... | collective-permute-start | bytes 1622024 | tf_op jit(solution)/shard_map/ppermute | solution.py:346
  10.8 23.1 %all-to-all-start = ((bf16[8,2,16,1536]{3,2,1,0:T(8,128)(2,1)}), bf16[8,2,16,1536]{3,2,1,0:T(8,128)(2,1)S(1)}, u32[]{:S(2)}, u32[]{:S(2)}) async-start(bf16[8,2,16,1536]{3,2,1,0:T(8,128)(2,1)} %broadcast_in_dim.18), calls=%async_computation | async-start | bytes 1572864 | tf_op jit(solution)/shard_map/all_to_all | solution.py:390
  16.3 43.3 %collective-permute-start.6 = (bf16[1536]{0:T(1024)(128)(2,1)S(1)}, bf16[1536]{0:T(1024)(128)(2,1)S(1)}, u32[]{:S(2)}, u32[]{:S(2)}) collective-permute-start(bf16[1536]{0:T(1024)(128)(2,1)S(1)} %copy-done.5), channel_id=1, source_target_pairs={{0,1},{1,0},{2,3},{3,2},{4,5},{5,4},{6,7},{7,6},{8,9},{9,8},{10,11... | collective-permute-start | bytes 9224 | tf_op jit(solution)/shard_map/ppermute | solution.py:342
  19.9 25.9 %collective-permute-start.1 = (bf16[528,512]{1,0:T(8,128)(2,1)S(1)}, bf16[528,512]{1,0:T(8,128)(2,1)}, u32[]{:S(2)}, u32[]{:S(2)}) collective-permute-start(bf16[528,512]{1,0:T(8,128)(2,1)S(1)} %collective-permute-done.refs_3_), channel_id=1, source_target_pairs={{0,32},{32,64},{64,96},{96,0},{1,33},{33,65},{65,97},{97,1},{2,34}... | collective-permute-start | bytes 1622024 | tf_op jit(solution)/shard_map/ppermute | solution.py:346
  30.1 15.6 %collective-permute-start.3 = (bf16[528,512]{1,0:T(8,128)(2,1)S(1)}, bf16[528,512]{1,0:T(8,128)(2,1)}, u32[]{:S(2)}, u32[]{:S(2)}) collective-permute-start(bf16[528,512]{1,0:T(8,128)(2,1)S(1)} %collective-permute-done.2.refs_7_), channel_id=1, source_target_pairs={{0,96},{32,0},{64,32},{96,64},{1,97},{33,1},{65,33},{97,65},{2,98}... | collective-permute-start | bytes 1622024 | tf_op jit(solution)/shard_map/ppermute | solution.py:346
  53.8 18.1 %all-to-all-start.1 = ((bf16[8,2,16,1664]{3,2,1,0:T(8,128)(2,1)}), bf16[8,2,16,1664]{3,2,1,0:T(8,128)(2,1)S(1)}, u32[]{:S(2)}, u32[]{:S(2)}) async-start(bf16[8,2,16,1664]{3,2,1,0:T(8,128)(2,1)} %copy-done.2), calls=%async_computation.1 | async-start | bytes 1703936 | tf_op jit(solution)/shard_map/all_to_all | solution.py:402
  59.7 11.2 %collective-permute-start.7 = (bf16[2,1536]{1,0:T(2,128)(2,1)S(1)}, bf16[2,1536]{1,0:T(2,128)(2,1)S(1)}, u32[]{:S(2)}, u32[]{:S(2)}) collective-permute-start(bf16[2,1536]{1,0:T(2,128)(2,1)S(1)} %broadcast_select_fusion.1), channel_id=1, source_target_pairs={{0,2},{2,0},{1,3},{3,1},{4,6},{6,4},{5,7},{7,5},{8,10},{10,8},{9,1... | collective-permute-start | bytes 18440 | tf_op jit(solution)/shard_map/ppermute | solution.py:342
  88.9 15.8 %collective-permute-start.8 = (bf16[256,1536]{1,0:T(8,128)(2,1)S(1)}, bf16[256,1536]{1,0:T(8,128)(2,1)S(1)}, u32[]{:S(2)}, u32[]{:S(2)}) collective-permute-start(bf16[256,1536]{1,0:T(8,128)(2,1)S(1)} %bitcast.44), channel_id=1, source_target_pairs={{0,4},{4,2},{2,6},{6,0},{1,5},{5,3},{3,7},{7,1},{8,12},{12,10},{10... | collective-permute-start | bytes 2359304 | tf_op jit(solution)/shard_map/ppermute | solution.py:351
  89.9 14.8 %collective-permute-start.9 = (bf16[256,1536]{1,0:T(8,128)(2,1)S(1)}, bf16[256,1536]{1,0:T(8,128)(2,1)S(1)}, u32[]{:S(2)}, u32[]{:S(2)}) collective-permute-start(bf16[256,1536]{1,0:T(8,128)(2,1)S(1)} %bitcast.45), channel_id=1, source_target_pairs={{0,6},{4,0},{2,4},{6,2},{1,7},{5,1},{3,5},{7,3},{8,14},{12,8},{10,... | collective-permute-start | bytes 2359304 | tf_op jit(solution)/shard_map/ppermute | solution.py:351
  104.7 3.9 %collective-permute-start.12 = (bf16[256,1536]{1,0:T(8,128)(2,1)S(1)}, bf16[256,1536]{1,0:T(8,128)(2,1)S(1)}, u32[]{:S(2)}, u32[]{:S(2)}) collective-permute-start(bf16[256,1536]{1,0:T(8,128)(2,1)S(1)} %collective-permute-done.8.below_ref.refs_1_), channel_id=1, source_target_pairs={{0,1},{1,0},{2,3},{3,2},{4,5},{5,4},{6,7},{7,6},{8,9},{9,8},{10,11... | collective-permute-start | bytes 2359304 | tf_op jit(solution)/shard_map/ppermute | solution.py:342
  104.7 3.9 %collective-permute-start.13 = (bf16[256,1536]{1,0:T(8,128)(2,1)S(1)}, bf16[256,1536]{1,0:T(8,128)(2,1)S(1)}, u32[]{:S(2)}, u32[]{:S(2)}) collective-permute-start(bf16[256,1536]{1,0:T(8,128)(2,1)S(1)} %collective-permute-done.9.above_ref.refs_3_), channel_id=1, source_target_pairs={{0,1},{1,0},{2,3},{3,2},{4,5},{5,4},{6,7},{7,6},{8,9},{9,8},{10,11... | collective-permute-start | bytes 2359304 | tf_op jit(solution)/shard_map/ppermute | solution.py:342
  105.3 13.0 %collective-permute-start.10 = (bf16[128,1536]{1,0:T(8,128)(2,1)S(1)}, bf16[128,1536]{1,0:T(8,128)(2,1)S(1)}, u32[]{:S(2)}, u32[]{:S(2)}) collective-permute-start(bf16[128,1536]{1,0:T(8,128)(2,1)S(1)} %get-tuple-element.27), channel_id=1, source_target_pairs={{0,4},{4,2},{2,6},{6,0},{1,5},{5,3},{3,7},{7,1},{8,12},{12,10},{10... | collective-permute-start | bytes 1179656 | tf_op jit(solution)/shard_map/ppermute | solution.py:351
  105.6 12.6 %collective-permute-start.11 = (bf16[128,1536]{1,0:T(8,128)(2,1)S(1)}, bf16[128,1536]{1,0:T(8,128)(2,1)S(1)}, u32[]{:S(2)}, u32[]{:S(2)}) collective-permute-start(bf16[128,1536]{1,0:T(8,128)(2,1)S(1)} %get-tuple-element.28), channel_id=1, source_target_pairs={{0,6},{4,0},{2,4},{6,2},{1,7},{5,1},{3,5},{7,3},{8,14},{12,8},{10,... | collective-permute-start | bytes 1179656 | tf_op jit(solution)/shard_map/ppermute | solution.py:351
  108.6 12.4 %collective-permute-start.17 = (bf16[256,1536]{1,0:T(8,128)(2,1)S(1)}, bf16[256,1536]{1,0:T(8,128)(2,1)S(1)}, u32[]{:S(2)}, u32[]{:S(2)}) collective-permute-start(bf16[256,1536]{1,0:T(8,128)(2,1)S(1)} %bitcast.46), channel_id=1, source_target_pairs={{0,1},{1,0},{2,3},{3,2},{4,5},{5,4},{6,7},{7,6},{8,9},{9,8},{10,11... | collective-permute-start | bytes 2359304 | tf_op jit(solution)/shard_map/ppermute | solution.py:342
  118.9 10.1 %collective-permute-start.15 = (bf16[256,512]{1,0:T(8,128)(2,1)S(1)}, bf16[256,512]{1,0:T(8,128)(2,1)S(1)}, u32[]{:S(2)}, u32[]{:S(2)}) collective-permute-start(bf16[256,512]{1,0:T(8,128)(2,1)S(1)} %hidden_units.2.refs_0_), channel_id=1, source_target_pairs={{0,2},{2,0},{1,3},{3,1},{4,6},{6,4},{5,7},{7,5},{8,10},{10,8},{9,1... | collective-permute-start | bytes 786440 | tf_op jit(solution)/shard_map/ppermute | solution.py:342
  125.3 9.9 %collective-permute-start.21 = (bf16[256,512]{1,0:T(8,128)(2,1)S(1)}, bf16[256,512]{1,0:T(8,128)(2,1)S(1)}, u32[]{:S(2)}, u32[]{:S(2)}) collective-permute-start(bf16[256,512]{1,0:T(8,128)(2,1)S(1)} %hidden_units.3.refs_4_), channel_id=1, source_target_pairs={{0,2},{2,0},{1,3},{3,1},{4,6},{6,4},{5,7},{7,5},{8,10},{10,8},{9,1... | collective-permute-start | bytes 786440 | tf_op jit(solution)/shard_map/ppermute | solution.py:342
  127.1 8.1 %collective-permute-start.14 = (bf16[256,512]{1,0:T(8,128)(2,1)S(1)}, bf16[256,512]{1,0:T(8,128)(2,1)S(1)}, u32[]{:S(2)}, u32[]{:S(2)}) collective-permute-start(bf16[256,512]{1,0:T(8,128)(2,1)S(1)} %hidden_units.2.refs_0_), channel_id=1, source_target_pairs={{0,1},{1,0},{2,3},{3,2},{4,5},{5,4},{6,7},{7,6},{8,9},{9,8},{10,11... | collective-permute-start | bytes 786440 | tf_op jit(solution)/shard_map/ppermute | solution.py:342
  129.1 6.1 %collective-permute-start.16 = (bf16[256,512]{1,0:T(8,128)(2,1)S(1)}, bf16[256,512]{1,0:T(8,128)(2,1)S(1)}, u32[]{:S(2)}, u32[]{:S(2)}) collective-permute-start(bf16[256,512]{1,0:T(8,128)(2,1)S(1)} %collective-permute-done.15.refs_2_), channel_id=1, source_target_pairs={{0,1},{1,0},{2,3},{3,2},{4,5},{5,4},{6,7},{7,6},{8,9},{9,8},{10,11... | collective-permute-start | bytes 786440 | tf_op jit(solution)/shard_map/ppermute | solution.py:342
  129.1 6.1 %collective-permute-start.20 = (bf16[256,512]{1,0:T(8,128)(2,1)S(1)}, bf16[256,512]{1,0:T(8,128)(2,1)S(1)}, u32[]{:S(2)}, u32[]{:S(2)}) collective-permute-start(bf16[256,512]{1,0:T(8,128)(2,1)S(1)} %hidden_units.3.refs_4_), channel_id=1, source_target_pairs={{0,1},{1,0},{2,3},{3,2},{4,5},{5,4},{6,7},{7,6},{8,9},{9,8},{10,11... | collective-permute-start | bytes 786440 | tf_op jit(solution)/shard_map/ppermute | solution.py:342
  141.9 28.2 %all-to-all-start.3 = ((bf16[32,16,1536]{2,1,0:T(8,128)(2,1)}), bf16[32,16,1536]{2,1,0:T(8,128)(2,1)S(1)}, u32[]{:S(2)}, u32[]{:S(2)}) async-start(bf16[32,16,1536]{2,1,0:T(8,128)(2,1)} %bitcast.24), calls=%async_computation.3 | async-start | bytes 3145728 | tf_op jit(solution)/shard_map/all_to_all | solution.py:504
  147.1 19.6 %collective-permute-start.24 = (f32[32,128]{1,0:T(8,128)S(1)}, f32[32,128]{1,0:T(8,128)S(1)}, u32[]{:S(2)}, u32[]{:S(2)}) collective-permute-start(f32[32,128]{1,0:T(8,128)S(1)} %add.115), channel_id=1, source_target_pairs={{0,2},{2,0},{1,3},{3,1},{4,6},{6,4},{5,7},{7,5},{8,10},{10,8},{9,1... | collective-permute-start | bytes 49160 | tf_op jit(solution)/shard_map/ppermute | solution.py:342
  (20 other events, 255.0 us)

commit v6 on v5

--- a/solution.py
+++ b/solution.py
@@ -218,24 +218,41 @@
     )(got, placing, gain)
 
 
-def halves_kernel(below_ref, above_ref, low_ref, high_ref):
+def bring_kernel(*refs):
+    refs[-1][...] = jnp.zeros_like(refs[-1])
+
+
+def bring(token, *arrays):
+    return pl.pallas_call(
+        bring_kernel,
+        in_specs=[pl.BlockSpec(memory_space=pl.ANY)]
+        + [pl.BlockSpec(memory_space=pltpu.VMEM)] * len(arrays),
+        out_specs=pl.BlockSpec(memory_space=pltpu.VMEM),
+        out_shape=jax.ShapeDtypeStruct((8, LANES), F32),
+        compiler_params=pltpu.CompilerParams(vmem_limit_bytes=1024 * 1024),
+        cost_estimate=cost(0, arrays),
+        name="bring",
+    )(token, *arrays)
+
+
+def halves_kernel(below_ref, above_ref, token_ref, low_ref, high_ref):
     middle = low_ref.shape[0]
     low_ref[...] = below_ref[:middle]
     high_ref[...] = above_ref[middle:]
 
 
-def halves(below, above):
+def halves(below, above, token):
     rows, width = below.shape
     half = jax.ShapeDtypeStruct((rows // 2, width), BF16)
     return pl.pallas_call(
         halves_kernel,
-        in_specs=[pl.BlockSpec(memory_space=pltpu.VMEM)] * 2,
+        in_specs=[pl.BlockSpec(memory_space=pltpu.VMEM)] * 3,
         out_specs=[pl.BlockSpec(memory_space=pltpu.VMEM)] * 2,
         out_shape=[half, half],
         compiler_params=pltpu.CompilerParams(vmem_limit_bytes=SMALL_LIMIT),
         cost_estimate=cost(0, [below, above]),
         name="halves",
-    )(below, above)
+    )(below, above, token)
 
 
 def hidden_kernel(info_ref, *refs, parts):
@@ -460,7 +477,9 @@
 
     from_below = shift_x(own_block, 1)
     from_above = shift_x(own_block, -1)
-    low_half, high_half = halves(from_below, from_above)
+    brought = bring(own_block, w_gate, w_up)
+    from_below, from_above, brought = lax.optimization_barrier((from_below, from_above, brought))
+    low_half, high_half = halves(from_below, from_above, brought)
     far_low, far_high = shift_x(low_half, 1), shift_x(high_half, -1)
     own_other = swap(own_block, "c")
     below_other = swap(from_below, "c")

time: 172 us -> 171 us (level)
  waiting for transfers between devices: 63.9 us -> 59.7 us
  local copies, waits for them, and re-layouts: 10.5 us -> 13.3 us
    ppermute x4, waiting for transfers between devices: 12.6 us -> 9.12 us  [shift_x(): lax.ppermute(array, ('xl', 'xh'), [(index[x], index[(x + by) % 4]) for x...]
    unnamed x36 -> x34, local copies, waits for them, and re-layouts: 7.64 us -> 10.4 us
  transfers between devices with their start and end apart: 28 -> 28, of which waited for: 11 -> 12; matrix products, arithmetic and copies ran while one was open for 3% -> 3% of each run, Pallas kernels for 16% -> 16%
where the time goes in v6:
time: 171 us
  waiting for transfers between devices  59.7 us (35%)
  starting transfers between devices  43.6 us (25%)
  Pallas kernels  33.3 us (19%)
  blocking collectives  16.1 us (9%)
  local copies, waits for them, and re-layouts  13.3 us (8%)
  other arithmetic  3.4 us (2%)
    ppermute x15, waiting for transfers between devices, swap(): return lax.ppermute(array, axis, [(0, 1), (1, 0)])  35.3 us
    pallas_call x2, Pallas kernels, attend(): pl.pallas_call(lambda *refs: attention_kernel(*refs, parts=parts, last=be...  18.9 us
    all_to_all x1, blocking collectives, on_device(): lax.all_to_all(outgoing, ('z', 'y'), split_axis=0, concat_axis=0, tiled=T...  16.1 us
    ppermute x6, waiting for transfers between devices, shift(): lax.ppermute(array, axis, [(i, (i + by) % size) for i in range(size)])  12.4 us
    ppermute x15, starting transfers between devices, swap(): return lax.ppermute(array, axis, [(0, 1), (1, 0)])  12.1 us
    unnamed x34, local copies, waits for them, and re-layouts  10.4 us
    ppermute x6, starting transfers between devices, shift(): lax.ppermute(array, axis, [(i, (i + by) % size) for i in range(size)])  9.89 us
    ppermute x4, waiting for transfers between devices, shift_x(): lax.ppermute(array, ('xl', 'xh'), [(index[x], index[(x + by) % 4]) for x...  9.12 us
  transfers between devices with their start and end apart: 28, of which 12 were waited for; matrix products, arithmetic and copies ran while one was open for 3% of the time, Pallas kernels for 16%

profile of v6, /device:TPU:0, one launch (start us, length us, event | category | flops | bytes accessed | tf_op | source)
XLA Modules:
  0.0 170.9 jit_solution(15445503883599270321)
XLA Ops:
  4.6 2.2 %collective-permute-start.4 = (bf16[528,512]{1,0:T(8,128)(2,1)S(1)}, bf16[528,512]{1,0:T(8,128)(2,1)}, u32[]{:S(2)}, u32[]{:S(2)}) collective-permute-start(bf16[528,512]{1,0:T(8,128)(2,1)S(1)} %bitcast.50), channel_id=1, source_target_pairs={{0,96},{32,0},{64,32},{96,64},{1,97},{33,1},{65,33},{97,65},{2,98}... | collective-permute-start | bytes 1622024 | tf_op jit(solution)/shard_map/ppermute | solution.py:363
  10.8 5.5 %all-to-all-start = ((bf16[8,2,16,1536]{3,2,1,0:T(8,128)(2,1)}), bf16[8,2,16,1536]{3,2,1,0:T(8,128)(2,1)S(1)}, u32[]{:S(2)}, u32[]{:S(2)}) async-start(bf16[8,2,16,1536]{3,2,1,0:T(8,128)(2,1)} %broadcast_in_dim.18), calls=%async_computation | async-start | bytes 1572864 | tf_op jit(solution)/shard_map/all_to_all | solution.py:407
  19.9 10.3 %collective-permute-done.2.refs_7_ = bf16[528,512]{1,0:T(8,128)(2,1)S(1)} collective-permute-done((bf16[528,512]{1,0:T(8,128)(2,1)S(1)}, bf16[528,512]{1,0:T(8,128)(2,1)S(1)}, u32[]{:S(2)}, u32[]{:S(2)}) %collective-permute-start.2) | collective-permute-done | bytes 540704 | tf_op jit(solution)/shard_map/ppermute | solution.py:363
  30.1 3.5 %collective-permute-start.3 = (bf16[528,512]{1,0:T(8,128)(2,1)S(1)}, bf16[528,512]{1,0:T(8,128)(2,1)}, u32[]{:S(2)}, u32[]{:S(2)}) collective-permute-start(bf16[528,512]{1,0:T(8,128)(2,1)S(1)} %collective-permute-done.2.refs_7_), channel_id=1, source_target_pairs={{0,96},{32,0},{64,32},{96,64},{1,97},{33,1},{65,33},{97,65},{2,98}... | collective-permute-start | bytes 1622024 | tf_op jit(solution)/shard_map/ppermute | solution.py:363
  33.9 11.8 %attend.2 = (f32[2,2,768,128]{3,2,1,0:T(8,128)S(1)}, f32[2,2,768,128]{3,2,1,0:T(8,128)S(1)}) custom-call(s32[8]{0:T(128)S(1)} %stack.101.refs_0_, bf16[8,2,16,1536]{3,2,1,0:T(8,128)(2,1)S(1)} %all-to-all-done.refs_1_, bf16[528,512]{1,0:T(8,128)(2,1)S(1)} %bitcast.51, bf16[528,512]{1,0:T(8,128)(2,1)S(1)} %collective-permute-done.refs_3_, ...), custom_call_target="tpu_custom_call" | custom-call | flops 5234491392 | bytes 4030464 | tf_op jit(solution)/shard_map/attend/pallas_call | solution.py:154
  45.8 7.1 %attend.3 = bf16[8,2,16,1664]{3,2,1,0:T(8,128)(2,1)S(1)} custom-call(s32[6]{0:T(128)S(1)} %stack.98.refs_0_, bf16[8,2,16,1536]{3,2,1,0:T(8,128)(2,1)S(1)} %all-to-all-done.refs_1_, bf16[528,512]{1,0:T(8,128)(2,1)} %collective-permute-done.1.refs_2_, bf16[528,512]{1,0:T(8,128)(2,1)} %collective-permute-done.3.refs_3_, ...), custom_call_target="tpu_custom_call" | custom-call | flops 2013265920 | bytes 5013504 | tf_op jit(solution)/shard_map/attend/pallas_call | solution.py:154
  53.8 5.5 %all-to-all-start.1 = ((bf16[8,2,16,1664]{3,2,1,0:T(8,128)(2,1)}), bf16[8,2,16,1664]{3,2,1,0:T(8,128)(2,1)S(1)}, u32[]{:S(2)}, u32[]{:S(2)}) async-start(bf16[8,2,16,1664]{3,2,1,0:T(8,128)(2,1)} %copy-done.3), calls=%async_computation.1 | async-start | bytes 1703936 | tf_op jit(solution)/shard_map/all_to_all | solution.py:419
  59.7 2.8 %collective-permute-start.7 = (bf16[2,1536]{1,0:T(2,128)(2,1)S(1)}, bf16[2,1536]{1,0:T(2,128)(2,1)S(1)}, u32[]{:S(2)}, u32[]{:S(2)}) collective-permute-start(bf16[2,1536]{1,0:T(2,128)(2,1)S(1)} %broadcast_select_fusion.1), channel_id=1, source_target_pairs={{0,2},{2,0},{1,3},{3,1},{4,6},{6,4},{5,7},{7,5},{8,10},{10,8},{9,1... | collective-permute-start | bytes 18440 | tf_op jit(solution)/shard_map/ppermute | solution.py:359
  62.5 8.3 %collective-permute-done.7 = bf16[2,1536]{1,0:T(2,128)(2,1)S(1)} collective-permute-done((bf16[2,1536]{1,0:T(2,128)(2,1)S(1)}, bf16[2,1536]{1,0:T(2,128)(2,1)S(1)}, u32[]{:S(2)}, u32[]{:S(2)}) %collective-permute-start.7) | collective-permute-done | bytes 6176 | tf_op jit(solution)/shard_map/ppermute | solution.py:359
  72.8 16.1 %all_to_all.20 = bf16[16,16,1536]{2,1,0:T(8,128)(2,1)S(1)} all-to-all(bf16[16,16,1536]{2,1,0:T(8,128)(2,1)S(1)} %get-tuple-element.29), channel_id=1, replica_groups=mesh['z'=4,'y'=4,'xl'=2,'xh'=2,'c'=2] {'z','y'}, dimensions={0} | all-to-all | bytes 1572864 | tf_op jit(solution)/shard_map/all_to_all | solution.py:473
  89.9 2.2 %collective-permute-start.9 = (bf16[256,1536]{1,0:T(8,128)(2,1)S(1)}, bf16[256,1536]{1,0:T(8,128)(2,1)S(1)}, u32[]{:S(2)}, u32[]{:S(2)}) collective-permute-start(bf16[256,1536]{1,0:T(8,128)(2,1)S(1)} %bitcast.45), channel_id=1, source_target_pairs={{0,6},{4,0},{2,4},{6,2},{1,7},{5,1},{3,5},{7,3},{8,14},{12,8},{10,... | collective-permute-start | bytes 2359304 | tf_op jit(solution)/shard_map/ppermute | solution.py:368
  92.1 2.8 %copy-done = bf16[1,6144,512]{2,1,0:T(8,128)(2,1)S(1)} copy-done((bf16[1,6144,512]{2,1,0:T(8,128)(2,1)S(1)}, bf16[1,6144,512]{2,1,0:T(8,128)(2,1)}, u32[]{:S(2)}) %copy-start) | copy-done | bytes 6291480
  94.9 2.8 %copy-done.1 = bf16[1,6144,512]{2,1,0:T(8,128)(2,1)S(1)} copy-done((bf16[1,6144,512]{2,1,0:T(8,128)(2,1)S(1)}, bf16[1,6144,512]{2,1,0:T(8,128)(2,1)}, u32[]{:S(2)}) %copy-start.1) | copy-done | bytes 6291480
  97.7 7.0 %collective-permute-done.8.below_ref.refs_1_ = bf16[256,1536]{1,0:T(8,128)(2,1)S(1)} collective-permute-done((bf16[256,1536]{1,0:T(8,128)(2,1)S(1)}, bf16[256,1536]{1,0:T(8,128)(2,1)S(1)}, u32[]{:S(2)}, u32[]{:S(2)}) %collective-permute-start.8) | collective-permute-done | bytes 786464 | tf_op jit(solution)/shard_map/ppermute | solution.py:368
  106.2 2.4 %collective-permute-start.11 = (bf16[128,1536]{1,0:T(8,128)(2,1)S(1)}, bf16[128,1536]{1,0:T(8,128)(2,1)S(1)}, u32[]{:S(2)}, u32[]{:S(2)}) collective-permute-start(bf16[128,1536]{1,0:T(8,128)(2,1)S(1)} %get-tuple-element.34), channel_id=1, source_target_pairs={{0,6},{4,0},{2,4},{6,2},{1,7},{5,1},{3,5},{7,3},{8,14},{12,8},{10,... | collective-permute-start | bytes 1179656 | tf_op jit(solution)/shard_map/ppermute | solution.py:368
  108.6 2.8 %copy-done.2 = bf16[1,6144,512]{2,1,0:T(8,128)(2,1)S(1)} copy-done((bf16[1,6144,512]{2,1,0:T(8,128)(2,1)S(1)}, bf16[1,6144,512]{2,1,0:T(8,128)(2,1)}, u32[]{:S(2)}) %copy-start.2) | copy-done | bytes 6291480
  111.4 4.1 %hidden_units.2.refs_0_ = bf16[256,512]{1,0:T(8,128)(2,1)S(1)} custom-call(s32[4]{0:T(128)S(1)} %get-tuple-element.35.refs_0_, bf16[256,1536]{1,0:T(8,128)(2,1)S(1)} %collective-permute-done.8.below_ref.refs_1_, bf16[256,1536]{1,0:T(8,128)(2,1)S(1)} %collective-permute-done.12.refs_2_, bf16[256,1536]{1,0:T(8,128)(2,1)S(1)} %collective-permute-done.9.above_ref.refs_3_, ...), custom_call_target="tpu_custom_call" | custom-call | flops 3221225472 | bytes 15728640 | tf_op jit(solution)/shard_map/hidden_units/pallas_call | solution.py:299
  118.1 2.9 %collective-permute-start.15 = (bf16[256,512]{1,0:T(8,128)(2,1)S(1)}, bf16[256,512]{1,0:T(8,128)(2,1)S(1)}, u32[]{:S(2)}, u32[]{:S(2)}) collective-permute-start(bf16[256,512]{1,0:T(8,128)(2,1)S(1)} %hidden_units.2.refs_0_), channel_id=1, source_target_pairs={{0,2},{2,0},{1,3},{3,1},{4,6},{6,4},{5,7},{7,5},{8,10},{10,8},{9,1... | collective-permute-start | bytes 786440 | tf_op jit(solution)/shard_map/ppermute | solution.py:359
  121.0 4.2 %hidden_units.3.refs_4_ = bf16[256,512]{1,0:T(8,128)(2,1)S(1)} custom-call(s32[4]{0:T(128)S(1)} %get-tuple-element.38.refs_0_, bf16[256,1536]{1,0:T(8,128)(2,1)S(1)} %bitcast.48, bf16[256,1536]{1,0:T(8,128)(2,1)S(1)} %collective-permute-done.17.refs_2_, bf16[128,1536]{1,0:T(8,128)(2,1)S(1)} %collective-permute-done.10.refs_3_, ...), custom_call_target="tpu_custom_call" | custom-call | flops 3221225472 | bytes 15728640 | tf_op jit(solution)/shard_map/hidden_units/pallas_call | solution.py:299
  128.3 6.5 %collective-permute-done.21.refs_6_ = bf16[256,512]{1,0:T(8,128)(2,1)S(1)} collective-permute-done((bf16[256,512]{1,0:T(8,128)(2,1)S(1)}, bf16[256,512]{1,0:T(8,128)(2,1)S(1)}, u32[]{:S(2)}, u32[]{:S(2)}) %collective-permute-start.21) | collective-permute-done | bytes 262176 | tf_op jit(solution)/shard_map/ppermute | solution.py:359
  136.3 5.1 %block_outputs.1 = bf16[16,2,16,1536]{3,2,1,0:T(8,128)(2,1)} custom-call(s32[2]{0:T(128)S(1)} %pad_add_fusion.2.info_ref, bf16[256,512]{1,0:T(8,128)(2,1)S(1)} %hidden_units.2.refs_0_, bf16[256,512]{1,0:T(8,128)(2,1)S(1)} %collective-permute-done.14.refs_1_, bf16[256,512]{1,0:T(8,128)(2,1)S(1)} %collective-permute-done.15.refs_2_, ...), custom_call_target="tpu_custom_call" | custom-call | flops 3221225472 | bytes 12582912 | tf_op jit(solution)/shard_map/block_outputs/pallas_call | solution.py:340
  141.5 4.0 %all-to-all-start.3 = ((bf16[32,16,1536]{2,1,0:T(8,128)(2,1)}), bf16[32,16,1536]{2,1,0:T(8,128)(2,1)S(1)}, u32[]{:S(2)}, u32[]{:S(2)}) async-start(bf16[32,16,1536]{2,1,0:T(8,128)(2,1)} %bitcast.24), calls=%async_computation.3 | async-start | bytes 3145728 | tf_op jit(solution)/shard_map/all_to_all | solution.py:523
  146.8 2.8 %collective-permute-start.24 = (f32[32,128]{1,0:T(8,128)S(1)}, f32[32,128]{1,0:T(8,128)S(1)}, u32[]{:S(2)}, u32[]{:S(2)}) collective-permute-start(f32[32,128]{1,0:T(8,128)S(1)} %add.115), channel_id=1, source_target_pairs={{0,2},{2,0},{1,3},{3,1},{4,6},{6,4},{5,7},{7,5},{8,10},{10,8},{9,1... | collective-permute-start | bytes 49160 | tf_op jit(solution)/shard_map/ppermute | solution.py:359
  149.5 17.2 %collective-permute-done.24 = f32[32,128]{1,0:T(8,128)S(1)} collective-permute-done((f32[32,128]{1,0:T(8,128)S(1)}, f32[32,128]{1,0:T(8,128)S(1)}, u32[]{:S(2)}, u32[]{:S(2)}) %collective-permute-start.24) | collective-permute-done | bytes 16416 | tf_op jit(solution)/shard_map/ppermute | solution.py:359
  (118 shorter events, 29.7 us)
Async XLA Ops:
  2.6 17.3 %collective-permute-start = (bf16[528,512]{1,0:T(8,128)(2,1)S(1)}, bf16[528,512]{1,0:T(8,128)(2,1)S(1)}, u32[]{:S(2)}, u32[]{:S(2)}) collective-permute-start(bf16[528,512]{1,0:T(8,128)(2,1)S(1)} %bitcast.49), channel_id=1, source_target_pairs={{0,32},{32,64},{64,96},{96,0},{1,33},{33,65},{65,97},{97,1},{2,34}... | collective-permute-start | bytes 1622024 | tf_op jit(solution)/shard_map/ppermute | solution.py:363
  4.6 29.3 %collective-permute-start.4 = (bf16[528,512]{1,0:T(8,128)(2,1)S(1)}, bf16[528,512]{1,0:T(8,128)(2,1)}, u32[]{:S(2)}, u32[]{:S(2)}) collective-permute-start(bf16[528,512]{1,0:T(8,128)(2,1)S(1)} %bitcast.50), channel_id=1, source_target_pairs={{0,96},{32,0},{64,32},{96,64},{1,97},{33,1},{65,33},{97,65},{2,98}... | collective-permute-start | bytes 1622024 | tf_op jit(solution)/shard_map/ppermute | solution.py:363
  7.7 22.5 %collective-permute-start.2 = (bf16[528,512]{1,0:T(8,128)(2,1)S(1)}, bf16[528,512]{1,0:T(8,128)(2,1)S(1)}, u32[]{:S(2)}, u32[]{:S(2)}) collective-permute-start(bf16[528,512]{1,0:T(8,128)(2,1)S(1)} %bitcast.52), channel_id=1, source_target_pairs={{0,96},{32,0},{64,32},{96,64},{1,97},{33,1},{65,33},{97,65},{2,98}... | collective-permute-start | bytes 1622024 | tf_op jit(solution)/shard_map/ppermute | solution.py:363
  9.7 24.2 %collective-permute-start.5 = (bf16[528,512]{1,0:T(8,128)(2,1)S(1)}, bf16[528,512]{1,0:T(8,128)(2,1)}, u32[]{:S(2)}, u32[]{:S(2)}) collective-permute-start(bf16[528,512]{1,0:T(8,128)(2,1)S(1)} %bitcast.53), channel_id=1, source_target_pairs={{0,32},{32,64},{64,96},{96,0},{1,33},{33,65},{65,97},{97,1},{2,34}... | collective-permute-start | bytes 1622024 | tf_op jit(solution)/shard_map/ppermute | solution.py:363
  10.8 23.1 %all-to-all-start = ((bf16[8,2,16,1536]{3,2,1,0:T(8,128)(2,1)}), bf16[8,2,16,1536]{3,2,1,0:T(8,128)(2,1)S(1)}, u32[]{:S(2)}, u32[]{:S(2)}) async-start(bf16[8,2,16,1536]{3,2,1,0:T(8,128)(2,1)} %broadcast_in_dim.18), calls=%async_computation | async-start | bytes 1572864 | tf_op jit(solution)/shard_map/all_to_all | solution.py:407
  16.3 43.3 %collective-permute-start.6 = (bf16[1536]{0:T(1024)(128)(2,1)S(1)}, bf16[1536]{0:T(1024)(128)(2,1)S(1)}, u32[]{:S(2)}, u32[]{:S(2)}) collective-permute-start(bf16[1536]{0:T(1024)(128)(2,1)S(1)} %copy-done.6), channel_id=1, source_target_pairs={{0,1},{1,0},{2,3},{3,2},{4,5},{5,4},{6,7},{7,6},{8,9},{9,8},{10,11... | collective-permute-start | bytes 9224 | tf_op jit(solution)/shard_map/ppermute | solution.py:359
  19.9 25.9 %collective-permute-start.1 = (bf16[528,512]{1,0:T(8,128)(2,1)S(1)}, bf16[528,512]{1,0:T(8,128)(2,1)}, u32[]{:S(2)}, u32[]{:S(2)}) collective-permute-start(bf16[528,512]{1,0:T(8,128)(2,1)S(1)} %collective-permute-done.refs_3_), channel_id=1, source_target_pairs={{0,32},{32,64},{64,96},{96,0},{1,33},{33,65},{65,97},{97,1},{2,34}... | collective-permute-start | bytes 1622024 | tf_op jit(solution)/shard_map/ppermute | solution.py:363
  30.1 15.6 %collective-permute-start.3 = (bf16[528,512]{1,0:T(8,128)(2,1)S(1)}, bf16[528,512]{1,0:T(8,128)(2,1)}, u32[]{:S(2)}, u32[]{:S(2)}) collective-permute-start(bf16[528,512]{1,0:T(8,128)(2,1)S(1)} %collective-permute-done.2.refs_7_), channel_id=1, source_target_pairs={{0,96},{32,0},{64,32},{96,64},{1,97},{33,1},{65,33},{97,65},{2,98}... | collective-permute-start | bytes 1622024 | tf_op jit(solution)/shard_map/ppermute | solution.py:363
  53.8 18.1 %all-to-all-start.1 = ((bf16[8,2,16,1664]{3,2,1,0:T(8,128)(2,1)}), bf16[8,2,16,1664]{3,2,1,0:T(8,128)(2,1)S(1)}, u32[]{:S(2)}, u32[]{:S(2)}) async-start(bf16[8,2,16,1664]{3,2,1,0:T(8,128)(2,1)} %copy-done.3), calls=%async_computation.1 | async-start | bytes 1703936 | tf_op jit(solution)/shard_map/all_to_all | solution.py:419
  59.7 11.2 %collective-permute-start.7 = (bf16[2,1536]{1,0:T(2,128)(2,1)S(1)}, bf16[2,1536]{1,0:T(2,128)(2,1)S(1)}, u32[]{:S(2)}, u32[]{:S(2)}) collective-permute-start(bf16[2,1536]{1,0:T(2,128)(2,1)S(1)} %broadcast_select_fusion.1), channel_id=1, source_target_pairs={{0,2},{2,0},{1,3},{3,1},{4,6},{6,4},{5,7},{7,5},{8,10},{10,8},{9,1... | collective-permute-start | bytes 18440 | tf_op jit(solution)/shard_map/ppermute | solution.py:359
  88.9 15.8 %collective-permute-start.8 = (bf16[256,1536]{1,0:T(8,128)(2,1)S(1)}, bf16[256,1536]{1,0:T(8,128)(2,1)S(1)}, u32[]{:S(2)}, u32[]{:S(2)}) collective-permute-start(bf16[256,1536]{1,0:T(8,128)(2,1)S(1)} %bitcast.44), channel_id=1, source_target_pairs={{0,4},{4,2},{2,6},{6,0},{1,5},{5,3},{3,7},{7,1},{8,12},{12,10},{10... | collective-permute-start | bytes 2359304 | tf_op jit(solution)/shard_map/ppermute | solution.py:368
  89.9 14.8 %collective-permute-start.9 = (bf16[256,1536]{1,0:T(8,128)(2,1)S(1)}, bf16[256,1536]{1,0:T(8,128)(2,1)S(1)}, u32[]{:S(2)}, u32[]{:S(2)}) collective-permute-start(bf16[256,1536]{1,0:T(8,128)(2,1)S(1)} %bitcast.45), channel_id=1, source_target_pairs={{0,6},{4,0},{2,4},{6,2},{1,7},{5,1},{3,5},{7,3},{8,14},{12,8},{10,... | collective-permute-start | bytes 2359304 | tf_op jit(solution)/shard_map/ppermute | solution.py:368
  104.7 3.9 %collective-permute-start.12 = (bf16[256,1536]{1,0:T(8,128)(2,1)S(1)}, bf16[256,1536]{1,0:T(8,128)(2,1)S(1)}, u32[]{:S(2)}, u32[]{:S(2)}) collective-permute-start(bf16[256,1536]{1,0:T(8,128)(2,1)S(1)} %collective-permute-done.8.below_ref.refs_1_), channel_id=1, source_target_pairs={{0,1},{1,0},{2,3},{3,2},{4,5},{5,4},{6,7},{7,6},{8,9},{9,8},{10,11... | collective-permute-start | bytes 2359304 | tf_op jit(solution)/shard_map/ppermute | solution.py:359
  104.7 3.9 %collective-permute-start.13 = (bf16[256,1536]{1,0:T(8,128)(2,1)S(1)}, bf16[256,1536]{1,0:T(8,128)(2,1)S(1)}, u32[]{:S(2)}, u32[]{:S(2)}) collective-permute-start(bf16[256,1536]{1,0:T(8,128)(2,1)S(1)} %collective-permute-done.9.above_ref.refs_3_), channel_id=1, source_target_pairs={{0,1},{1,0},{2,3},{3,2},{4,5},{5,4},{6,7},{7,6},{8,9},{9,8},{10,11... | collective-permute-start | bytes 2359304 | tf_op jit(solution)/shard_map/ppermute | solution.py:359
  105.3 12.3 %collective-permute-start.10 = (bf16[128,1536]{1,0:T(8,128)(2,1)S(1)}, bf16[128,1536]{1,0:T(8,128)(2,1)S(1)}, u32[]{:S(2)}, u32[]{:S(2)}) collective-permute-start(bf16[128,1536]{1,0:T(8,128)(2,1)S(1)} %get-tuple-element.33), channel_id=1, source_target_pairs={{0,4},{4,2},{2,6},{6,0},{1,5},{5,3},{3,7},{7,1},{8,12},{12,10},{10... | collective-permute-start | bytes 1179656 | tf_op jit(solution)/shard_map/ppermute | solution.py:368
  106.2 11.4 %collective-permute-start.11 = (bf16[128,1536]{1,0:T(8,128)(2,1)S(1)}, bf16[128,1536]{1,0:T(8,128)(2,1)S(1)}, u32[]{:S(2)}, u32[]{:S(2)}) collective-permute-start(bf16[128,1536]{1,0:T(8,128)(2,1)S(1)} %get-tuple-element.34), channel_id=1, source_target_pairs={{0,6},{4,0},{2,4},{6,2},{1,7},{5,1},{3,5},{7,3},{8,14},{12,8},{10,... | collective-permute-start | bytes 1179656 | tf_op jit(solution)/shard_map/ppermute | solution.py:368
  108.6 12.4 %collective-permute-start.17 = (bf16[256,1536]{1,0:T(8,128)(2,1)S(1)}, bf16[256,1536]{1,0:T(8,128)(2,1)S(1)}, u32[]{:S(2)}, u32[]{:S(2)}) collective-permute-start(bf16[256,1536]{1,0:T(8,128)(2,1)S(1)} %bitcast.47), channel_id=1, source_target_pairs={{0,1},{1,0},{2,3},{3,2},{4,5},{5,4},{6,7},{7,6},{8,9},{9,8},{10,11... | collective-permute-start | bytes 2359304 | tf_op jit(solution)/shard_map/ppermute | solution.py:359
  118.1 9.7 %collective-permute-start.15 = (bf16[256,512]{1,0:T(8,128)(2,1)S(1)}, bf16[256,512]{1,0:T(8,128)(2,1)S(1)}, u32[]{:S(2)}, u32[]{:S(2)}) collective-permute-start(bf16[256,512]{1,0:T(8,128)(2,1)S(1)} %hidden_units.2.refs_0_), channel_id=1, source_target_pairs={{0,2},{2,0},{1,3},{3,1},{4,6},{6,4},{5,7},{7,5},{8,10},{10,8},{9,1... | collective-permute-start | bytes 786440 | tf_op jit(solution)/shard_map/ppermute | solution.py:359
  125.3 9.5 %collective-permute-start.21 = (bf16[256,512]{1,0:T(8,128)(2,1)S(1)}, bf16[256,512]{1,0:T(8,128)(2,1)S(1)}, u32[]{:S(2)}, u32[]{:S(2)}) collective-permute-start(bf16[256,512]{1,0:T(8,128)(2,1)S(1)} %hidden_units.3.refs_4_), channel_id=1, source_target_pairs={{0,2},{2,0},{1,3},{3,1},{4,6},{6,4},{5,7},{7,5},{8,10},{10,8},{9,1... | collective-permute-start | bytes 786440 | tf_op jit(solution)/shard_map/ppermute | solution.py:359
  127.1 7.7 %collective-permute-start.14 = (bf16[256,512]{1,0:T(8,128)(2,1)S(1)}, bf16[256,512]{1,0:T(8,128)(2,1)S(1)}, u32[]{:S(2)}, u32[]{:S(2)}) collective-permute-start(bf16[256,512]{1,0:T(8,128)(2,1)S(1)} %hidden_units.2.refs_0_), channel_id=1, source_target_pairs={{0,1},{1,0},{2,3},{3,2},{4,5},{5,4},{6,7},{7,6},{8,9},{9,8},{10,11... | collective-permute-start | bytes 786440 | tf_op jit(solution)/shard_map/ppermute | solution.py:359
  127.8 7.0 %collective-permute-start.16 = (bf16[256,512]{1,0:T(8,128)(2,1)S(1)}, bf16[256,512]{1,0:T(8,128)(2,1)S(1)}, u32[]{:S(2)}, u32[]{:S(2)}) collective-permute-start(bf16[256,512]{1,0:T(8,128)(2,1)S(1)} %collective-permute-done.15.refs_2_), channel_id=1, source_target_pairs={{0,1},{1,0},{2,3},{3,2},{4,5},{5,4},{6,7},{7,6},{8,9},{9,8},{10,11... | collective-permute-start | bytes 786440 | tf_op jit(solution)/shard_map/ppermute | solution.py:359
  127.8 7.0 %collective-permute-start.20 = (bf16[256,512]{1,0:T(8,128)(2,1)S(1)}, bf16[256,512]{1,0:T(8,128)(2,1)S(1)}, u32[]{:S(2)}, u32[]{:S(2)}) collective-permute-start(bf16[256,512]{1,0:T(8,128)(2,1)S(1)} %hidden_units.3.refs_4_), channel_id=1, source_target_pairs={{0,1},{1,0},{2,3},{3,2},{4,5},{5,4},{6,7},{7,6},{8,9},{9,8},{10,11... | collective-permute-start | bytes 786440 | tf_op jit(solution)/shard_map/ppermute | solution.py:359
  141.5 28.2 %all-to-all-start.3 = ((bf16[32,16,1536]{2,1,0:T(8,128)(2,1)}), bf16[32,16,1536]{2,1,0:T(8,128)(2,1)S(1)}, u32[]{:S(2)}, u32[]{:S(2)}) async-start(bf16[32,16,1536]{2,1,0:T(8,128)(2,1)} %bitcast.24), calls=%async_computation.3 | async-start | bytes 3145728 | tf_op jit(solution)/shard_map/all_to_all | solution.py:523
  146.8 20.0 %collective-permute-start.24 = (f32[32,128]{1,0:T(8,128)S(1)}, f32[32,128]{1,0:T(8,128)S(1)}, u32[]{:S(2)}, u32[]{:S(2)}) collective-permute-start(f32[32,128]{1,0:T(8,128)S(1)} %add.115), channel_id=1, source_target_pairs={{0,2},{2,0},{1,3},{3,1},{4,6},{6,4},{5,7},{7,5},{8,10},{10,8},{9,1... | collective-permute-start | bytes 49160 | tf_op jit(solution)/shard_map/ppermute | solution.py:359
  (19 other events, 200.1 us)
